TPU v7x, 256 devices: a whole 4x4x8 slice. The times are simulated.
256 devices in a mesh: tile: 64 (over y, z, core), freq: 4 (over x).
Axes of the slice: x: 4, y: 4, z: 8, core: 2. Of those that a mesh axis runs over, the one named last changes fastest.
Arguments:
- spectrum: float32 [32, 24, 131072], P('freq', None, 'tile'), may hold values from 0.02 to 8, as said below
- forcing: float32 [4, 131072], P(None, 'tile'), may hold values from -24 to 24, as said below
- send_rows: int32 [4096, 256], P('tile'), may hold values from 0 to 2047
- point_slot: int32 [4, 131072], P(None, 'tile'), may hold values from 0 to 16383, as said below
- remap_weight: float32 [4, 131072], P(None, 'tile'), may hold values from 0 to 1, as said below
- neighbours: int32 [4, 131072], P(None, 'tile'), may hold values from 0 to 2303
- halo_send: int32 [16384], P('tile'), may hold values from 0 to 2047
Outputs:
- new_spectrum: float32 [32, 24, 131072], P('freq', None, 'tile')
- returned: float32 [4, 131072], P('freq', 'tile')
Inputs may be any that keep to these rules, and one draw needn't show every extreme that they name: `point_slot`: the four corners of a point name the same band. Of the list from a band to a tile only the first n slots are named, 1 <= n <= 256, n differing from list to list; for one tile n = 256 on the lists from every band. `remap_weight`: the four weights of a point are positive and sum to one. `spectrum`: Positive. `forcing`: winds within -24 to 24, density 1.0 to 1.4, gustiness 0 to 2.
All inputs are finite; a program needn't handle non-finite values.
Results may differ from a plain program's by a relative error of at most 0.0001.
Values sent between devices are 32-bit elements; how exact they have to be, the bound alone decides.
No kernel may reach another device: no remote copies, remote signals or barrier semaphores. Data moves between devices by JAX's collectives and lax.ppermute only.
A program may use at most 128 MiB of HBM per device.

v0:
```python
import math

import jax
import jax.numpy as jnp
from jax import lax
from jax.sharding import PartitionSpec as P

G_ACC = 9.81
WATER_DENSITY = 1025.0
FREQ_LOW = 0.03453
FREQ_RATIO = 1.1
E_UNIT = 0.001
DT_SRC = 120.0
COURANT_MAX = 0.7
DISSIP_COEF = 2.33e-05
STEEP_PM = 0.00302
TOP_EXPONENT = 31.0
LANE_WIDTH = 128


def extended_2(x, sides, width):
    for axis, dim in sides:
        devices, length = (lax.axis_size(axis), x.shape[dim])
        up = [(i, (i + 1) % devices) for i in range(devices - 1)]
        down = [(j, i) for i, j in up]
        last = lax.slice_in_dim(x, length - width, length, axis=dim)
        first = lax.slice_in_dim(x, 0, width, axis=dim)
        before = lax.ppermute(last, axis, up)
        after = lax.ppermute(first, axis, down)
        x = jnp.concatenate([before, x, after], axis=dim)
    return x


def spectral_bins(findex):
    radian_freq = 2.0 * math.pi * FREQ_LOW * jnp.power(FREQ_RATIO, findex)
    phase_speed = G_ACC / radian_freq
    wavenum = radian_freq * radian_freq / G_ACC
    courant = COURANT_MAX * jnp.power(FREQ_RATIO, -findex)
    return (radian_freq, phase_speed, wavenum, courant)


def direction_tables(count):
    theta = (jnp.arange(count, dtype=jnp.float32) + 0.5) * (2.0 * math.pi / count)
    return (jnp.cos(theta), jnp.sin(theta))


def surface_wind(wind_field):
    east_wind, north_wind, density, gust = (
        wind_field[0],
        wind_field[1],
        wind_field[2],
        wind_field[3],
    )
    wind_speed = jnp.sqrt(east_wind * east_wind + north_wind * north_wind + 1.0)
    friction_vel = jnp.sqrt(0.001 * (0.8 + 0.065 * wind_speed)) * wind_speed * (1.0 + 0.15 * gust)
    return (east_wind, north_wind, density, wind_speed, friction_vel)


def wind_input(radian_freq, phase_speed, aligned_cos, friction_vel, density):
    excess = jnp.maximum(28.0 * friction_vel * aligned_cos / phase_speed - 1.0, 0.0)
    return 0.25 * (density / WATER_DENSITY) * excess * radian_freq


def partial_moments(spectra, findex, cos_dir, sin_dir, aligned_cos, friction_vel, density):
    radian_freq, phase_speed, wavenum, courant = spectral_bins(findex)
    sum_axes = tuple(range(spectra.ndim - friction_vel.ndim))
    growth = wind_input(radian_freq, phase_speed, aligned_cos, friction_vel, density)
    momentum = growth * spectra / phase_speed
    return jnp.stack(
        [
            jnp.sum(spectra, axis=sum_axes),
            jnp.sum(spectra / radian_freq, axis=sum_axes),
            jnp.sum(spectra / jnp.sqrt(wavenum), axis=sum_axes),
            jnp.sum(momentum * cos_dir, axis=sum_axes),
            jnp.sum(momentum * sin_dir, axis=sum_axes),
        ]
    )


def finish_moments(moments, east_wind, north_wind, density, wind_speed, friction_vel):
    total_energy, inv_sigma_sum, inv_root_sum = (moments[0], moments[1], moments[2])
    stress_east, stress_north = (moments[3], moments[4])
    mean_sigma = total_energy / inv_sigma_sum
    mean_wavenum = jnp.square(total_energy / inv_root_sum)
    steepness = mean_wavenum * mean_wavenum * total_energy * E_UNIT
    dissipation = DISSIP_COEF * mean_sigma * jnp.square(steepness / STEEP_PM) / mean_wavenum
    stress_scale = WATER_DENSITY / density * G_ACC * E_UNIT
    friction_sq = friction_vel * friction_vel
    east_ratio = stress_scale * stress_east / friction_sq
    north_ratio = stress_scale * stress_north / friction_sq
    aligned = (east_ratio * east_wind + north_ratio * north_wind) / wind_speed
    charnock = 0.01 / jnp.sqrt(1.0 - 0.9 * aligned / (1.0 + jnp.abs(aligned)))
    wave_height = 4.0 * jnp.sqrt(E_UNIT * total_energy)
    return (dissipation, jnp.stack([east_ratio, north_ratio, charnock / 0.01, wave_height]))


def binned_sum(values, targets, total):
    field_count, row_count = values.shape
    upper_count = total // LANE_WIDTH
    block_rows = math.gcd(row_count, 2048)
    block_count = row_count // block_rows
    value_blocks = values.reshape(field_count, block_count, block_rows).transpose(1, 0, 2)
    target_blocks = targets.reshape(block_count, block_rows)
    upper_ids = jnp.arange(upper_count, dtype=jnp.int32)
    lower_ids = jnp.arange(LANE_WIDTH, dtype=jnp.int32)

    def add_block(carry, inputs):
        value_rows, target_rows = inputs
        upper_table = (target_rows[:, None] // LANE_WIDTH == upper_ids[None, :]).astype(jnp.float32)
        lower_table = (target_rows[:, None] % LANE_WIDTH == lower_ids[None, :]).astype(jnp.float32)
        weighted = value_rows[:, :, None] * upper_table[None]
        term = jnp.einsum(
            "frh,rl->fhl",
            weighted,
            lower_table,
            precision=lax.Precision.HIGHEST,
            preferred_element_type=jnp.float32,
        )
        return (carry + term, None)

    start = jnp.zeros((field_count, upper_count, LANE_WIDTH), jnp.float32)
    summed, unused = lax.scan(add_block, start, (value_blocks, target_blocks))
    return summed.reshape(field_count, total)


def on_device(spectrum, forcing, send_rows, point_slot, remap_weight, neighbours, halo_send):
    group_size, dir_count, point_count = spectrum.shape
    tile_count = lax.axis_size("tile")
    group_count = lax.axis_size("freq")
    slot_count = send_rows.shape[1]
    rim_width = halo_send.shape[0] // 2
    outgoing = forcing[:, send_rows]
    arrived = lax.all_to_all(outgoing, "tile", split_axis=1, concat_axis=1, tiled=True)
    received = arrived.reshape(arrived.shape[0], tile_count * slot_count)
    wind_field = jnp.sum(received[:, point_slot] * remap_weight[None], axis=1)
    east_wind, north_wind, density, wind_speed, friction_vel = surface_wind(wind_field)
    cos_dir, sin_dir = direction_tables(dir_count)
    cos_dir = cos_dir[:, None]
    sin_dir = sin_dir[:, None]
    aligned_cos = (east_wind * cos_dir + north_wind * sin_dir) / wind_speed
    whole_count = group_size * group_count
    findex = (lax.axis_index("freq") * group_size + jnp.arange(group_size)).astype(jnp.float32)
    findex = (findex * (TOP_EXPONENT / (whole_count - 1)))[:, None, None]
    local_moments = partial_moments(
        spectrum, findex, cos_dir, sin_dir, aligned_cos, friction_vel, density
    )
    moments = lax.psum(local_moments, "freq")
    dissipation, fields = finish_moments(
        moments, east_wind, north_wind, density, wind_speed, friction_vel
    )
    rim_cells = extended_2(spectrum[:, :, halo_send], (("tile", 2),), rim_width)
    extended = jnp.concatenate(
        [rim_cells[:, :, :rim_width], spectrum, rim_cells[:, :, -rim_width:]], axis=2
    )
    west_cells = extended[:, :, neighbours[0]]
    east_cells = extended[:, :, neighbours[1]]
    south_cells = extended[:, :, neighbours[2]]
    north_cells = extended[:, :, neighbours[3]]
    from_x = jnp.where(cos_dir > 0, west_cells, east_cells)
    from_y = jnp.where(sin_dir > 0, south_cells, north_cells)
    radian_freq, phase_speed, wavenum, courant = spectral_bins(findex)
    moved = (
        spectrum
        - courant * jnp.abs(cos_dir) * (spectrum - from_x)
        - courant * jnp.abs(sin_dir) * (spectrum - from_y)
    )
    growth = (
        wind_input(radian_freq, phase_speed, aligned_cos, friction_vel, density)
        - dissipation * wavenum
    )
    new_spectrum = moved * jnp.exp(DT_SRC * growth)
    field_count = 4 // group_count
    own_fields = lax.dynamic_slice_in_dim(
        fields, lax.axis_index("freq") * field_count, field_count, 0
    )
    weighted = remap_weight[None, :, :] * own_fields[:, None, :]
    slot_sums = binned_sum(
        weighted.reshape(field_count, -1), point_slot.reshape(-1), tile_count * slot_count
    )
    arrived_sums = lax.all_to_all(
        slot_sums.reshape(field_count, tile_count, slot_count),
        "tile",
        split_axis=1,
        concat_axis=1,
        tiled=True,
    )
    returned = binned_sum(
        arrived_sums.reshape(field_count, -1), send_rows.reshape(-1), forcing.shape[1]
    )
    return (new_spectrum, returned)


def solution(mesh):
    placed = (
        P("freq", None, "tile"),
        P(None, "tile"),
        P("tile", None),
        P(None, "tile"),
        P(None, "tile"),
        P(None, "tile"),
        P("tile"),
    )
    return jax.shard_map(
        on_device,
        mesh=mesh,
        in_specs=placed,
        out_specs=(P("freq", None, "tile"), P("freq", "tile")),
        check_vma=False,
    )
```

profile of v0, /device:TPU:1, one launch (start us, length us, event | category | flops | bytes accessed | tf_op | source)
XLA Modules:
  0.0 319.8 jit_solution(1071787944959272374)
XLA Ops:
  0.6 6.1 %copy.84 = f32[8,24,2048]{1,0,2:T(8,128)} copy(f32[8,24,2048]{2,1,0:T(8,128)} %param.11) | data formatting | bytes 3145728 | tf_op args[0]
  6.8 4.1 %gather_fusion = f32[256,8,24]{2,1,0:T(8,128)S(1)} fusion(f32[8,24,2048]{1,0,2:T(8,128)} %copy.84, s32[1024]{0:T(1024)S(1)} %pad_clamp_fusion), kind=kCustom, calls=%fused_computation | custom fusion | bytes 394240 | tf_op jit(solution)/shard_map/gather | solution.py:151
  11.0 5.1 %collective-permute-start.1 = (f32[8,24,128]{1,0,2:T(8,128)S(1)}, f32[8,24,128]{1,0,2:T(8,128)S(1)}, u32[]{:S(2)}, u32[]{:S(2)}) collective-permute-start(f32[8,24,128]{1,0,2:T(8,128)S(1)} %get-tuple-element.278), channel_id=1, source_target_pairs={{4,0},{8,4},{12,8},{16,12},{20,16},{24,20},{28,24},{32,28},{36,32}... | collective-permute-start | bytes 294920 | tf_op jit(solution)/shard_map/ppermute | solution.py:29
  16.2 1.9 collective-permute-start
  18.6 54.5 %gather_fusion.5 = f32[16384,4]{1,0:T(8,128)} fusion(f32[4,2048]{0,1:T(8,128)S(1)} %copy.90, s32[16384]{0:T(1024)S(1)} %broadcast_clamp_fusion), kind=kCustom, calls=%fused_computation.5 | custom fusion | bytes 589824 | tf_op jit(solution)/shard_map/gather | solution.py:132
  73.1 5.9 %copy.91 = f32[64,256,4]{1,2,0:T(4,128)} copy(f32[64,256,4]{2,1,0:T(8,128)} %bitcast.82) | data formatting | bytes 524288 | tf_op jit(solution)/shard_map/gather | solution.py:132
  79.0 11.9 %all-to-all-start = ((f32[4,64,256]{2,0,1:T(4,128)}), f32[4,64,256]{2,0,1:T(4,128)S(1)}, u32[]{:S(2)}, u32[]{:S(2)}) async-start(f32[4,64,256]{2,0,1:T(4,128)} %bitcast.12), calls=%async_computation | async-start | bytes 524288 | tf_op jit(solution)/shard_map/all_to_all | solution.py:133
  93.2 9.9 %pad_maximum_fusion = f32[8,24,2304]{1,0,2:T(8,128)} fusion(f32[8,24,128]{1,0,2:T(8,128)S(1)} %collective-permute-done.1, f32[8,24,2048]{1,0,2:T(8,128)} %copy.84, f32[8,24,128]{1,0,2:T(8,128)S(1)} %collective-permute-done), kind=kLoop, calls=%fused_computation.50 | loop fusion | flops 884736 | bytes 3538944 | tf_op jit(solution)/shard_map/concatenate | solution.py:152
  103.0 19.5 %gather_fusion.3 = f32[2048,8,24]{2,1,0:T(8,128)} fusion(f32[8,24,2304]{1,0,2:T(8,128)} %pad_maximum_fusion, s32[2048]{0:T(1024)S(1)} %broadcast_clamp_fusion.3), kind=kCustom, calls=%fused_computation.3 | custom fusion | bytes 3153920 | tf_op jit(solution)/shard_map/gather | solution.py:157
  122.6 5.1 %copy.88 = f32[2048,8,24]{0,2,1:T(8,128)S(1)} copy(f32[2048,8,24]{2,1,0:T(8,128)} %gather_fusion.3) | data formatting | bytes 3145728 | tf_op jit(solution)/shard_map/gather | solution.py:157
  127.7 19.6 %gather_fusion.4 = f32[2048,8,24]{2,1,0:T(8,128)} fusion(f32[8,24,2304]{1,0,2:T(8,128)} %pad_maximum_fusion, s32[2048]{0:T(1024)S(1)} %broadcast_clamp_fusion.2), kind=kCustom, calls=%fused_computation.4 | custom fusion | bytes 3153920 | tf_op jit(solution)/shard_map/gather | solution.py:158
  147.3 6.1 %copy.89 = f32[2048,8,24]{0,2,1:T(8,128)} copy(f32[2048,8,24]{2,1,0:T(8,128)} %gather_fusion.4) | data formatting | bytes 3145728 | tf_op jit(solution)/shard_map/gather | solution.py:158
  153.4 19.5 %gather_fusion.1 = f32[2048,8,24]{2,1,0:T(8,128)} fusion(f32[8,24,2304]{1,0,2:T(8,128)} %pad_maximum_fusion, s32[2048]{0:T(1024)S(1)} %broadcast_clamp_fusion.5), kind=kCustom, calls=%fused_computation.1 | custom fusion | bytes 3153920 | tf_op jit(solution)/shard_map/gather | solution.py:155
  172.9 6.2 %copy.86 = f32[2048,8,24]{0,2,1:T(8,128)} copy(f32[2048,8,24]{2,1,0:T(8,128)} %gather_fusion.1) | data formatting | bytes 3145728 | tf_op jit(solution)/shard_map/gather | solution.py:155
  179.1 19.5 %gather_fusion.2 = f32[2048,8,24]{2,1,0:T(8,128)} fusion(f32[8,24,2304]{1,0,2:T(8,128)} %pad_maximum_fusion, s32[2048]{0:T(1024)S(1)} %broadcast_clamp_fusion.4), kind=kCustom, calls=%fused_computation.2 | custom fusion | bytes 3153920 | tf_op jit(solution)/shard_map/gather | solution.py:156
  198.7 6.2 %copy.87 = f32[2048,8,24]{0,2,1:T(8,128)} copy(f32[2048,8,24]{2,1,0:T(8,128)} %gather_fusion.2) | data formatting | bytes 3145728 | tf_op jit(solution)/shard_map/gather | solution.py:156
  204.8 4.8 %copy.92 = f32[4,64,256]{0,2,1:T(8,128)} copy(f32[4,64,256]{2,0,1:T(4,128)S(1)} %all-to-all-done) | data formatting | bytes 524288 | tf_op jit(solution)/shard_map/all_to_all | solution.py:133
  209.7 31.1 %gather_fusion.6 = f32[8192,4]{1,0:T(8,128)} fusion(f32[4,16384]{0,1:T(8,128)} %bitcast.81, s32[8192]{0:T(1024)S(1)} %broadcast_clamp_fusion.1), kind=kCustom, calls=%fused_computation.6 | custom fusion | bytes 294912 | tf_op jit(solution)/shard_map/gather | solution.py:135
  240.8 4.0 %multiply_reduce_fusion = f32[2048,4]{1,0:T(8,128)} fusion(f32[4,2048,4]{2,1,0:T(8,128)} %bitcast.83, f32[4,2048]{1,0:T(4,128)S(1)} %copy-done.3), kind=kLoop, calls=%fused_computation.51 | loop fusion | flops 57344 | bytes 196608 | tf_op jit(solution)/shard_map/reduce_sum | solution.py:135
  250.3 14.3 %psum.7 = f32[5,2048]{1,0:T(8,128)} all-reduce(f32[5,2048]{1,0:T(8,128)S(1)} %stack.30), channel_id=1, replica_groups=mesh['tile'=64,'freq'=4] {'freq'}, use_global_device_ids=true, to_apply=%region_6.0 | all-reduce | flops 10240 | bytes 81920 | tf_op jit(solution)/shard_map/psum | solution.py:147
  267.3 12.8 %while.29 = (s32[]{:T(128)}, f32[1,128,128]{2,1,0:T(8,128)}, s32[4,2048]{1,0:T(4,128)S(1)}, f32[4,1,2048]{2,1,0:T(1,128)S(1)}, s32[]{:T(128)}, /*index=5*/s32[]{:T(128)}) while((s32[]{:T(128)}, f32[1,128,128]{2,1,0:T(8,128)}, s32[4,2048]{1,0:T(4,128)S(1)}, f32[4,1,2048]{2,1,0:T(1,128)S(1)}, s32[]{:T(128)}, ...), condition=%wide.region_8.9_spmd.clone.clone, body=%wide.region_7.8_spmd.clone.clone.sunk | while | flops 403511296 | bytes 213087 | solution.py:122
  267.4 2.5 fusion.57
  270.0 3.3 %fusion.57 = f32[1,128,128]{2,1,0:T(8,128)} fusion(s32[2048]{0:T(1024)S(1)} %get-tuple-element.359, f32[2048]{0:T(1024)S(1)} %bitcast.90, s32[2048]{0:T(1024)S(1)} %get-tuple-element.360, f32[1,128,128]{2,1,0:T(8,128)} %get-tuple-element.368, pred[]{:T(512)S(6)} %compare.35), kind=kOutput, calls=%fused_computation.33.clone.1 | convolution fusion | flops 403472384 | bytes 155649 | tf_op jit(solution)/shard_map/while/body/eval_jaxpr/frh,rl->fhl/dot_general | solution.py:112
  273.4 3.3 %fusion.57 = f32[1,128,128]{2,1,0:T(8,128)} fusion(s32[2048]{0:T(1024)S(1)} %get-tuple-element.359, f32[2048]{0:T(1024)S(1)} %bitcast.90, s32[2048]{0:T(1024)S(1)} %get-tuple-element.360, f32[1,128,128]{2,1,0:T(8,128)} %get-tuple-element.368, pred[]{:T(512)S(6)} %compare.35), kind=kOutput, calls=%fused_computation.33.clone.1 | convolution fusion | flops 403472384 | bytes 155649 | tf_op jit(solution)/shard_map/while/body/eval_jaxpr/frh,rl->fhl/dot_general | solution.py:112
  276.8 3.3 %fusion.57 = f32[1,128,128]{2,1,0:T(8,128)} fusion(s32[2048]{0:T(1024)S(1)} %get-tuple-element.359, f32[2048]{0:T(1024)S(1)} %bitcast.90, s32[2048]{0:T(1024)S(1)} %get-tuple-element.360, f32[1,128,128]{2,1,0:T(8,128)} %get-tuple-element.368, pred[]{:T(512)S(6)} %compare.35), kind=kOutput, calls=%fused_computation.33.clone.1 | convolution fusion | flops 403472384 | bytes 155649 | tf_op jit(solution)/shard_map/while/body/eval_jaxpr/frh,rl->fhl/dot_general | solution.py:112
  280.1 14.1 %all-to-all-start.1 = ((f32[1,64,256]{2,0,1:T(1,128)}), f32[1,64,256]{2,0,1:T(1,128)S(1)}, u32[]{:S(2)}, u32[]{:S(2)}) async-start(f32[1,64,256]{2,0,1:T(1,128)} %bitcast.97), calls=%async_computation.1 | async-start | bytes 131072 | tf_op jit(solution)/shard_map/all_to_all | solution.py:180
  295.0 4.7 %fusion.29 = f32[8,24,2048]{2,1,0:T(8,128)} fusion(f32[8,24,2048]{2,1,0:T(8,128)S(1)} %copy-done, f32[2048,8,24]{0,2,1:T(8,128)S(1)} %copy.88, f32[2048,8,24]{0,2,1:T(8,128)} %copy.89, f32[2048,8,24]{0,2,1:T(8,128)} %copy.86, f32[2048,8,24]{0,2,1:T(8,128)} %copy.87, f32[8,2048]{1,0:T(8,128)S(1)} %broadcast_multiply_fusion, f32[8]{0:T(128)} %copy-done.12, ...), kind=kLoop, calls=%fused_computation.59 | loop fusion | flops 6291456 | bytes 9709168 | tf_op jit(solution)/shard_map/mul | solution.py:171
  299.8 4.2 %all-to-all-done.1 = f32[1,64,256]{2,0,1:T(1,128)S(1)} async-done(((f32[1,64,256]{2,0,1:T(1,128)}), f32[1,64,256]{2,0,1:T(1,128)S(1)}, u32[]{:S(2)}, u32[]{:S(2)}) %all-to-all-start.1) | async-done | bytes 65568 | tf_op jit(solution)/shard_map/all_to_all | solution.py:180
  304.0 15.2 %while.28 = (s32[]{:T(128)}, f32[1,16,128]{2,1,0:T(8,128)S(1)}, s32[8,2048]{1,0:T(8,128)S(1)}, f32[8,1,2048]{2,1,0:T(1,128)S(1)}, s32[]{:T(128)}, /*index=5*/s32[]{:T(128)}) while((s32[]{:T(128)}, f32[1,16,128]{2,1,0:T(8,128)S(1)}, s32[8,2048]{1,0:T(8,128)S(1)}, f32[8,1,2048]{2,1,0:T(1,128)S(1)}, s32[]{:T(128)}, ...), condition=%wide.region_10.11_spmd.clone, body=%wide.region_9.10_spmd.clone.sunk | while | flops 50702336 | bytes 98399 | solution.py:122
  306.0 1.8 fusion.55
  307.9 1.8 fusion.55
  309.8 1.8 fusion.55
  (113 shorter events, 21.8 us)
Async XLA Ops:
  0.6 6.1 %copy-start.13 = (s32[256]{0:T(256)S(1)}, s32[256]{0:T(256)}, u32[]{:S(2)}) copy-start(s32[256]{0:T(256)} %param.17) | copy-start | bytes 3076
  6.8 11.3 %copy-start.4 = (f32[4,2048]{1,0:T(4,128)S(1)}, f32[4,2048]{1,0:T(4,128)}, u32[]{:S(2)}) copy-start(f32[4,2048]{1,0:T(4,128)} %param.12) | copy-start | bytes 98308
  10.9 7.6 %copy-start.1 = (s32[64,256]{1,0:T(8,128)S(1)}, s32[64,256]{1,0:T(8,128)}, u32[]{:S(2)}) copy-start(s32[64,256]{1,0:T(8,128)} %param.13) | copy-start | bytes 196612
  11.0 82.2 %collective-permute-start.1 = (f32[8,24,128]{1,0,2:T(8,128)S(1)}, f32[8,24,128]{1,0,2:T(8,128)S(1)}, u32[]{:S(2)}, u32[]{:S(2)}) collective-permute-start(f32[8,24,128]{1,0,2:T(8,128)S(1)} %get-tuple-element.278), channel_id=1, source_target_pairs={{4,0},{8,4},{12,8},{16,12},{20,16},{24,20},{28,24},{32,28},{36,32}... | collective-permute-start | bytes 294920 | tf_op jit(solution)/shard_map/ppermute | solution.py:29
  16.2 77.0 %collective-permute-start = (f32[8,24,128]{1,0,2:T(8,128)S(1)}, f32[8,24,128]{1,0,2:T(8,128)S(1)}, u32[]{:S(2)}, u32[]{:S(2)}) collective-permute-start(f32[8,24,128]{1,0,2:T(8,128)S(1)} %get-tuple-element.277), channel_id=1, source_target_pairs={{0,4},{4,8},{8,12},{12,16},{16,20},{20,24},{24,28},{28,32},{32,36}... | collective-permute-start | bytes 294920 | tf_op jit(solution)/shard_map/ppermute | solution.py:28
  73.1 18.0 %copy-start.5 = (s32[4,2048]{1,0:T(4,128)S(1)}, s32[4,2048]{1,0:T(4,128)}, u32[]{:S(2)}) copy-start(s32[4,2048]{1,0:T(4,128)} %param.16) | copy-start | bytes 98308
  73.1 18.1 %copy-start.2 = (s32[4,2048]{1,0:T(4,128)S(1)}, s32[4,2048]{1,0:T(4,128)}, u32[]{:S(2)}) copy-start(s32[4,2048]{1,0:T(4,128)} %param.14) | copy-start | bytes 98308
  79.0 125.8 %all-to-all-start = ((f32[4,64,256]{2,0,1:T(4,128)}), f32[4,64,256]{2,0,1:T(4,128)S(1)}, u32[]{:S(2)}, u32[]{:S(2)}) async-start(f32[4,64,256]{2,0,1:T(4,128)} %bitcast.12), calls=%async_computation | async-start | bytes 524288 | tf_op jit(solution)/shard_map/all_to_all | solution.py:133
  90.9 156.3 %copy-start.11 = (f32[8]{0:T(128)}, f32[8]{0:T(128)S(1)}, u32[]{:S(2)}) copy-start(f32[8]{0:T(128)S(1)} %get-tuple-element.295) | copy-start | bytes 100
  90.9 156.3 %copy-start.12 = (f32[8]{0:T(128)}, f32[8]{0:T(128)S(1)}, u32[]{:S(2)}) copy-start(f32[8]{0:T(128)S(1)} %get-tuple-element.293) | copy-start | bytes 100
  204.8 36.0 %copy-start.3 = (f32[4,2048]{1,0:T(4,128)S(1)}, f32[4,2048]{1,0:T(4,128)}, u32[]{:S(2)}) copy-start(f32[4,2048]{1,0:T(4,128)} %param.15) | copy-start | bytes 98308
  240.8 6.4 %copy-start = (f32[8,24,2048]{2,1,0:T(8,128)S(1)}, f32[8,24,2048]{2,1,0:T(8,128)}, u32[]{:S(2)}) copy-start(f32[8,24,2048]{2,1,0:T(8,128)} %param.11) | copy-start | bytes 4718596
  267.3 26.9 %copy-start.6 = (f32[1,2048]{1,0:T(1,128)S(1)}, f32[1,2048]{1,0:T(1,128)}, u32[]{:S(2)}) copy-start(f32[1,2048]{1,0:T(1,128)} %get-tuple-element.280) | copy-start | bytes 24580
  267.3 26.9 %copy-start.7 = (f32[1,2048]{1,0:T(1,128)S(1)}, f32[1,2048]{1,0:T(1,128)}, u32[]{:S(2)}) copy-start(f32[1,2048]{1,0:T(1,128)} %get-tuple-element.281) | copy-start | bytes 24580
  267.3 26.9 %copy-start.8 = (f32[1,2048]{1,0:T(1,128)S(1)}, f32[1,2048]{1,0:T(1,128)}, u32[]{:S(2)}) copy-start(f32[1,2048]{1,0:T(1,128)} %get-tuple-element.282) | copy-start | bytes 24580
  267.3 27.7 %copy-start.9 = (f32[8,24]{1,0:T(8,128)S(1)}, f32[8,24]{1,0:T(8,128)}, u32[]{:S(2)}) copy-start(f32[8,24]{1,0:T(8,128)} %get-tuple-element.291) | copy-start | bytes 2308
  267.3 27.7 %copy-start.10 = (f32[8,24]{1,0:T(8,128)S(1)}, f32[8,24]{1,0:T(8,128)}, u32[]{:S(2)}) copy-start(f32[8,24]{1,0:T(8,128)} %get-tuple-element.292) | copy-start | bytes 2308
  280.1 23.9 %all-to-all-start.1 = ((f32[1,64,256]{2,0,1:T(1,128)}), f32[1,64,256]{2,0,1:T(1,128)S(1)}, u32[]{:S(2)}, u32[]{:S(2)}) async-start(f32[1,64,256]{2,0,1:T(1,128)} %bitcast.97), calls=%async_computation.1 | async-start | bytes 131072 | tf_op jit(solution)/shard_map/all_to_all | solution.py:180
  295.0 9.0 %copy-start.14 = (f32[1,16,128]{2,1,0:T(8,128)S(1)}, f32[1,16,128]{2,1,0:T(8,128)}, u32[]{:S(2)}) copy-start(f32[1,16,128]{2,1,0:T(8,128)} %custom-call) | copy-start | bytes 24580
  319.2 0.6 copy-start.15
where the time goes:
time: 321 us; the launch traced here: 320 us
  local copies, waits for them, and re-layouts  212 us (66%)
  starting transfers between devices  33 us (10%)
  other arithmetic  27.4 us (9%)
  matrix products  27.1 us (8%)
  blocking collectives  14.3 us (4%)
  waiting for transfers between devices  4.23 us (1%)
    gather x2, local copies, waits for them, and re-layouts, on_device(): outgoing = forcing[:, send_rows]  60.4 us
    gather x1, local copies, waits for them, and re-layouts, on_device(): wind_field = jnp.sum(received[:, point_slot] * remap_weight[None], axis=1)  31.1 us
    dot_general x12, matrix products, add_block(): jnp.einsum('frh,rl->fhl', weighted, lower_table, precision=lax.Precision....  27.1 us
    gather x2, local copies, waits for them, and re-layouts, on_device(): east_cells = extended[:, :, neighbours[1]]  25.7 us
    gather x2, local copies, waits for them, and re-layouts, on_device(): west_cells = extended[:, :, neighbours[0]]  25.7 us
    gather x2, local copies, waits for them, and re-layouts, on_device(): north_cells = extended[:, :, neighbours[3]]  25.7 us
    gather x2, local copies, waits for them, and re-layouts, on_device(): south_cells = extended[:, :, neighbours[2]]  24.7 us
    psum x1, blocking collectives, on_device(): moments = lax.psum(local_moments, 'freq')  14.3 us
  transfers between devices with their start and end apart: 4, of which 1 were waited for; matrix products, arithmetic and copies ran while one was open for 56% of the time, Pallas kernels for 0%

commit v1 on v0

v1 whole, which is shorter than its diff:
```python
import math

import jax
import jax.numpy as jnp
import numpy as np
from jax import lax
from jax.experimental import pallas as pl
from jax.experimental.pallas import tpu as pltpu
from jax.sharding import PartitionSpec as P

G_ACC = 9.81
WATER_DENSITY = 1025.0
FREQ_LOW = 0.03453
FREQ_RATIO = 1.1
E_UNIT = 0.001
DT_SRC = 120.0
COURANT_MAX = 0.7
DISSIP_COEF = 2.33e-05
STEEP_PM = 0.00302
TOP_EXPONENT = 31.0

NF = 32
ND = 24
GS = 8
PTS = 2048
TILES = 64
CAP = 256
RIM = 128
EXT = PTS + 2 * RIM

F32 = jnp.float32
BF = jnp.bfloat16
I32 = jnp.int32

THETA = [(k + 0.5) * 2.0 * math.pi / ND for k in range(ND)]
COS = [math.cos(t) for t in THETA]
SIN = [math.sin(t) for t in THETA]

OMEGA, INV_C, WAVENUM, COURANT, INV_OMEGA, INV_ROOT, OMEGA_C = range(7)


def frequency_table():
    e = np.arange(NF, dtype=np.float64) * (TOP_EXPONENT / (NF - 1))
    omega = 2.0 * math.pi * FREQ_LOW * FREQ_RATIO**e
    speed = G_ACC / omega
    wavenum = omega * omega / G_ACC
    courant = COURANT_MAX * FREQ_RATIO ** (-e)
    rows = [omega, 1 / speed, wavenum, courant, 1 / omega, 1 / np.sqrt(wavenum), omega / speed]
    return np.stack(rows).astype(np.float32)


def direction_tiles():
    both = np.stack([np.array(COS), np.array(SIN)]).astype(np.float32)
    return np.broadcast_to(both[:, :, None], (2, ND, 128)).copy()


def lane_gather(block, index):
    return jnp.take_along_axis(block, index, axis=1, mode="promise_in_bounds")


def parts2(x):
    first = x.astype(BF)
    return first, (x - first.astype(F32)).astype(BF)


def parts3(x):
    first = x.astype(BF)
    rest = x - first.astype(F32)
    second = rest.astype(BF)
    return first, second, (rest - second.astype(F32)).astype(BF)


def outgoing_kernel(forcing_ref, rows_ref, out_ref):
    def eight_tiles(q, carry):
        d = pl.ds(pl.multiple_of(q * 8, 8), 8)
        for half in range(2):
            index = rows_ref[d, half * 128 : half * 128 + 128]
            low, high = index & 127, index >> 7
            for i in range(4):
                got = None
                for h in range(16):
                    block = jnp.broadcast_to(forcing_ref[i : i + 1, h * 128 : h * 128 + 128], (8, 128))
                    piece = lane_gather(block, low)
                    got = piece if h == 0 else jnp.where(high == h, piece, got)
                out_ref[d, 2 * i + half, :] = got
        return carry

    lax.fori_loop(0, TILES // 8, eight_tiles, 0)


def rim_kernel(spec_ref, list_ref, before_ref, after_ref):
    for side, out_ref in ((0, before_ref), (1, after_ref)):
        index = jnp.broadcast_to(list_ref[side : side + 1, :], (8, 128))
        low, high = index & 127, index >> 7

        def one_freq(i, carry):
            for g in range(3):
                got = None
                for h in range(16):
                    piece = lane_gather(spec_ref[i, 8 * g : 8 * g + 8, h * 128 : h * 128 + 128], low)
                    got = piece if h == 0 else jnp.where(high == h, piece, got)
                out_ref[i, 8 * g : 8 * g + 8, :] = got
            return carry

        lax.fori_loop(0, GS, one_freq, 0)


def weight_matrix(slot_ref, weight_ref, cols, width):
    slots = lax.broadcasted_iota(I32, (CAP, width), 0)
    total = None
    for j in range(4):
        index = slot_ref[j : j + 1, cols] & (CAP - 1)
        term = jnp.where(slots == index, weight_ref[j : j + 1, cols], 0.0)
        total = term if j == 0 else total + term
    return total, slot_ref[0:1, cols] >> 8


WB = 256


def wind_kernel(tab_ref, freq_ref, arrived_ref, slot_ref, weight_ref, spec_ref, dir_ref, wind_ref, mom_ref, left_ref):
    base = freq_ref[0] * GS
    for i in range(4):
        for half in range(2):
            p0, p1, p2 = parts3(arrived_ref[:, 2 * i + half, :])
            for n, part in enumerate((p0, p1, p2, p0, p1, p0)):
                left_ref[i * 64 : i * 64 + 64, n * 256 + half * 128 : n * 256 + half * 128 + 128] = part

    def block(c, carry):
        cols = pl.ds(pl.multiple_of(c * WB, WB), WB)
        weights, band = weight_matrix(slot_ref, weight_ref, cols, WB)
        w0, w1, w2 = parts3(weights)
        right = jnp.concatenate([w0, w0, w0, w1, w1, w2], axis=0)
        mixed = jnp.dot(left_ref[...], right, preferred_element_type=F32)
        mine = lax.broadcasted_iota(I32, (TILES, WB), 0) == band
        east, north, density, gust = (
            jnp.sum(jnp.where(mine, mixed[i * 64 : i * 64 + 64], 0.0), axis=0, keepdims=True) for i in range(4)
        )
        speed = jnp.sqrt(east * east + north * north + 1.0)
        friction = jnp.sqrt(0.001 * (0.8 + 0.065 * speed)) * speed * (1.0 + 0.15 * gust)
        pull = 28.0 * friction
        share = 0.25 * (density / WATER_DENSITY)
        spread = lambda v: jnp.broadcast_to(v, (8, WB))
        east8, north8, speed8, pull8 = spread(east), spread(north), spread(speed), spread(pull)
        m0 = jnp.zeros((8, WB), F32)
        ms, mk, sx, sy = m0, m0, m0, m0
        for g in range(3):
            cos8 = jnp.concatenate([dir_ref[0, 8 * g : 8 * g + 8, :]] * (WB // 128), axis=1)
            sin8 = jnp.concatenate([dir_ref[1, 8 * g : 8 * g + 8, :]] * (WB // 128), axis=1)
            push = pull8 * ((east8 * cos8 + north8 * sin8) / speed8)
            stress = jnp.zeros((8, WB), F32)
            for i in range(GS):
                spec = spec_ref[i, 8 * g : 8 * g + 8, cols]
                m0 = m0 + spec
                ms = ms + spec * tab_ref[INV_OMEGA, base + i]
                mk = mk + spec * tab_ref[INV_ROOT, base + i]
                excess = jnp.maximum(push * tab_ref[INV_C, base + i] - 1.0, 0.0)
                stress = stress + (excess * tab_ref[OMEGA_C, base + i]) * spec
            sx = sx + stress * cos8
            sy = sy + stress * sin8
        down = lambda v: jnp.sum(v, axis=0, keepdims=True)
        for n, row in enumerate((down(m0), down(ms), down(mk), down(sx) * share, down(sy) * share)):
            for half in range(WB // 128):
                mom_ref[pl.ds(n * 16 + c * (WB // 128) + half, 1), :] = row[:, half * 128 : half * 128 + 128]
        for n, row in enumerate((east, north, density, speed, friction)):
            for half in range(WB // 128):
                wind_ref[pl.ds(n * 16 + c * (WB // 128) + half, 1), :] = row[:, half * 128 : half * 128 + 128]
        return carry

    lax.fori_loop(0, PTS // WB, block, 0)


def field_kernel(freq_ref, m0_ref, m1_ref, m2_ref, m3_ref, wind_ref, slot_ref, weight_ref, diss_ref, sums_ref, own_ref):
    moments = m0_ref[...] + m1_ref[...] + m2_ref[...] + m3_ref[...]
    total, inv_sigma, inv_root, stress_e, stress_n = (moments[16 * n : 16 * n + 16] for n in range(5))
    east, north, density, speed, friction = (wind_ref[16 * n : 16 * n + 16, :] for n in range(5))
    mean_sigma = total / inv_sigma
    mean_wavenum = jnp.square(total / inv_root)
    steepness = mean_wavenum * mean_wavenum * total * E_UNIT
    diss_ref[...] = DISSIP_COEF * mean_sigma * jnp.square(steepness / STEEP_PM) / mean_wavenum
    scale = WATER_DENSITY / density * G_ACC * E_UNIT
    friction_sq = friction * friction
    east_ratio = scale * stress_e / friction_sq
    north_ratio = scale * stress_n / friction_sq
    aligned = (east_ratio * east + north_ratio * north) / speed
    charnock = 1.0 / jnp.sqrt(1.0 - 0.9 * aligned / (1.0 + jnp.abs(aligned)))
    height = 4.0 * jnp.sqrt(E_UNIT * total)
    f = freq_ref[0]
    own_ref[...] = jnp.where(f == 0, east_ratio, jnp.where(f == 1, north_ratio, jnp.where(f == 2, charnock, height)))

    def block(c, acc):
        cols = pl.ds(pl.multiple_of(c * WB, WB), WB)
        weights, band = weight_matrix(slot_ref, weight_ref, cols, WB)
        w0, w1 = parts2(weights)
        field = jnp.concatenate([own_ref[pl.ds(c * (WB // 128) + half, 1), :] for half in range(WB // 128)], axis=1)
        spread = jnp.where(lax.broadcasted_iota(I32, (TILES, WB), 0) == band, field, 0.0)
        f0, f1 = parts2(spread)
        left = jnp.concatenate([f0, f1, f0], axis=1)
        right = jnp.concatenate([w0, w0, w1], axis=1)
        return acc + lax.dot_general(left, right, (((1,), (1,)), ((), ())), preferred_element_type=F32)

    acc = lax.fori_loop(0, PTS // WB, block, jnp.zeros((TILES, CAP), F32))
    for half in range(2):
        sums_ref[:, half, :] = acc[:, half * 128 : half * 128 + 128]


def band_kernel(arrived_ref, rows_ref, out_ref):
    def eight_tiles(q, acc):
        ones, values = [], []
        for t in range(8):
            index = rows_ref[pl.ds(q * 8 + t, 1), :]
            tile = arrived_ref[q * 8 + t]
            row = jnp.concatenate([tile[0:1, :], tile[1:2, :]], axis=1)
            v0, v1 = parts2(row)
            high = lax.broadcasted_iota(I32, (16, CAP), 0) == (index >> 7)
            v0, v1 = v0.astype(F32), v1.astype(F32)
            values.append(jnp.concatenate([jnp.where(high, v0, 0.0), jnp.where(high, v1, 0.0)], axis=0).astype(BF))
            ones.append((lax.broadcasted_iota(I32, (128, CAP), 0) == (index & 127)).astype(F32).astype(BF))
        left = jnp.concatenate(ones, axis=1)
        right = jnp.concatenate(values, axis=1)
        return acc + lax.dot_general(left, right, (((1,), (1,)), ((), ())), preferred_element_type=F32)

    acc = lax.fori_loop(0, TILES // 8, eight_tiles, jnp.zeros((128, 32), F32))
    out_ref[...] = jnp.transpose(acc[:, :16] + acc[:, 16:])


ROLL = 6
KCOPIES = 30
NB = 512


def move_kernel(tab_ref, freq_ref, spec_ref, low_ref, high_ref, near_ref, out_ref, x_ref):
    base = freq_ref[0] * GS

    def put(ref, source, target):
        for kp in range(KCOPIES):
            k = (kp + ND - ROLL) % ND
            v = ref[:, k, source]
            p0 = v.astype(BF).astype(F32)
            x_ref[kp * 16 : kp * 16 + 16, target] = jnp.concatenate([p0, v - p0], axis=0).astype(BF)

    put(low_ref, slice(0, 128), slice(0, 128))
    put(high_ref, slice(0, 128), slice(EXT - 128, EXT))

    def put_block(h, carry):
        put(spec_ref, pl.ds(pl.multiple_of(h * 128, 128), 128), pl.ds(pl.multiple_of(h * 128 + 128, 128), 128))
        return carry

    lax.fori_loop(0, PTS // 128, put_block, 0)
    which = lax.broadcasted_iota(I32, (8, NB), 0)
    courant = jnp.zeros((8, NB), F32)
    for i in range(GS):
        courant = jnp.where(which == i, tab_ref[COURANT, base + i], courant)

    def block(c, carry):
        cols = pl.ds(pl.multiple_of(c * NB, NB), NB)
        got = []
        for n, first in enumerate((0, 12, 6, 18)):
            index = near_ref[n : n + 1, cols].astype(jnp.int16)
            hot = jnp.where(
                lax.broadcasted_iota(jnp.int16, (EXT, NB), 0) == index, jnp.ones((), BF), jnp.zeros((), BF)
            )
            got.append(jnp.dot(x_ref[first * 16 : first * 16 + 192, :], hot, preferred_element_type=F32))
        for k in range(ND):
            a = (k + ROLL) % ND
            x_of = got[0] if a < 12 else got[1]
            a = a % 12
            y_of = got[2] if k < 12 else got[3]
            b = k % 12
            from_x = x_of[a * 16 : a * 16 + 8] + x_of[a * 16 + 8 : a * 16 + 16]
            from_y = y_of[b * 16 : b * 16 + 8] + y_of[b * 16 + 8 : b * 16 + 16]
            spec = spec_ref[:, k, cols]
            out_ref[:, k, cols] = (
                spec - (courant * abs(COS[k])) * (spec - from_x) - (courant * abs(SIN[k])) * (spec - from_y)
            )
        return carry

    lax.fori_loop(0, PTS // NB, block, 0)


def source_kernel(tab_ref, freq_ref, moved_ref, wind_ref, diss_ref, dir_ref, out_ref):
    base = freq_ref[0] * GS + pl.program_id(0) * 2

    def block(c, carry):
        cols = pl.ds(pl.multiple_of(c * 128, 128), 128)
        row = lambda n: jnp.broadcast_to(wind_ref[pl.ds(n * 16 + c, 1), :], (8, 128))
        east, north, density, speed, friction = (row(n) for n in range(5))
        loss = jnp.broadcast_to(diss_ref[pl.ds(c, 1), :], (8, 128))
        share = 0.25 * (density / WATER_DENSITY)
        pull = 28.0 * friction / speed
        for g in range(3):
            push = pull * (east * dir_ref[0, 8 * g : 8 * g + 8, :] + north * dir_ref[1, 8 * g : 8 * g + 8, :])
            for i in range(2):
                excess = jnp.maximum(push * tab_ref[INV_C, base + i] - 1.0, 0.0)
                growth = share * excess * tab_ref[OMEGA, base + i] - loss * tab_ref[WAVENUM, base + i]
                out_ref[i, 8 * g : 8 * g + 8, cols] = moved_ref[i, 8 * g : 8 * g + 8, cols] * jnp.exp(DT_SRC * growth)
        return carry

    lax.fori_loop(0, PTS // 128, block, 0)


SMEM = pl.BlockSpec(memory_space=pltpu.SMEM)
VMEM = pl.BlockSpec(memory_space=pltpu.VMEM)


def params(mib):
    return pltpu.CompilerParams(vmem_limit_bytes=mib * 2**20)


def shape(*dims):
    return jax.ShapeDtypeStruct(dims, F32)


def on_device(spectrum, forcing, send_rows, point_slot, remap_weight, neighbours, halo_send):
    table = jnp.asarray(frequency_table())
    dirs = jnp.asarray(direction_tiles())
    freq = lax.axis_index("freq").astype(I32).reshape(1)

    outgoing = pl.pallas_call(
        outgoing_kernel, out_shape=shape(TILES, 8, 128), name="outgoing", compiler_params=params(16)
    )(forcing, send_rows)
    arrived = lax.all_to_all(outgoing, "tile", split_axis=0, concat_axis=0, tiled=True)

    to_before, to_after = pl.pallas_call(
        rim_kernel, out_shape=(shape(GS, ND, RIM), shape(GS, ND, RIM)), name="rims", compiler_params=params(16)
    )(spectrum, halo_send.reshape(2, RIM))
    up = [(d, d + 1) for d in range(TILES - 1)]
    low_rim = lax.ppermute(to_after, "tile", up)
    high_rim = lax.ppermute(to_before, "tile", [(b, a) for a, b in up])

    moved = pl.pallas_call(
        move_kernel,
        out_shape=shape(GS, ND, PTS),
        in_specs=[SMEM, SMEM, VMEM, VMEM, VMEM, VMEM],
        scratch_shapes=[pltpu.VMEM((KCOPIES * 16, EXT), BF)],
        name="move",
        compiler_params=params(48),
    )(table, freq, spectrum, low_rim, high_rim, neighbours)

    wind, moments = pl.pallas_call(
        wind_kernel,
        out_shape=(shape(80, 128), shape(80, 128)),
        in_specs=[SMEM, SMEM] + [VMEM] * 5,
        scratch_shapes=[pltpu.VMEM((256, 6 * 256), BF)],
        name="wind",
        compiler_params=params(32),
    )(table, freq, arrived, point_slot, remap_weight, spectrum, dirs)
    others = [lax.ppermute(moments, "freq", [(i, (i + n) % 4) for i in range(4)]) for n in (1, 2, 3)]

    diss, slot_sums = pl.pallas_call(
        field_kernel,
        out_shape=(shape(16, 128), shape(TILES, 2, 128)),
        in_specs=[SMEM] + [VMEM] * 7,
        scratch_shapes=[pltpu.VMEM((16, 128), F32)],
        name="fields",
        compiler_params=params(32),
    )(freq, moments, *others, wind, point_slot, remap_weight)
    arrived_sums = lax.all_to_all(slot_sums, "tile", split_axis=0, concat_axis=0, tiled=True)

    whole = lambda s: (0, 0)
    new_spectrum = pl.pallas_call(
        source_kernel,
        out_shape=shape(GS, ND, PTS),
        grid=(GS // 2,),
        in_specs=[
            SMEM,
            SMEM,
            pl.BlockSpec((2, ND, PTS), lambda s: (s, 0, 0)),
            pl.BlockSpec((80, 128), whole),
            pl.BlockSpec((16, 128), whole),
            pl.BlockSpec((2, ND, 128), lambda s: (0, 0, 0)),
        ],
        out_specs=pl.BlockSpec((2, ND, PTS), lambda s: (s, 0, 0)),
        name="source",
        compiler_params=params(16),
    )(table, freq, moved, wind, diss, dirs)

    returned = pl.pallas_call(
        band_kernel, out_shape=shape(16, 128), name="band", compiler_params=params(32)
    )(arrived_sums, send_rows)
    return (new_spectrum, returned.reshape(1, PTS))


def solution(mesh):
    placed = (
        P("freq", None, "tile"),
        P(None, "tile"),
        P("tile", None),
        P(None, "tile"),
        P(None, "tile"),
        P(None, "tile"),
        P("tile"),
    )
    return jax.shard_map(
        on_device,
        mesh=mesh,
        in_specs=placed,
        out_specs=(P("freq", None, "tile"), P("freq", "tile")),
        check_vma=False,
    )
```

time: 321 us -> 89.2 us (0.28)
  local copies, waits for them, and re-layouts: 212 us -> 5.97 us
  Pallas kernels: 0 us -> 32.1 us
  other arithmetic: 27.4 us -> 0 us
  matrix products: 27.1 us -> 0 us
  waiting for transfers between devices: 4.23 us -> 19.7 us
  blocking collectives: 14.3 us -> 0 us
    gather x12 -> x0, local copies, waits for them, and re-layouts: 197 us -> none  [the longest x2 60.4 us: on_device(): outgoing = forcing[:, send_rows]]
    pallas_call x0 -> x7, Pallas kernels: none -> 32.1 us  [the longest x1 11.9 us: on_device(): pl.pallas_call(move_kernel, out_shape=shape(GS, ND, PTS), in_specs=[SMEM,...]
    dot_general x12 -> x0, matrix products: 27.1 us -> none  [add_block(): jnp.einsum('frh,rl->fhl', weighted, lower_table, precision=lax.Precision....]
    psum x1 -> x0, blocking collectives: 14.3 us -> none  [on_device(): moments = lax.psum(local_moments, 'freq')]
    concatenate x1 -> x0, other arithmetic: 9.87 us -> none  [on_device(): jnp.concatenate([rim_cells[:, :, :rim_width], spectrum, rim_cells[:, :, -...]
    all_to_all x2, waiting for transfers between devices: 4.22 us -> 12 us  [the longest x1 12 us: on_device(): lax.all_to_all(outgoing, 'tile', split_axis=0, concat_axis=0, tiled=True)]
    mul x7 -> x0, other arithmetic: 7.76 us -> none  [the longest x1 4.75 us: on_device(): new_spectrum = moved * jnp.exp(DT_SRC * growth)]
    ppermute x2 -> x5, waiting for transfers between devices: 0.01 us -> 7.67 us  [the longest x1 4 us: on_device(): high_rim = lax.ppermute(to_before, 'tile', [(b, a) for a, b in up])]
  transfers between devices with their start and end apart: 4 -> 7, of which waited for: 1 -> 4; matrix products, arithmetic and copies ran while one was open for 56% -> 0% of each run, Pallas kernels for 0% -> 20%
where the time goes in v1:
time: 89.2 us; the launch traced here: 88.3 us
  Pallas kernels  32.1 us (36%)
  starting transfers between devices  29.8 us (33%)
  waiting for transfers between devices  19.7 us (22%)
  local copies, waits for them, and re-layouts  5.97 us (7%)
    all_to_all x1, starting transfers between devices, on_device(): lax.all_to_all(outgoing, 'tile', split_axis=0, concat_axis=0, tiled=True)  13.2 us
    all_to_all x1, waiting for transfers between devices, on_device(): lax.all_to_all(outgoing, 'tile', split_axis=0, concat_axis=0, tiled=True)  12 us
    pallas_call x1, Pallas kernels, on_device(): pl.pallas_call(move_kernel, out_shape=shape(GS, ND, PTS), in_specs=[SMEM,...  11.9 us
    all_to_all x1, starting transfers between devices, on_device(): lax.all_to_all(slot_sums, 'tile', split_axis=0, concat_axis=0, tiled=True)  7.53 us
    pallas_call x1, Pallas kernels, on_device(): pl.pallas_call(wind_kernel, out_shape=(shape(80, 128), shape(80, 128)), i...  6.08 us
    unnamed x26, local copies, waits for them, and re-layouts  5.97 us
    ppermute x1, waiting for transfers between devices, on_device(): high_rim = lax.ppermute(to_before, 'tile', [(b, a) for a, b in up])  4 us
    ppermute x3, starting transfers between devices, on_device(): lax.ppermute(moments, 'freq', [(i, (i + n) % 4) for i in range(4)])  3.67 us
  transfers between devices with their start and end apart: 7, of which 4 were waited for; matrix products, arithmetic and copies ran while one was open for 0% of the time, Pallas kernels for 20%

profile of v1, /device:TPU:1, one launch (start us, length us, event | category | flops | bytes accessed | tf_op | source)
XLA Modules:
  0.0 88.3 jit_solution(6188666003029371195)
XLA Ops:
  0.6 0.0 copy-start.2
  0.6 0.8 copy-done.2
  1.5 0.8 copy-done.11
  2.2 2.4 %outgoing.1 = f32[64,8,128]{2,1,0:T(8,128)} custom-call(f32[4,2048]{1,0:T(4,128)S(1)} %copy-done.11, s32[64,256]{1,0:T(8,128)S(1)} %copy-done.2), custom_call_target="tpu_custom_call" | custom-call | tf_op jit(solution)/shard_map/outgoing/pallas_call | solution.py:319
  4.7 13.2 %all-to-all-start = ((f32[64,8,128]{2,1,0:T(8,128)}), f32[64,8,128]{2,1,0:T(8,128)S(1)}, u32[]{:S(2)}, u32[]{:S(2)}) async-start(f32[64,8,128]{2,1,0:T(8,128)} %outgoing.1), calls=%async_computation | async-start | bytes 524288 | tf_op jit(solution)/shard_map/all_to_all | solution.py:322
  17.8 12.0 %all-to-all-done.arrived_ref = f32[64,8,128]{2,1,0:T(8,128)S(1)} async-done(((f32[64,8,128]{2,1,0:T(8,128)}), f32[64,8,128]{2,1,0:T(8,128)S(1)}, u32[]{:S(2)}, u32[]{:S(2)}) %all-to-all-start) | async-done | bytes 262176 | tf_op jit(solution)/shard_map/all_to_all | solution.py:322
  29.8 1.4 %copy-done = f32[8,24,2048]{2,1,0:T(8,128)S(1)} copy-done((f32[8,24,2048]{2,1,0:T(8,128)S(1)}, f32[8,24,2048]{2,1,0:T(8,128)}, u32[]{:S(2)}) %copy-start) | copy-done | bytes 1572888
  31.2 0.8 copy-done.4
  32.0 0.8 copy-done.5
  32.8 0.7 copy-done.6
  33.5 0.7 copy-done.8
  34.2 6.1 %wind.1 = (f32[80,128]{1,0:T(8,128)S(1)}, f32[80,128]{1,0:T(8,128)S(1)}) custom-call(f32[7,32]{1,0:T(8,128)S(1)} %copy-done.8, s32[1]{0:T(128)} %bitcast.freq_ref, f32[64,8,128]{2,1,0:T(8,128)S(1)} %all-to-all-done.arrived_ref, s32[4,2048]{1,0:T(4,128)S(1)} %copy-done.4, f32[4,2048]{1,0:T(4,128)S(1)} %copy-done.5, f32[8,24,2048]{2,1,0:T(8,128)S(1)} %copy-done, ...), custom_call_target="tpu_custom_call" | custom-call | tf_op jit(solution)/shard_map/wind/pallas_call | solution.py:340
  40.3 2.5 %collective-permute-start.4 = (f32[80,128]{1,0:T(8,128)S(1)}, f32[80,128]{1,0:T(8,128)S(1)}, u32[]{:S(2)}, u32[]{:S(2)}) collective-permute-start(f32[80,128]{1,0:T(8,128)S(1)} %get-tuple-element.11.m0_ref), channel_id=1, source_target_pairs={{0,3},{1,0},{2,1},{3,2},{4,7},{5,4},{6,5},{7,6},{8,11},{9,8},{10,9... | collective-permute-start | bytes 122888 | tf_op jit(solution)/shard_map/ppermute | solution.py:348
  42.8 0.5 collective-permute-start.3
  43.3 0.6 collective-permute-start.2
  43.9 0.0 collective-permute-done.4.m3_ref
  43.9 3.3 %collective-permute-done.3.m2_ref = f32[80,128]{1,0:T(8,128)S(1)} collective-permute-done((f32[80,128]{1,0:T(8,128)S(1)}, f32[80,128]{1,0:T(8,128)S(1)}, u32[]{:S(2)}, u32[]{:S(2)}) %collective-permute-start.3) | collective-permute-done | bytes 40992 | tf_op jit(solution)/shard_map/ppermute | solution.py:348
  47.2 0.4 collective-permute-done.2.m1_ref
  47.6 3.2 %fields.1 = (f32[16,128]{1,0:T(8,128)S(1)}, f32[64,2,128]{2,1,0:T(2,128)}) custom-call(s32[1]{0:T(128)} %bitcast.freq_ref, f32[80,128]{1,0:T(8,128)S(1)} %get-tuple-element.11.m0_ref, f32[80,128]{1,0:T(8,128)S(1)} %collective-permute-done.2.m1_ref, f32[80,128]{1,0:T(8,128)S(1)} %collective-permute-done.3.m2_ref, ...), custom_call_target="tpu_custom_call" | custom-call | tf_op jit(solution)/shard_map/fields/pallas_call | solution.py:350
  50.8 7.5 %all-to-all-start.1 = ((f32[64,2,128]{2,1,0:T(2,128)}), f32[64,2,128]{2,1,0:T(2,128)S(1)}, u32[]{:S(2)}, u32[]{:S(2)}) async-start(f32[64,2,128]{2,1,0:T(2,128)} %get-tuple-element.13), calls=%async_computation.1 | async-start | bytes 131072 | tf_op jit(solution)/shard_map/all_to_all | solution.py:358
  58.3 0.0 copy-done.12
  58.3 1.9 %rims.1 = (f32[8,24,128]{2,1,0:T(8,128)S(1)}, f32[8,24,128]{2,1,0:T(8,128)S(1)}) custom-call(f32[8,24,2048]{2,1,0:T(8,128)S(1)} %copy-done.1, s32[2,128]{1,0:T(2,128)S(1)} %bitcast.3), custom_call_target="tpu_custom_call" | custom-call | tf_op jit(solution)/shard_map/rims/pallas_call | solution.py:324
  60.3 3.5 %collective-permute-start = (f32[8,24,128]{2,1,0:T(8,128)S(1)}, f32[8,24,128]{2,1,0:T(8,128)S(1)}, u32[]{:S(2)}, u32[]{:S(2)}) collective-permute-start(f32[8,24,128]{2,1,0:T(8,128)S(1)} %get-tuple-element.8), channel_id=1, source_target_pairs={{0,4},{4,8},{8,12},{12,16},{16,20},{20,24},{24,28},{28,32},{32,36}... | collective-permute-start | bytes 294920 | tf_op jit(solution)/shard_map/ppermute | solution.py:328
  63.8 0.0 copy-start.7
  63.8 1.9 %collective-permute-start.1 = (f32[8,24,128]{2,1,0:T(8,128)S(1)}, f32[8,24,128]{2,1,0:T(8,128)S(1)}, u32[]{:S(2)}, u32[]{:S(2)}) collective-permute-start(f32[8,24,128]{2,1,0:T(8,128)S(1)} %get-tuple-element.9), channel_id=1, source_target_pairs={{4,0},{8,4},{12,8},{16,12},{20,16},{24,20},{28,24},{32,28},{36,32}... | collective-permute-start | bytes 294920 | tf_op jit(solution)/shard_map/ppermute | solution.py:329
  65.8 0.0 collective-permute-done.low_ref
  65.8 4.0 %collective-permute-done.1.high_ref = f32[8,24,128]{2,1,0:T(8,128)S(1)} collective-permute-done((f32[8,24,128]{2,1,0:T(8,128)S(1)}, f32[8,24,128]{2,1,0:T(8,128)S(1)}, u32[]{:S(2)}, u32[]{:S(2)}) %collective-permute-start.1) | collective-permute-done | bytes 98336 | tf_op jit(solution)/shard_map/ppermute | solution.py:329
  69.8 11.9 %move.1.moved_ref = f32[8,24,2048]{2,1,0:T(8,128)S(1)} custom-call(f32[7,32]{1,0:T(8,128)S(1)} %copy-done.9, s32[1]{0:T(128)} %bitcast.freq_ref, f32[8,24,2048]{2,1,0:T(8,128)S(1)} %copy-done.1, f32[8,24,128]{2,1,0:T(8,128)S(1)} %collective-permute-done.low_ref, f32[8,24,128]{2,1,0:T(8,128)S(1)} %collective-permute-done.1.high_ref, s32[4,2048]{1,0:T(4,128)S(1)} %copy-done.10), custom_call_target="tpu_custom_call" | custom-call | tf_op jit(solution)/shard_map/move/pallas_call | solution.py:331
  81.7 0.0 copy-start.3
  81.7 3.5 %source.1 = f32[8,24,2048]{2,1,0:T(8,128)} custom-call(f32[7,32]{1,0:T(8,128)S(1)} %copy-done.9, s32[1]{0:T(128)} %bitcast.freq_ref, f32[8,24,2048]{2,1,0:T(8,128)S(1)} %move.1.moved_ref, f32[80,128]{1,0:T(8,128)S(1)} %get-tuple-element.10.wind_ref, f32[16,128]{1,0:T(8,128)S(1)} %get-tuple-element.12.diss_ref, f32[2,24,128]{2,1,0:T(8,128)S(1)} %copy-done.7), custom_call_target="tpu_custom_call" | custom-call | tf_op jit(solution)/shard_map/source/pallas_call | solution.py:361
  85.3 0.0 all-to-all-done.1.arrived_ref
  85.3 3.0 %band.1 = f32[16,128]{1,0:T(8,128)} custom-call(f32[64,2,128]{2,1,0:T(2,128)S(1)} %all-to-all-done.1.arrived_ref, s32[64,256]{1,0:T(8,128)S(1)} %copy-done.3), custom_call_target="tpu_custom_call" | custom-call | tf_op jit(solution)/shard_map/band/pallas_call | solution.py:378
  (15 shorter events, 0.0 us)
Async XLA Ops:
  0.6 0.8 copy-start.2
  1.5 0.8 copy-start.11
  2.2 56.1 %copy-start.12 = (s32[256]{0:T(256)S(1)}, s32[256]{0:T(256)}, u32[]{:S(2)}) copy-start(s32[256]{0:T(256)} %param.15) | copy-start | bytes 3076
  4.7 25.2 %all-to-all-start = ((f32[64,8,128]{2,1,0:T(8,128)}), f32[64,8,128]{2,1,0:T(8,128)S(1)}, u32[]{:S(2)}, u32[]{:S(2)}) async-start(f32[64,8,128]{2,1,0:T(8,128)} %outgoing.1), calls=%async_computation | async-start | bytes 524288 | tf_op jit(solution)/shard_map/all_to_all | solution.py:322
  29.8 1.4 %copy-start = (f32[8,24,2048]{2,1,0:T(8,128)S(1)}, f32[8,24,2048]{2,1,0:T(8,128)}, u32[]{:S(2)}) copy-start(f32[8,24,2048]{2,1,0:T(8,128)} %spec_ref.5) | copy-start | bytes 4718596
  31.2 0.8 copy-start.4
  32.0 0.8 copy-start.5
  32.8 0.7 copy-start.6
  33.5 0.7 copy-start.8
  34.2 24.2 %copy-start.1 = (f32[8,24,2048]{2,1,0:T(8,128)S(1)}, f32[8,24,2048]{2,1,0:T(8,128)}, u32[]{:S(2)}) copy-start(f32[8,24,2048]{2,1,0:T(8,128)} %spec_ref.5) | copy-start | bytes 4718596
  34.2 35.6 %copy-start.9 = (f32[7,32]{1,0:T(8,128)S(1)}, f32[7,32]{1,0:T(8,128)}, u32[]{:S(2)}) copy-start(f32[7,32]{1,0:T(8,128)} %constant.8.clone.tab_ref) | copy-start | bytes 2692
  34.2 35.6 %copy-start.10 = (s32[4,2048]{1,0:T(4,128)S(1)}, s32[4,2048]{1,0:T(4,128)}, u32[]{:S(2)}) copy-start(s32[4,2048]{1,0:T(4,128)} %near_ref.1) | copy-start | bytes 98308
  40.3 3.7 %collective-permute-start.4 = (f32[80,128]{1,0:T(8,128)S(1)}, f32[80,128]{1,0:T(8,128)S(1)}, u32[]{:S(2)}, u32[]{:S(2)}) collective-permute-start(f32[80,128]{1,0:T(8,128)S(1)} %get-tuple-element.11.m0_ref), channel_id=1, source_target_pairs={{0,3},{1,0},{2,1},{3,2},{4,7},{5,4},{6,5},{7,6},{8,11},{9,8},{10,9... | collective-permute-start | bytes 122888 | tf_op jit(solution)/shard_map/ppermute | solution.py:348
  42.8 4.4 %collective-permute-start.3 = (f32[80,128]{1,0:T(8,128)S(1)}, f32[80,128]{1,0:T(8,128)S(1)}, u32[]{:S(2)}, u32[]{:S(2)}) collective-permute-start(f32[80,128]{1,0:T(8,128)S(1)} %get-tuple-element.11.m0_ref), channel_id=1, source_target_pairs={{0,2},{1,3},{2,0},{3,1},{4,6},{5,7},{6,4},{7,5},{8,10},{9,11},{10,... | collective-permute-start | bytes 122888 | tf_op jit(solution)/shard_map/ppermute | solution.py:348
  43.3 4.3 %collective-permute-start.2 = (f32[80,128]{1,0:T(8,128)S(1)}, f32[80,128]{1,0:T(8,128)S(1)}, u32[]{:S(2)}, u32[]{:S(2)}) collective-permute-start(f32[80,128]{1,0:T(8,128)S(1)} %get-tuple-element.11.m0_ref), channel_id=1, source_target_pairs={{0,1},{1,2},{2,3},{3,0},{4,5},{5,6},{6,7},{7,4},{8,9},{9,10},{10,1... | collective-permute-start | bytes 122888 | tf_op jit(solution)/shard_map/ppermute | solution.py:348
  50.8 34.5 %all-to-all-start.1 = ((f32[64,2,128]{2,1,0:T(2,128)}), f32[64,2,128]{2,1,0:T(2,128)S(1)}, u32[]{:S(2)}, u32[]{:S(2)}) async-start(f32[64,2,128]{2,1,0:T(2,128)} %get-tuple-element.13), calls=%async_computation.1 | async-start | bytes 131072 | tf_op jit(solution)/shard_map/all_to_all | solution.py:358
  60.3 5.5 %collective-permute-start = (f32[8,24,128]{2,1,0:T(8,128)S(1)}, f32[8,24,128]{2,1,0:T(8,128)S(1)}, u32[]{:S(2)}, u32[]{:S(2)}) collective-permute-start(f32[8,24,128]{2,1,0:T(8,128)S(1)} %get-tuple-element.8), channel_id=1, source_target_pairs={{0,4},{4,8},{8,12},{12,16},{16,20},{20,24},{24,28},{28,32},{32,36}... | collective-permute-start | bytes 294920 | tf_op jit(solution)/shard_map/ppermute | solution.py:328
  63.8 17.9 %copy-start.7 = (f32[2,24,128]{2,1,0:T(8,128)S(1)}, f32[2,24,128]{2,1,0:T(8,128)}, u32[]{:S(2)}) copy-start(f32[2,24,128]{2,1,0:T(8,128)} %constant.9.clone.dir_ref) | copy-start | bytes 73732
  63.8 5.9 %collective-permute-start.1 = (f32[8,24,128]{2,1,0:T(8,128)S(1)}, f32[8,24,128]{2,1,0:T(8,128)S(1)}, u32[]{:S(2)}, u32[]{:S(2)}) collective-permute-start(f32[8,24,128]{2,1,0:T(8,128)S(1)} %get-tuple-element.9), channel_id=1, source_target_pairs={{4,0},{8,4},{12,8},{16,12},{20,16},{24,20},{28,24},{32,28},{36,32}... | collective-permute-start | bytes 294920 | tf_op jit(solution)/shard_map/ppermute | solution.py:329
  81.7 3.6 %copy-start.3 = (s32[64,256]{1,0:T(8,128)S(1)}, s32[64,256]{1,0:T(8,128)}, u32[]{:S(2)}) copy-start(s32[64,256]{1,0:T(8,128)} %rows_ref.3) | copy-start | bytes 196612

commit v2 on v1

--- a/solution.py
+++ b/solution.py
@@ -227,40 +227,49 @@
 ROLL = 6
 KCOPIES = 30
 NB = 512
-
-
-def move_kernel(tab_ref, freq_ref, spec_ref, low_ref, high_ref, near_ref, out_ref, x_ref):
+HALF = PTS // 2
+
+
+def put_parts(ref, source, x_ref, target):
+    for kp in range(KCOPIES):
+        v = ref[:, (kp + ND - ROLL) % ND, source]
+        p0 = v.astype(BF).astype(F32)
+        x_ref[kp * 16 : kp * 16 + 16, target] = jnp.concatenate([p0, v - p0], axis=0).astype(BF)
+
+
+def operand_kernel(spec_ref, x_ref):
+    def put_block(h, carry):
+        cols = pl.ds(pl.multiple_of(h * 128, 128), 128)
+        put_parts(spec_ref, cols, x_ref, cols)
+        return carry
+
+    lax.fori_loop(0, PTS // 128, put_block, 0)
+
+
+def move_kernel(start, tab_ref, freq_ref, spec_ref, x_ref, low_ref, high_ref, near_ref, out_ref, rim_ref):
     base = freq_ref[0] * GS
-
-    def put(ref, source, target):
-        for kp in range(KCOPIES):
-            k = (kp + ND - ROLL) % ND
-            v = ref[:, k, source]
-            p0 = v.astype(BF).astype(F32)
-            x_ref[kp * 16 : kp * 16 + 16, target] = jnp.concatenate([p0, v - p0], axis=0).astype(BF)
-
-    put(low_ref, slice(0, 128), slice(0, 128))
-    put(high_ref, slice(0, 128), slice(EXT - 128, EXT))
-
-    def put_block(h, carry):
-        put(spec_ref, pl.ds(pl.multiple_of(h * 128, 128), 128), pl.ds(pl.multiple_of(h * 128 + 128, 128), 128))
-        return carry
-
-    lax.fori_loop(0, PTS // 128, put_block, 0)
+    put_parts(low_ref, slice(0, RIM), rim_ref, slice(0, RIM))
+    put_parts(high_ref, slice(0, RIM), rim_ref, slice(RIM, 2 * RIM))
     which = lax.broadcasted_iota(I32, (8, NB), 0)
     courant = jnp.zeros((8, NB), F32)
     for i in range(GS):
         courant = jnp.where(which == i, tab_ref[COURANT, base + i], courant)
 
+    def hot(rows, index):
+        match = lax.broadcasted_iota(jnp.int16, (rows, NB), 0) == index
+        return jnp.where(match, jnp.ones((), BF), jnp.zeros((), BF))
+
     def block(c, carry):
-        cols = pl.ds(pl.multiple_of(c * NB, NB), NB)
+        cols = pl.ds(pl.multiple_of(start + c * NB, NB), NB)
+        outs = pl.ds(pl.multiple_of(c * NB, NB), NB)
         got = []
         for n, first in enumerate((0, 12, 6, 18)):
-            index = near_ref[n : n + 1, cols].astype(jnp.int16)
-            hot = jnp.where(
-                lax.broadcasted_iota(jnp.int16, (EXT, NB), 0) == index, jnp.ones((), BF), jnp.zeros((), BF)
-            )
-            got.append(jnp.dot(x_ref[first * 16 : first * 16 + 192, :], hot, preferred_element_type=F32))
+            index = near_ref[n : n + 1, cols]
+            rim_index = jnp.where(index < RIM, index, jnp.where(index < RIM + PTS, 2 * RIM, index - PTS))
+            rows = slice(first * 16, first * 16 + 192)
+            own = jnp.dot(x_ref[rows, :], hot(PTS, (index - RIM).astype(jnp.int16)), preferred_element_type=F32)
+            rim = jnp.dot(rim_ref[rows, :], hot(2 * RIM, rim_index.astype(jnp.int16)), preferred_element_type=F32)
+            got.append(own + rim)
         for k in range(ND):
             a = (k + ROLL) % ND
             x_of = got[0] if a < 12 else got[1]
@@ -270,45 +279,79 @@
             from_x = x_of[a * 16 : a * 16 + 8] + x_of[a * 16 + 8 : a * 16 + 16]
             from_y = y_of[b * 16 : b * 16 + 8] + y_of[b * 16 + 8 : b * 16 + 16]
             spec = spec_ref[:, k, cols]
-            out_ref[:, k, cols] = (
+            out_ref[:, k, outs] = (
                 spec - (courant * abs(COS[k])) * (spec - from_x) - (courant * abs(SIN[k])) * (spec - from_y)
             )
         return carry
 
-    lax.fori_loop(0, PTS // NB, block, 0)
-
-
-def source_kernel(tab_ref, freq_ref, moved_ref, wind_ref, diss_ref, dir_ref, out_ref):
-    base = freq_ref[0] * GS + pl.program_id(0) * 2
-
-    def block(c, carry):
-        cols = pl.ds(pl.multiple_of(c * 128, 128), 128)
-        row = lambda n: jnp.broadcast_to(wind_ref[pl.ds(n * 16 + c, 1), :], (8, 128))
-        east, north, density, speed, friction = (row(n) for n in range(5))
-        loss = jnp.broadcast_to(diss_ref[pl.ds(c, 1), :], (8, 128))
-        share = 0.25 * (density / WATER_DENSITY)
-        pull = 28.0 * friction / speed
-        for g in range(3):
-            push = pull * (east * dir_ref[0, 8 * g : 8 * g + 8, :] + north * dir_ref[1, 8 * g : 8 * g + 8, :])
-            for i in range(2):
-                excess = jnp.maximum(push * tab_ref[INV_C, base + i] - 1.0, 0.0)
-                growth = share * excess * tab_ref[OMEGA, base + i] - loss * tab_ref[WAVENUM, base + i]
-                out_ref[i, 8 * g : 8 * g + 8, cols] = moved_ref[i, 8 * g : 8 * g + 8, cols] * jnp.exp(DT_SRC * growth)
-        return carry
-
-    lax.fori_loop(0, PTS // 128, block, 0)
+    lax.fori_loop(0, HALF // NB, block, 0)
+
+
+def source_kernel(tab_ref, freq_ref, moved0_ref, moved1_ref, wind_ref, diss_ref, dir_ref, out_ref, new_ref, sems):
+    base = freq_ref[0] * GS
+    copies = [pltpu.make_async_copy(new_ref.at[i], out_ref.at[i], sems.at[i]) for i in range(GS)]
+    for i in range(GS):
+
+        def block(c, carry):
+            cols = pl.ds(pl.multiple_of(c * 128, 128), 128)
+            for part, moved_ref in ((0, moved0_ref), (1, moved1_ref)):
+                at = c + part * (HALF // 128)
+                row = lambda n: jnp.broadcast_to(wind_ref[pl.ds(n * 16 + at, 1), :], (8, 128))
+                east, north, density, speed, friction = (row(n) for n in range(5))
+                loss = jnp.broadcast_to(diss_ref[pl.ds(at, 1), :], (8, 128))
+                share = 0.25 * (density / WATER_DENSITY)
+                pull = 28.0 * friction / speed
+                to = pl.ds(pl.multiple_of(part * HALF + c * 128, 128), 128)
+                for g in range(3):
+                    rows = slice(8 * g, 8 * g + 8)
+                    push = pull * (east * dir_ref[0, rows, :] + north * dir_ref[1, rows, :])
+                    excess = jnp.maximum(push * tab_ref[INV_C, base + i] - 1.0, 0.0)
+                    growth = share * excess * tab_ref[OMEGA, base + i] - loss * tab_ref[WAVENUM, base + i]
+                    new_ref[i, rows, to] = moved_ref[i, rows, cols] * jnp.exp(DT_SRC * growth)
+            return carry
+
+        lax.fori_loop(0, HALF // 128, block, 0)
+        copies[i].start()
+    for copy in copies:
+        copy.wait()
 
 
 SMEM = pl.BlockSpec(memory_space=pltpu.SMEM)
 VMEM = pl.BlockSpec(memory_space=pltpu.VMEM)
-
-
-def params(mib):
-    return pltpu.CompilerParams(vmem_limit_bytes=mib * 2**20)
-
-
-def shape(*dims):
-    return jax.ShapeDtypeStruct(dims, F32)
+ANY = pl.BlockSpec(memory_space=pl.ANY)
+
+
+def array(*dims, dtype=F32):
+    return jax.ShapeDtypeStruct(dims, dtype)
+
+
+def call(body, name, out, specs, scratch=(), mib=16, microseconds=1.0, out_specs=None, behind=False, mark=False):
+    out = list(out)
+    out_specs = [VMEM] * len(out) if out_specs is None else list(out_specs)
+    specs = [*specs, VMEM] if behind else specs
+    inputs = len(specs) - behind
+    outputs = len(out)
+    if mark:
+        out.append(array(8, 128))
+        out_specs.append(VMEM)
+
+    def kernel(*refs):
+        results = inputs + behind
+        if mark:
+            refs[results + outputs][...] = jnp.zeros((8, 128), F32)
+        body(*refs[:inputs], *refs[results : results + outputs], *refs[results + outputs + mark :])
+
+    cost = pl.CostEstimate(flops=0, bytes_accessed=int(microseconds * 3.0e6), transcendentals=0)
+    return pl.pallas_call(
+        kernel,
+        out_shape=out,
+        in_specs=specs,
+        out_specs=out_specs,
+        scratch_shapes=list(scratch),
+        name=name,
+        cost_estimate=cost,
+        compiler_params=pltpu.CompilerParams(vmem_limit_bytes=mib * 2**20),
+    )
 
 
 def on_device(spectrum, forcing, send_rows, point_slot, remap_weight, neighbours, halo_send):
@@ -316,68 +359,81 @@
     dirs = jnp.asarray(direction_tiles())
     freq = lax.axis_index("freq").astype(I32).reshape(1)
 
-    outgoing = pl.pallas_call(
-        outgoing_kernel, out_shape=shape(TILES, 8, 128), name="outgoing", compiler_params=params(16)
+    outgoing, mark = call(
+        outgoing_kernel, "outgoing", [array(TILES, 8, 128)], [VMEM] * 2, microseconds=2.4, mark=True
     )(forcing, send_rows)
     arrived = lax.all_to_all(outgoing, "tile", split_axis=0, concat_axis=0, tiled=True)
 
-    to_before, to_after = pl.pallas_call(
-        rim_kernel, out_shape=(shape(GS, ND, RIM), shape(GS, ND, RIM)), name="rims", compiler_params=params(16)
-    )(spectrum, halo_send.reshape(2, RIM))
+    to_before, to_after, mark = call(
+        rim_kernel, "rims", [array(GS, ND, RIM)] * 2, [VMEM] * 2, microseconds=1.9, behind=True, mark=True
+    )(spectrum, halo_send.reshape(2, RIM), mark)
     up = [(d, d + 1) for d in range(TILES - 1)]
     low_rim = lax.ppermute(to_after, "tile", up)
     high_rim = lax.ppermute(to_before, "tile", [(b, a) for a, b in up])
-
-    moved = pl.pallas_call(
-        move_kernel,
-        out_shape=shape(GS, ND, PTS),
-        in_specs=[SMEM, SMEM, VMEM, VMEM, VMEM, VMEM],
-        scratch_shapes=[pltpu.VMEM((KCOPIES * 16, EXT), BF)],
-        name="move",
-        compiler_params=params(48),
-    )(table, freq, spectrum, low_rim, high_rim, neighbours)
-
-    wind, moments = pl.pallas_call(
+    operand, mark = call(
+        operand_kernel,
+        "operand",
+        [array(KCOPIES * 16, PTS, dtype=BF)],
+        [VMEM],
+        microseconds=3.0,
+        behind=True,
+        mark=True,
+    )(spectrum, mark)
+
+    def move(half, mark):
+        return call(
+            lambda *refs: move_kernel(half * HALF, *refs),
+            f"move{half}",
+            [array(GS, ND, HALF)],
+            [SMEM, SMEM] + [VMEM] * 5,
+            [pltpu.VMEM((KCOPIES * 16, 2 * RIM), BF)],
+            mib=24,
+            microseconds=5.0,
+            behind=True,
+            mark=True,
+        )(table, freq, spectrum, operand, low_rim, high_rim, neighbours, mark)
+
+    moved0, mark = move(0, mark)
+    wind, moments, mark = call(
         wind_kernel,
-        out_shape=(shape(80, 128), shape(80, 128)),
-        in_specs=[SMEM, SMEM] + [VMEM] * 5,
-        scratch_shapes=[pltpu.VMEM((256, 6 * 256), BF)],
-        name="wind",
-        compiler_params=params(32),
-    )(table, freq, arrived, point_slot, remap_weight, spectrum, dirs)
+        "wind",
+        [array(80, 128), array(80, 128)],
+        [SMEM, SMEM] + [VMEM] * 5,
+        [pltpu.VMEM((256, 6 * 256), BF)],
+        mib=16,
+        microseconds=6.0,
+        behind=True,
+        mark=True,
+    )(table, freq, arrived, point_slot, remap_weight, spectrum, dirs, mark)
     others = [lax.ppermute(moments, "freq", [(i, (i + n) % 4) for i in range(4)]) for n in (1, 2, 3)]
-
-    diss, slot_sums = pl.pallas_call(
+    moved1, mark = move(1, mark)
+
+    diss, slot_sums = call(
         field_kernel,
-        out_shape=(shape(16, 128), shape(TILES, 2, 128)),
-        in_specs=[SMEM] + [VMEM] * 7,
-        scratch_shapes=[pltpu.VMEM((16, 128), F32)],
-        name="fields",
-        compiler_params=params(32),
-    )(freq, moments, *others, wind, point_slot, remap_weight)
+        "fields",
+        [array(16, 128), array(TILES, 2, 128)],
+        [SMEM] + [VMEM] * 7,
+        [pltpu.VMEM((16, 128), F32)],
+        mib=16,
+        microseconds=3.0,
+        behind=True,
+    )(freq, moments, *others, wind, point_slot, remap_weight, mark)
     arrived_sums = lax.all_to_all(slot_sums, "tile", split_axis=0, concat_axis=0, tiled=True)
 
-    whole = lambda s: (0, 0)
-    new_spectrum = pl.pallas_call(
+    new_spectrum, mark = call(
         source_kernel,
-        out_shape=shape(GS, ND, PTS),
-        grid=(GS // 2,),
-        in_specs=[
-            SMEM,
-            SMEM,
-            pl.BlockSpec((2, ND, PTS), lambda s: (s, 0, 0)),
-            pl.BlockSpec((80, 128), whole),
-            pl.BlockSpec((16, 128), whole),
-            pl.BlockSpec((2, ND, 128), lambda s: (0, 0, 0)),
-        ],
-        out_specs=pl.BlockSpec((2, ND, PTS), lambda s: (s, 0, 0)),
-        name="source",
-        compiler_params=params(16),
-    )(table, freq, moved, wind, diss, dirs)
-
-    returned = pl.pallas_call(
-        band_kernel, out_shape=shape(16, 128), name="band", compiler_params=params(32)
-    )(arrived_sums, send_rows)
+        "source",
+        [array(GS, ND, PTS)],
+        [SMEM, SMEM] + [VMEM] * 5,
+        [pltpu.VMEM((GS, ND, PTS), F32), pltpu.SemaphoreType.DMA((GS,))],
+        microseconds=3.0,
+        out_specs=[ANY],
+        mark=True,
+    )(table, freq, moved0, moved1, wind, diss, dirs)
+
+    (returned,) = call(
+        band_kernel, "band", [array(16, 128)], [VMEM] * 2, mib=16, microseconds=2.5, behind=True
+    )(arrived_sums, send_rows, mark)
     return (new_spectrum, returned.reshape(1, PTS))
 
 

time: 89.2 us -> 86.3 us (0.967)
  waiting for transfers between devices: 19.7 us -> 4.39 us
  local copies, waits for them, and re-layouts: 5.97 us -> 12.2 us
  starting transfers between devices: 29.8 us -> 33.3 us
  Pallas kernels: 32.1 us -> 34.6 us
    all_to_all x1, waiting for transfers between devices: 12 us -> 0.01 us  [on_device(): lax.all_to_all(outgoing, 'tile', split_axis=0, concat_axis=0, tiled=True)]
    unnamed x26 -> x42, local copies, waits for them, and re-layouts: 5.97 us -> 12.2 us
    ppermute x3, waiting for transfers between devices: 3.67 us -> 0.01 us  [on_device(): lax.ppermute(moments, 'freq', [(i, (i + n) % 4) for i in range(4)])]
    all_to_all x1, starting transfers between devices: 7.53 us -> 10.8 us  [on_device(): lax.all_to_all(slot_sums, 'tile', split_axis=0, concat_axis=0, tiled=True)]
    all_to_all x1, waiting for transfers between devices: 0.01 us -> 2.72 us  [on_device(): lax.all_to_all(slot_sums, 'tile', split_axis=0, concat_axis=0, tiled=True)]
    pallas_call x7 -> x9, Pallas kernels: 32.1 us -> 34.6 us  [the longest x2 11.1 us: move(): call(lambda *refs: move_kernel(half * HALF, *refs), f'move{half}', [array...]
    ppermute x1, waiting for transfers between devices: 4 us -> 1.66 us  [on_device(): high_rim = lax.ppermute(to_before, 'tile', [(b, a) for a, b in up])]
  transfers between devices with their start and end apart: 7 -> 7, of which waited for: 4 -> 2; matrix products, arithmetic and copies ran while one was open for 0% -> 0% of each run, Pallas kernels for 20% -> 23%
where the time goes in v2:
time: 86.3 us; the launch traced here: 85.3 us
  Pallas kernels  34.6 us (40%)
  starting transfers between devices  33.3 us (39%)
  local copies, waits for them, and re-layouts  12.2 us (14%)
  waiting for transfers between devices  4.39 us (5%)
    all_to_all x1, starting transfers between devices, on_device(): lax.all_to_all(outgoing, 'tile', split_axis=0, concat_axis=0, tiled=True)  13.3 us
    unnamed x42, local copies, waits for them, and re-layouts  12.2 us
    pallas_call x2, Pallas kernels, move(): call(lambda *refs: move_kernel(half * HALF, *refs), f'move{half}', [array...  11.1 us
    all_to_all x1, starting transfers between devices, on_device(): lax.all_to_all(slot_sums, 'tile', split_axis=0, concat_axis=0, tiled=True)  10.8 us
    pallas_call x1, Pallas kernels, on_device(): call(wind_kernel, 'wind', [array(80, 128), array(80, 128)], [SMEM, SMEM]...  6.42 us
    ppermute x3, starting transfers between devices, on_device(): lax.ppermute(moments, 'freq', [(i, (i + n) % 4) for i in range(4)])  3.69 us
    ppermute x1, starting transfers between devices, on_device(): low_rim = lax.ppermute(to_after, 'tile', up)  3.53 us
    pallas_call x1, Pallas kernels, on_device(): call(source_kernel, 'source', [array(GS, ND, PTS)], [SMEM, SMEM] + [VMEM]...  3.27 us
  transfers between devices with their start and end apart: 7, of which 2 were waited for; matrix products, arithmetic and copies ran while one was open for 0% of the time, Pallas kernels for 23%

profile of v2, /device:TPU:1, one launch (start us, length us, event | category | flops | bytes accessed | tf_op | source)
XLA Modules:
  0.0 85.3 jit_solution(16612426639789399454)
XLA Ops:
  0.6 0.8 copy-done.6
  1.5 0.8 copy-done.19
  2.2 2.4 %outgoing.1 = (f32[64,8,128]{2,1,0:T(8,128)}, f32[8,128]{1,0:T(8,128)S(1)}) custom-call(f32[4,2048]{1,0:T(4,128)S(1)} %copy-done.19, s32[64,256]{1,0:T(8,128)S(1)} %copy-done.6), custom_call_target="tpu_custom_call" | custom-call | bytes 7200000 | tf_op jit(solution)/shard_map/outgoing/pallas_call | solution.py:362
  4.7 13.3 %all-to-all-start = ((f32[64,8,128]{2,1,0:T(8,128)}), f32[64,8,128]{2,1,0:T(8,128)}, u32[]{:S(2)}, u32[]{:S(2)}) async-start(f32[64,8,128]{2,1,0:T(8,128)} %get-tuple-element.27), calls=%async_computation | async-start | bytes 524288 | tf_op jit(solution)/shard_map/all_to_all | solution.py:365
  18.0 1.4 %copy-done = f32[8,24,2048]{2,1,0:T(8,128)S(1)} copy-done((f32[8,24,2048]{2,1,0:T(8,128)S(1)}, f32[8,24,2048]{2,1,0:T(8,128)}, u32[]{:S(2)}) %copy-start) | copy-done | bytes 1572888
  19.4 0.7 copy-done.20
  20.1 2.6 %rims.1 = (f32[8,24,128]{2,1,0:T(8,128)}, f32[8,24,128]{2,1,0:T(8,128)}, f32[8,128]{1,0:T(8,128)S(1)}) custom-call(f32[8,24,2048]{2,1,0:T(8,128)S(1)} %copy-done, s32[2,128]{1,0:T(2,128)S(1)} %bitcast.3, f32[8,128]{1,0:T(8,128)S(1)} %get-tuple-element.20.refs_2_), custom_call_target="tpu_custom_call" | custom-call | bytes 5700000 | tf_op jit(solution)/shard_map/rims/pallas_call | solution.py:367
  22.7 3.5 %collective-permute-start = (f32[8,24,128]{2,1,0:T(8,128)}, f32[8,24,128]{2,1,0:T(8,128)}, u32[]{:S(2)}, u32[]{:S(2)}) collective-permute-start(f32[8,24,128]{2,1,0:T(8,128)} %get-tuple-element.23), channel_id=1, source_target_pairs={{0,4},{4,8},{8,12},{12,16},{16,20},{20,24},{24,28},{28,32},{32,36}... | collective-permute-start | bytes 294920 | tf_op jit(solution)/shard_map/ppermute | solution.py:371
  26.2 1.9 %collective-permute-start.1 = (f32[8,24,128]{2,1,0:T(8,128)}, f32[8,24,128]{2,1,0:T(8,128)}, u32[]{:S(2)}, u32[]{:S(2)}) collective-permute-start(f32[8,24,128]{2,1,0:T(8,128)} %get-tuple-element.24), channel_id=1, source_target_pairs={{4,0},{8,4},{12,8},{16,12},{20,16},{24,20},{28,24},{32,28},{36,32}... | collective-permute-start | bytes 294920 | tf_op jit(solution)/shard_map/ppermute | solution.py:372
  28.2 2.6 %operand.1 = (bf16[480,2048]{1,0:T(8,128)(2,1)S(1)}, f32[8,128]{1,0:T(8,128)S(1)}) custom-call(f32[8,24,2048]{2,1,0:T(8,128)S(1)} %copy-done.1, f32[8,128]{1,0:T(8,128)S(1)} %get-tuple-element.21.refs_1_), custom_call_target="tpu_custom_call" | custom-call | bytes 9000000 | tf_op jit(solution)/shard_map/operand/pallas_call | solution.py:373
  30.8 1.7 %collective-permute-done.1.refs_5_ = f32[8,24,128]{2,1,0:T(8,128)} collective-permute-done((f32[8,24,128]{2,1,0:T(8,128)}, f32[8,24,128]{2,1,0:T(8,128)}, u32[]{:S(2)}, u32[]{:S(2)}) %collective-permute-start.1) | collective-permute-done | bytes 98336 | tf_op jit(solution)/shard_map/ppermute | solution.py:372
  32.5 0.8 copy-done.10
  33.2 5.5 %move0.1 = (f32[8,24,1024]{2,1,0:T(8,128)S(1)}, f32[8,128]{1,0:T(8,128)S(1)}) custom-call(f32[7,32]{1,0:T(8,128)S(1)} %copy-done.18, s32[1]{0:T(128)} %bitcast.refs_1_.refs_0_, f32[8,24,2048]{2,1,0:T(8,128)S(1)} %copy-done.1, bf16[480,2048]{1,0:T(8,128)(2,1)S(1)} %get-tuple-element.22.refs_3_, f32[8,24,128]{2,1,0:T(8,128)} %collective-permute-done.refs_4_, ...), custom_call_target="tpu_custom_call" | custom-call | bytes 15000000 | tf_op jit(solution)/shard_map/move0/pallas_call | solution.py:384
  38.8 0.9 %copy-done.2 = f32[8,24,1024]{2,1,0:T(8,128)} copy-done((f32[8,24,1024]{2,1,0:T(8,128)}, f32[8,24,1024]{2,1,0:T(8,128)S(1)}, u32[]{:S(2)}) %copy-start.2) | copy-done | bytes 786456
  39.7 0.8 copy-done.12
  40.4 0.8 copy-done.14
  41.2 0.7 copy-done.16
  41.9 6.4 %wind.1 = (f32[80,128]{1,0:T(8,128)S(1)}, f32[80,128]{1,0:T(8,128)S(1)}, f32[8,128]{1,0:T(8,128)S(1)}) custom-call(f32[7,32]{1,0:T(8,128)S(1)} %copy-done.18, s32[1]{0:T(128)} %bitcast.refs_1_.refs_0_, f32[64,8,128]{2,1,0:T(8,128)} %all-to-all-done.refs_2_, s32[4,2048]{1,0:T(4,128)S(1)} %copy-done.12, f32[4,2048]{1,0:T(4,128)S(1)} %copy-done.14, ...), custom_call_target="tpu_custom_call" | custom-call | bytes 18000000 | tf_op jit(solution)/shard_map/wind/pallas_call | solution.py:397
  48.4 2.5 %collective-permute-start.4 = (f32[80,128]{1,0:T(8,128)S(1)}, f32[80,128]{1,0:T(8,128)S(1)}, u32[]{:S(2)}, u32[]{:S(2)}) collective-permute-start(f32[80,128]{1,0:T(8,128)S(1)} %get-tuple-element.32.refs_1_), channel_id=1, source_target_pairs={{0,3},{1,0},{2,1},{3,2},{4,7},{5,4},{6,5},{7,6},{8,11},{9,8},{10,9... | collective-permute-start | bytes 122888 | tf_op jit(solution)/shard_map/ppermute | solution.py:408
  50.9 0.5 collective-permute-start.3
  51.4 0.6 collective-permute-start.2
  52.1 5.5 %move1.1 = (f32[8,24,1024]{2,1,0:T(8,128)S(1)}, f32[8,128]{1,0:T(8,128)S(1)}) custom-call(f32[7,32]{1,0:T(8,128)S(1)} %copy-done.18, s32[1]{0:T(128)} %bitcast.refs_1_.refs_0_, f32[8,24,2048]{2,1,0:T(8,128)S(1)} %copy-done.1, bf16[480,2048]{1,0:T(8,128)(2,1)S(1)} %get-tuple-element.22.refs_3_, f32[8,24,128]{2,1,0:T(8,128)} %collective-permute-done.refs_4_, ...), custom_call_target="tpu_custom_call" | custom-call | bytes 15000000 | tf_op jit(solution)/shard_map/move1/pallas_call | solution.py:384
  57.6 0.9 %copy-done.4 = f32[8,24,1024]{2,1,0:T(8,128)} copy-done((f32[8,24,1024]{2,1,0:T(8,128)}, f32[8,24,1024]{2,1,0:T(8,128)S(1)}, u32[]{:S(2)}) %copy-start.4) | copy-done | bytes 786456
  58.5 3.2 %fields.1 = (f32[16,128]{1,0:T(8,128)S(1)}, f32[64,2,128]{2,1,0:T(2,128)}) custom-call(s32[1]{0:T(128)} %bitcast.refs_1_.refs_0_, f32[80,128]{1,0:T(8,128)S(1)} %get-tuple-element.32.refs_1_, f32[80,128]{1,0:T(8,128)S(1)} %collective-permute-done.2.refs_2_, f32[80,128]{1,0:T(8,128)S(1)} %collective-permute-done.3.refs_3_, ...), custom_call_target="tpu_custom_call" | custom-call | bytes 9000000 | tf_op jit(solution)/shard_map/fields/pallas_call | solution.py:411
  61.7 10.8 %all-to-all-start.1 = ((f32[64,2,128]{2,1,0:T(2,128)}), f32[64,2,128]{2,1,0:T(2,128)S(1)}, u32[]{:S(2)}, u32[]{:S(2)}) async-start(f32[64,2,128]{2,1,0:T(2,128)} %get-tuple-element.36), calls=%async_computation.1 | async-start | bytes 131072 | tf_op jit(solution)/shard_map/all_to_all | solution.py:421
  72.6 1.1 %copy-done.3 = f32[8,24,1024]{2,1,0:T(8,128)S(1)} copy-done((f32[8,24,1024]{2,1,0:T(8,128)S(1)}, f32[8,24,1024]{2,1,0:T(8,128)}, u32[]{:S(2)}) %copy-start.3) | copy-done | bytes 786456
  73.7 1.1 %copy-done.5 = f32[8,24,1024]{2,1,0:T(8,128)S(1)} copy-done((f32[8,24,1024]{2,1,0:T(8,128)S(1)}, f32[8,24,1024]{2,1,0:T(8,128)}, u32[]{:S(2)}) %copy-start.5) | copy-done | bytes 786456
  74.8 0.8 copy-done.9
  75.6 0.7 copy-done.17
  76.3 3.3 %source.1 = (f32[8,24,2048]{2,1,0:T(8,128)}, f32[8,128]{1,0:T(8,128)S(1)}) custom-call(f32[7,32]{1,0:T(8,128)S(1)} %copy-done.18, s32[1]{0:T(128)} %bitcast.refs_1_.refs_0_, f32[8,24,1024]{2,1,0:T(8,128)S(1)} %copy-done.3, f32[8,24,1024]{2,1,0:T(8,128)S(1)} %copy-done.5, f32[80,128]{1,0:T(8,128)S(1)} %copy-done.9, f32[16,128]{1,0:T(8,128)S(1)} %get-tuple-element.34.refs_5_, ...), custom_call_target="tpu_custom_call" | custom-call | bytes 9000000 | tf_op jit(solution)/shard_map/source/pallas_call | solution.py:423
  79.6 2.7 %all-to-all-done.1.refs_0_ = f32[64,2,128]{2,1,0:T(2,128)S(1)} async-done(((f32[64,2,128]{2,1,0:T(2,128)}), f32[64,2,128]{2,1,0:T(2,128)S(1)}, u32[]{:S(2)}, u32[]{:S(2)}) %all-to-all-start.1) | async-done | bytes 65568 | tf_op jit(solution)/shard_map/all_to_all | solution.py:421
  82.3 3.0 %band.1 = f32[16,128]{1,0:T(8,128)} custom-call(f32[64,2,128]{2,1,0:T(2,128)S(1)} %all-to-all-done.1.refs_0_, s32[64,256]{1,0:T(8,128)S(1)} %copy-done.7, f32[8,128]{1,0:T(8,128)S(1)} %get-tuple-element.37.refs_2_), custom_call_target="tpu_custom_call" | custom-call | bytes 7500000 | tf_op jit(solution)/shard_map/band/pallas_call | solution.py:434
  (33 shorter events, 0.1 us)
Async XLA Ops:
  0.6 0.8 copy-start.6
  1.5 0.8 copy-start.19
  4.7 35.0 %all-to-all-start = ((f32[64,8,128]{2,1,0:T(8,128)}), f32[64,8,128]{2,1,0:T(8,128)}, u32[]{:S(2)}, u32[]{:S(2)}) async-start(f32[64,8,128]{2,1,0:T(8,128)} %get-tuple-element.27), calls=%async_computation | async-start | bytes 524288 | tf_op jit(solution)/shard_map/all_to_all | solution.py:365
  18.0 1.4 %copy-start = (f32[8,24,2048]{2,1,0:T(8,128)S(1)}, f32[8,24,2048]{2,1,0:T(8,128)}, u32[]{:S(2)}) copy-start(f32[8,24,2048]{2,1,0:T(8,128)} %refs_2_.3) | copy-start | bytes 4718596
  19.4 0.7 copy-start.20
  20.1 8.0 %copy-start.1 = (f32[8,24,2048]{2,1,0:T(8,128)S(1)}, f32[8,24,2048]{2,1,0:T(8,128)}, u32[]{:S(2)}) copy-start(f32[8,24,2048]{2,1,0:T(8,128)} %refs_2_.3) | copy-start | bytes 4718596
  20.1 12.4 %copy-start.18 = (f32[7,32]{1,0:T(8,128)S(1)}, f32[7,32]{1,0:T(8,128)}, u32[]{:S(2)}) copy-start(f32[7,32]{1,0:T(8,128)} %constant.8.clone.refs_0_) | copy-start | bytes 2692
  22.7 8.1 %collective-permute-start = (f32[8,24,128]{2,1,0:T(8,128)}, f32[8,24,128]{2,1,0:T(8,128)}, u32[]{:S(2)}, u32[]{:S(2)}) collective-permute-start(f32[8,24,128]{2,1,0:T(8,128)} %get-tuple-element.23), channel_id=1, source_target_pairs={{0,4},{4,8},{8,12},{12,16},{16,20},{20,24},{24,28},{28,32},{32,36}... | collective-permute-start | bytes 294920 | tf_op jit(solution)/shard_map/ppermute | solution.py:371
  26.2 6.3 %collective-permute-start.1 = (f32[8,24,128]{2,1,0:T(8,128)}, f32[8,24,128]{2,1,0:T(8,128)}, u32[]{:S(2)}, u32[]{:S(2)}) collective-permute-start(f32[8,24,128]{2,1,0:T(8,128)} %get-tuple-element.24), channel_id=1, source_target_pairs={{4,0},{8,4},{12,8},{16,12},{20,16},{24,20},{28,24},{32,28},{36,32}... | collective-permute-start | bytes 294920 | tf_op jit(solution)/shard_map/ppermute | solution.py:372
  32.5 0.8 copy-start.10
  38.8 0.9 %copy-start.2 = (f32[8,24,1024]{2,1,0:T(8,128)}, f32[8,24,1024]{2,1,0:T(8,128)S(1)}, u32[]{:S(2)}) copy-start(f32[8,24,1024]{2,1,0:T(8,128)S(1)} %get-tuple-element.26.refs_2_) | copy-start | bytes 2359300
  39.6 12.4 %copy-start.11 = (s32[4,2048]{1,0:T(4,128)S(1)}, s32[4,2048]{1,0:T(4,128)}, u32[]{:S(2)}) copy-start(s32[4,2048]{1,0:T(4,128)} %refs_6_.6) | copy-start | bytes 98308
  39.7 0.8 copy-start.12
  40.4 0.8 copy-start.14
  41.2 0.7 copy-start.16
  48.3 10.2 %copy-start.8 = (f32[80,128]{1,0:T(8,128)}, f32[80,128]{1,0:T(8,128)S(1)}, u32[]{:S(2)}) copy-start(f32[80,128]{1,0:T(8,128)S(1)} %get-tuple-element.31.refs_5_.refs_4_) | copy-start | bytes 122884
  48.4 10.1 %collective-permute-start.4 = (f32[80,128]{1,0:T(8,128)S(1)}, f32[80,128]{1,0:T(8,128)S(1)}, u32[]{:S(2)}, u32[]{:S(2)}) collective-permute-start(f32[80,128]{1,0:T(8,128)S(1)} %get-tuple-element.32.refs_1_), channel_id=1, source_target_pairs={{0,3},{1,0},{2,1},{3,2},{4,7},{5,4},{6,5},{7,6},{8,11},{9,8},{10,9... | collective-permute-start | bytes 122888 | tf_op jit(solution)/shard_map/ppermute | solution.py:408
  50.9 7.6 %collective-permute-start.3 = (f32[80,128]{1,0:T(8,128)S(1)}, f32[80,128]{1,0:T(8,128)S(1)}, u32[]{:S(2)}, u32[]{:S(2)}) collective-permute-start(f32[80,128]{1,0:T(8,128)S(1)} %get-tuple-element.32.refs_1_), channel_id=1, source_target_pairs={{0,2},{1,3},{2,0},{3,1},{4,6},{5,7},{6,4},{7,5},{8,10},{9,11},{10,... | collective-permute-start | bytes 122888 | tf_op jit(solution)/shard_map/ppermute | solution.py:408
  51.4 7.1 %collective-permute-start.2 = (f32[80,128]{1,0:T(8,128)S(1)}, f32[80,128]{1,0:T(8,128)S(1)}, u32[]{:S(2)}, u32[]{:S(2)}) collective-permute-start(f32[80,128]{1,0:T(8,128)S(1)} %get-tuple-element.32.refs_1_), channel_id=1, source_target_pairs={{0,1},{1,2},{2,3},{3,0},{4,5},{5,6},{6,7},{7,4},{8,9},{9,10},{10,1... | collective-permute-start | bytes 122888 | tf_op jit(solution)/shard_map/ppermute | solution.py:408
  52.1 6.5 %copy-start.13 = (s32[4,2048]{1,0:T(4,128)S(1)}, s32[4,2048]{1,0:T(4,128)}, u32[]{:S(2)}) copy-start(s32[4,2048]{1,0:T(4,128)} %refs_6_.7) | copy-start | bytes 98308
  52.1 6.5 %copy-start.15 = (f32[4,2048]{1,0:T(4,128)S(1)}, f32[4,2048]{1,0:T(4,128)}, u32[]{:S(2)}) copy-start(f32[4,2048]{1,0:T(4,128)} %refs_7_.1) | copy-start | bytes 98308
  57.6 0.9 %copy-start.4 = (f32[8,24,1024]{2,1,0:T(8,128)}, f32[8,24,1024]{2,1,0:T(8,128)S(1)}, u32[]{:S(2)}) copy-start(f32[8,24,1024]{2,1,0:T(8,128)S(1)} %get-tuple-element.30.refs_3_) | copy-start | bytes 2359300
  58.5 23.8 %copy-start.7 = (s32[64,256]{1,0:T(8,128)S(1)}, s32[64,256]{1,0:T(8,128)}, u32[]{:S(2)}) copy-start(s32[64,256]{1,0:T(8,128)} %refs_1_.3) | copy-start | bytes 196612
  61.7 20.6 %all-to-all-start.1 = ((f32[64,2,128]{2,1,0:T(2,128)}), f32[64,2,128]{2,1,0:T(2,128)S(1)}, u32[]{:S(2)}, u32[]{:S(2)}) async-start(f32[64,2,128]{2,1,0:T(2,128)} %get-tuple-element.36), calls=%async_computation.1 | async-start | bytes 131072 | tf_op jit(solution)/shard_map/all_to_all | solution.py:421
  72.5 1.1 %copy-start.3 = (f32[8,24,1024]{2,1,0:T(8,128)S(1)}, f32[8,24,1024]{2,1,0:T(8,128)}, u32[]{:S(2)}) copy-start(f32[8,24,1024]{2,1,0:T(8,128)} %copy-done.2) | copy-start | bytes 2359300
  73.7 1.1 %copy-start.5 = (f32[8,24,1024]{2,1,0:T(8,128)S(1)}, f32[8,24,1024]{2,1,0:T(8,128)}, u32[]{:S(2)}) copy-start(f32[8,24,1024]{2,1,0:T(8,128)} %copy-done.4) | copy-start | bytes 2359300
  74.8 0.8 copy-start.9
  75.6 0.7 copy-start.17

commit v3 on v2

v3 whole, which is shorter than its diff:
```python
import functools
import math

import jax
import jax.numpy as jnp
from jax import lax
from jax.experimental import pallas as pl
from jax.experimental.pallas import tpu as pltpu
from jax.sharding import PartitionSpec as P

G_ACC = 9.81
WATER_DENSITY = 1025.0
FREQ_LOW = 0.03453
FREQ_RATIO = 1.1
E_UNIT = 0.001
DT_SRC = 120.0
COURANT_MAX = 0.7
DISSIP_COEF = 2.33e-05
STEEP_PM = 0.00302
TOP_EXPONENT = 31.0

NF = 32
ND = 24
GS = 8
PTS = 2048
TILES = 64
CAP = 256
RIM = 128
EXT = PTS + 2 * RIM

F32 = jnp.float32
BF = jnp.bfloat16
I32 = jnp.int32

THETA = [(k + 0.5) * 2.0 * math.pi / ND for k in range(ND)]
COS = [math.cos(t) for t in THETA]
SIN = [math.sin(t) for t in THETA]

OMEGA = [2.0 * math.pi * FREQ_LOW * FREQ_RATIO**i for i in range(GS)]
COURANT = [COURANT_MAX * FREQ_RATIO ** (-i) for i in range(GS)]


def group_scale():
    f = lax.axis_index("freq")
    pick = lambda v: jnp.where(f == 0, v[0], jnp.where(f == 1, v[1], jnp.where(f == 2, v[2], v[3]))).astype(F32)
    return pick([FREQ_RATIO ** (GS * n) for n in range(4)]), pick([FREQ_RATIO ** (-GS * n) for n in range(4)])


def by_sublane(values):
    which = lax.broadcasted_iota(I32, (8, 128), 0)
    tile = jnp.full((8, 128), values[7], F32)
    for n in range(7):
        tile = jnp.where(which == n, values[n], tile)
    return tile


def direction_tiles(values):
    return [by_sublane(values[8 * g : 8 * g + 8]) for g in range(3)]


def lane_gather(block, index):
    return jnp.take_along_axis(block, index, axis=1, mode="promise_in_bounds")


def parts2(x):
    first = x.astype(BF)
    return first, (x - first.astype(F32)).astype(BF)


def parts3(x):
    first = x.astype(BF)
    rest = x - first.astype(F32)
    second = rest.astype(BF)
    return first, second, (rest - second.astype(F32)).astype(BF)


ROLL = 6
KCOPIES = 30
NB = 512
HALF = PTS // 2
MOVE_SEMS = 10


def put_parts(ref, source, x_ref, target):
    for kp in range(KCOPIES):
        v = ref[:, (kp + ND - ROLL) % ND, source]
        p0 = v.astype(BF).astype(F32)
        x_ref[kp * 16 : kp * 16 + 16, target] = jnp.concatenate([p0, v - p0], axis=0).astype(BF)


def first_kernel(
    forcing_hbm, rows_hbm, list_hbm, spec_hbm, out_hbm, before_ref, after_ref, x_ref,
    forcing_ref, rows_ref, list_ref, spec_ref, out_ref, sems, out_sems,
):
    pairs = ((rows_hbm, rows_ref), (forcing_hbm, forcing_ref), (list_hbm, list_ref), (spec_hbm, spec_ref))
    copies = [pltpu.make_async_copy(src, dst, sems.at[n]) for n, (src, dst) in enumerate(pairs)]
    for copy in copies:
        copy.start()
    for copy in copies:
        copy.wait()
    rims = []
    for side, rim_ref in ((0, before_ref), (1, after_ref)):
        index = jnp.broadcast_to(list_ref[side : side + 1, :], (8, 128))
        rims.append((index & 127, index >> 7, rim_ref))

    def step(q, carry):
        d = pl.ds(pl.multiple_of(q * 8, 8), 8)
        for half in range(2):
            index = rows_ref[d, half * 128 : half * 128 + 128]
            low, high = index & 127, index >> 7
            for i in range(4):
                got = None
                for h in range(16):
                    block = jnp.broadcast_to(forcing_ref[i : i + 1, h * 128 : h * 128 + 128], (8, 128))
                    piece = lane_gather(block, low)
                    got = piece if h == 0 else jnp.where(high == h, piece, got)
                out_ref[d, 2 * i + half, :] = got
        pltpu.make_async_copy(out_ref.at[d], out_hbm.at[d], out_sems.at[q]).start()
        for low, high, rim_ref in rims:
            for g in range(3):
                rows = slice(8 * g, 8 * g + 8)
                got = None
                for h in range(16):
                    piece = lane_gather(spec_ref[q, rows, h * 128 : h * 128 + 128], low)
                    got = piece if h == 0 else jnp.where(high == h, piece, got)
                rim_ref[q, rows, :] = got
        for half in range(2):
            cols = pl.ds(pl.multiple_of(q * 256 + half * 128, 128), 128)
            put_parts(spec_ref, cols, x_ref, cols)
        return carry

    lax.fori_loop(0, TILES // 8, step, 0)
    for q in range(TILES // 8):
        d = pl.ds(q * 8, 8)
        pltpu.make_async_copy(out_ref.at[d], out_hbm.at[d], out_sems.at[q]).wait()


def weight_matrix(slot_ref, weight_ref, cols, width):
    slots = lax.broadcasted_iota(I32, (CAP, width), 0)
    total = None
    for j in range(4):
        index = slot_ref[j : j + 1, cols] & (CAP - 1)
        term = jnp.where(slots == index, weight_ref[j : j + 1, cols], 0.0)
        total = term if j == 0 else total + term
    return total, slot_ref[0:1, cols] >> 8


WB = 256


def wind_kernel(
    arrived_ref, slot_hbm, weight_hbm, spec_ref, wind_ref, mom_ref, left_ref, slot_ref, weight_ref, sems
):
    copies = [
        pltpu.make_async_copy(slot_hbm, slot_ref, sems.at[0]),
        pltpu.make_async_copy(weight_hbm, weight_ref, sems.at[1]),
    ]
    for copy in copies:
        copy.start()
    up, down_scale = group_scale()
    inv_c = [w / G_ACC * up for w in OMEGA]
    inv_omega = [1.0 / w * down_scale for w in OMEGA]
    inv_root = [math.sqrt(G_ACC) / w * down_scale for w in OMEGA]
    omega_c = [w * w / G_ACC * (up * up) for w in OMEGA]
    cos_tiles = [jnp.concatenate([t] * (WB // 128), axis=1) for t in direction_tiles(COS)]
    sin_tiles = [jnp.concatenate([t] * (WB // 128), axis=1) for t in direction_tiles(SIN)]
    for i in range(4):
        for half in range(2):
            p0, p1, p2 = parts3(arrived_ref[:, 2 * i + half, :])
            for n, part in enumerate((p0, p1, p2, p0, p1, p0)):
                left_ref[i * 64 : i * 64 + 64, n * 256 + half * 128 : n * 256 + half * 128 + 128] = part

    for copy in copies:
        copy.wait()

    def block(c, carry):
        cols = pl.ds(pl.multiple_of(c * WB, WB), WB)
        weights, band = weight_matrix(slot_ref, weight_ref, cols, WB)
        w0, w1, w2 = parts3(weights)
        right = jnp.concatenate([w0, w0, w0, w1, w1, w2], axis=0)
        mixed = jnp.dot(left_ref[...], right, preferred_element_type=F32)
        mine = lax.broadcasted_iota(I32, (TILES, WB), 0) == band
        east, north, density, gust = (
            jnp.sum(jnp.where(mine, mixed[i * 64 : i * 64 + 64], 0.0), axis=0, keepdims=True) for i in range(4)
        )
        speed = jnp.sqrt(east * east + north * north + 1.0)
        friction = jnp.sqrt(0.001 * (0.8 + 0.065 * speed)) * speed * (1.0 + 0.15 * gust)
        pull = 28.0 * friction
        share = 0.25 * (density / WATER_DENSITY)
        spread = lambda v: jnp.broadcast_to(v, (8, WB))
        east8, north8, speed8, pull8 = spread(east), spread(north), spread(speed), spread(pull)
        m0 = jnp.zeros((8, WB), F32)
        ms, mk, sx, sy = m0, m0, m0, m0
        for g in range(3):
            cos8, sin8 = cos_tiles[g], sin_tiles[g]
            push = pull8 * ((east8 * cos8 + north8 * sin8) / speed8)
            stress = jnp.zeros((8, WB), F32)
            for i in range(GS):
                spec = spec_ref[i, 8 * g : 8 * g + 8, cols]
                m0 = m0 + spec
                ms = ms + spec * inv_omega[i]
                mk = mk + spec * inv_root[i]
                excess = jnp.maximum(push * inv_c[i] - 1.0, 0.0)
                stress = stress + (excess * omega_c[i]) * spec
            sx = sx + stress * cos8
            sy = sy + stress * sin8
        down = lambda v: jnp.sum(v, axis=0, keepdims=True)
        for n, row in enumerate((down(m0), down(ms), down(mk), down(sx) * share, down(sy) * share)):
            for half in range(WB // 128):
                mom_ref[pl.ds(n * 16 + c * (WB // 128) + half, 1), :] = row[:, half * 128 : half * 128 + 128]
        for n, row in enumerate((east, north, density, speed, friction)):
            for half in range(WB // 128):
                wind_ref[pl.ds(n * 16 + c * (WB // 128) + half, 1), :] = row[:, half * 128 : half * 128 + 128]
        return carry

    lax.fori_loop(0, PTS // WB, block, 0)


def field_kernel(m0_ref, m1_ref, m2_ref, m3_ref, wind_ref, slot_ref, weight_ref, diss_ref, sums_ref, own_ref):
    moments = m0_ref[...] + m1_ref[...] + m2_ref[...] + m3_ref[...]
    total, inv_sigma, inv_root, stress_e, stress_n = (moments[16 * n : 16 * n + 16] for n in range(5))
    east, north, density, speed, friction = (wind_ref[16 * n : 16 * n + 16, :] for n in range(5))
    mean_sigma = total / inv_sigma
    mean_wavenum = jnp.square(total / inv_root)
    steepness = mean_wavenum * mean_wavenum * total * E_UNIT
    diss_ref[...] = DISSIP_COEF * mean_sigma * jnp.square(steepness / STEEP_PM) / mean_wavenum
    scale = WATER_DENSITY / density * G_ACC * E_UNIT
    friction_sq = friction * friction
    east_ratio = scale * stress_e / friction_sq
    north_ratio = scale * stress_n / friction_sq
    aligned = (east_ratio * east + north_ratio * north) / speed
    charnock = 1.0 / jnp.sqrt(1.0 - 0.9 * aligned / (1.0 + jnp.abs(aligned)))
    height = 4.0 * jnp.sqrt(E_UNIT * total)
    f = lax.axis_index("freq")
    own_ref[...] = jnp.where(f == 0, east_ratio, jnp.where(f == 1, north_ratio, jnp.where(f == 2, charnock, height)))

    def block(c, acc):
        cols = pl.ds(pl.multiple_of(c * WB, WB), WB)
        weights, band = weight_matrix(slot_ref, weight_ref, cols, WB)
        w0, w1 = parts2(weights)
        field = jnp.concatenate([own_ref[pl.ds(c * (WB // 128) + half, 1), :] for half in range(WB // 128)], axis=1)
        spread = jnp.where(lax.broadcasted_iota(I32, (TILES, WB), 0) == band, field, 0.0)
        f0, f1 = parts2(spread)
        left = jnp.concatenate([f0, f1, f0], axis=1)
        right = jnp.concatenate([w0, w0, w1], axis=1)
        return acc + lax.dot_general(left, right, (((1,), (1,)), ((), ())), preferred_element_type=F32)

    acc = lax.fori_loop(0, PTS // WB, block, jnp.zeros((TILES, CAP), F32))
    for half in range(2):
        sums_ref[:, half, :] = acc[:, half * 128 : half * 128 + 128]


def band_kernel(arrived_ref, rows_ref, out_ref):
    def eight_tiles(q, acc):
        ones, values = [], []
        for t in range(8):
            index = rows_ref[pl.ds(q * 8 + t, 1), :]
            tile = arrived_ref[q * 8 + t]
            row = jnp.concatenate([tile[0:1, :], tile[1:2, :]], axis=1)
            v0, v1 = parts2(row)
            high = lax.broadcasted_iota(I32, (16, CAP), 0) == (index >> 7)
            v0, v1 = v0.astype(F32), v1.astype(F32)
            values.append(jnp.concatenate([jnp.where(high, v0, 0.0), jnp.where(high, v1, 0.0)], axis=0).astype(BF))
            ones.append((lax.broadcasted_iota(I32, (128, CAP), 0) == (index & 127)).astype(F32).astype(BF))
        left = jnp.concatenate(ones, axis=1)
        right = jnp.concatenate(values, axis=1)
        return acc + lax.dot_general(left, right, (((1,), (1,)), ((), ())), preferred_element_type=F32)

    acc = lax.fori_loop(0, TILES // 8, eight_tiles, jnp.zeros((128, 32), F32))
    out_ref[...] = jnp.transpose(acc[:, :16] + acc[:, 16:])


def move_kernel(half, spec_hbm, x_hbm, low_hbm, high_hbm, near_hbm, *refs):
    if half == 0:
        out_hbm, rim_hbm, *refs = refs
    else:
        out_hbm, *refs = refs
    x_ref, spec_ref, rim_ref, near_ref, low_ref, high_ref, out_ref, sems = refs
    start = half * HALF
    here = pl.ds(start, HALF)
    copies = []

    def load(source, target):
        copies.append(pltpu.make_async_copy(source, target, sems.at[len(copies)]))
        copies[-1].start()
        return copies[-1]

    near_load = load(near_hbm.at[:, here], near_ref)
    if half == 0:
        rim_loads = [load(low_hbm, low_ref), load(high_hbm, high_ref)]
    else:
        rim_loads = [load(low_hbm, rim_ref)]
    piece = KCOPIES * 16 // 5
    x_loads = [load(x_hbm.at[pl.ds(n * piece, piece)], x_ref.at[pl.ds(n * piece, piece)]) for n in range(5)]
    spec_load = load(spec_hbm.at[:, :, here], spec_ref)
    for copy in rim_loads:
        copy.wait()
    if half == 0:
        put_parts(low_ref, slice(0, RIM), rim_ref, slice(0, RIM))
        put_parts(high_ref, slice(0, RIM), rim_ref, slice(RIM, 2 * RIM))
        load(rim_ref, rim_hbm)
    scale = group_scale()[1]
    courant = jnp.concatenate([by_sublane(COURANT) * scale] * (NB // 128), axis=1)
    near_load.wait()
    for copy in x_loads:
        copy.wait()
    spec_load.wait()

    def hot(rows, index):
        match = lax.broadcasted_iota(jnp.int16, (rows, NB), 0) == index
        return jnp.where(match, jnp.ones((), BF), jnp.zeros((), BF))

    def block(c, carry):
        outs = pl.ds(pl.multiple_of(c * NB, NB), NB)
        got = []
        for n, first in enumerate((0, 12, 6, 18)):
            index = near_ref[n : n + 1, outs]
            rim_index = jnp.where(index < RIM, index, jnp.where(index < RIM + PTS, 2 * RIM, index - PTS))
            rows = slice(first * 16, first * 16 + 192)
            own = jnp.dot(x_ref[rows, :], hot(PTS, (index - RIM).astype(jnp.int16)), preferred_element_type=F32)
            rim = jnp.dot(rim_ref[rows, :], hot(2 * RIM, rim_index.astype(jnp.int16)), preferred_element_type=F32)
            got.append(own + rim)
        for k in range(ND):
            a = (k + ROLL) % ND
            x_of = got[0] if a < 12 else got[1]
            a = a % 12
            y_of = got[2] if k < 12 else got[3]
            b = k % 12
            from_x = x_of[a * 16 : a * 16 + 8] + x_of[a * 16 + 8 : a * 16 + 16]
            from_y = y_of[b * 16 : b * 16 + 8] + y_of[b * 16 + 8 : b * 16 + 16]
            spec = spec_ref[:, k, outs]
            out_ref[:, k, outs] = (
                spec - (courant * abs(COS[k])) * (spec - from_x) - (courant * abs(SIN[k])) * (spec - from_y)
            )
        pltpu.make_async_copy(out_ref.at[:, :, outs], out_hbm.at[:, :, outs], sems.at[MOVE_SEMS + c]).start()
        return carry

    lax.fori_loop(0, HALF // NB, block, 0)
    for c in range(HALF // NB):
        outs = pl.ds(c * NB, NB)
        pltpu.make_async_copy(out_ref.at[:, :, outs], out_hbm.at[:, :, outs], sems.at[MOVE_SEMS + c]).wait()
    if half == 0:
        copies[-1].wait()


def source_kernel(moved0_hbm, moved1_hbm, wind_ref, diss_ref, out_hbm, moved_ref, push_ref, new_ref, loads, stores):
    copies = []
    for i in range(GS):
        for half, moved_hbm in ((0, moved0_hbm), (1, moved1_hbm)):
            target = moved_ref.at[i, :, half * HALF : half * HALF + HALF]
            copies.append(pltpu.make_async_copy(moved_hbm.at[i], target, loads.at[2 * i + half]))
    for copy in copies:
        copy.start()
    up = group_scale()[0]
    cos_tiles, sin_tiles = direction_tiles(COS), direction_tiles(SIN)

    def spread(c):
        row = lambda n: jnp.broadcast_to(wind_ref[pl.ds(n * 16 + c, 1), :], (8, 128))
        return [row(n) for n in range(5)]

    def prepare(c, carry):
        east, north, density, speed, friction = spread(c)
        pull = 28.0 * friction / speed
        for g in range(3):
            push_ref[c, 8 * g : 8 * g + 8, :] = pull * (east * cos_tiles[g] + north * sin_tiles[g])
        push_ref[c, 24:32, :] = (0.25 * DT_SRC) * (density / WATER_DENSITY)
        push_ref[c, 32:40, :] = DT_SRC * jnp.broadcast_to(diss_ref[pl.ds(c, 1), :], (8, 128))
        return carry

    lax.fori_loop(0, PTS // 128, prepare, 0)
    for i in range(GS):
        inv_c, omega, wavenum = OMEGA[i] / G_ACC * up, OMEGA[i] * up, OMEGA[i] ** 2 / G_ACC * (up * up)
        copies[2 * i].wait()
        copies[2 * i + 1].wait()

        def block(c, carry):
            cols = pl.ds(pl.multiple_of(c * 128, 128), 128)
            share, loss = push_ref[c, 24:32, :] * omega, push_ref[c, 32:40, :] * wavenum
            for g in range(3):
                rows = slice(8 * g, 8 * g + 8)
                excess = jnp.maximum(push_ref[c, rows, :] * inv_c - 1.0, 0.0)
                new_ref[i, rows, cols] = moved_ref[i, rows, cols] * jnp.exp(share * excess - loss)
            return carry

        lax.fori_loop(0, PTS // 128, block, 0, unroll=4)
        pltpu.make_async_copy(new_ref.at[i], out_hbm.at[i], stores.at[i]).start()
    for i in range(GS):
        pltpu.make_async_copy(new_ref.at[i], out_hbm.at[i], stores.at[i]).wait()


VMEM = pl.BlockSpec(memory_space=pltpu.VMEM)
HBM = pl.BlockSpec(memory_space=pltpu.HBM)


def array(*dims, dtype=F32):
    return jax.ShapeDtypeStruct(dims, dtype)


def call(body, name, out, specs, scratch=(), mib=64, microseconds=1.0, out_specs=None, behind=False, mark=False):
    out = list(out)
    out_specs = [VMEM] * len(out) if out_specs is None else list(out_specs)
    specs = [*specs, VMEM] if behind else specs
    inputs = len(specs) - behind
    outputs = len(out)
    if mark:
        out.append(array(8, 128))
        out_specs.append(VMEM)

    def kernel(*refs):
        results = inputs + behind
        if mark:
            refs[results + outputs][...] = jnp.zeros((8, 128), F32)
        body(*refs[:inputs], *refs[results : results + outputs], *refs[results + outputs + mark :])

    cost = pl.CostEstimate(flops=0, bytes_accessed=int(microseconds * 3.0e6), transcendentals=0)
    return pl.pallas_call(
        kernel,
        out_shape=out,
        in_specs=specs,
        out_specs=out_specs,
        scratch_shapes=list(scratch),
        name=name,
        cost_estimate=cost,
        compiler_params=pltpu.CompilerParams(vmem_limit_bytes=mib * 2**20),
    )


def on_device(spectrum, forcing, send_rows, point_slot, remap_weight, neighbours, halo_send):
    dma = pltpu.SemaphoreType.DMA
    outgoing, to_before, to_after, operand, mark = call(
        first_kernel,
        "first",
        [array(TILES, 8, 128), array(GS, ND, RIM), array(GS, ND, RIM), array(KCOPIES * 16, PTS, dtype=BF)],
        [HBM] * 4,
        [
            pltpu.VMEM((4, PTS), F32),
            pltpu.VMEM((TILES, CAP), I32),
            pltpu.VMEM((2, RIM), I32),
            pltpu.VMEM((GS, ND, PTS), F32),
            pltpu.VMEM((TILES, 8, 128), F32),
            dma((4,)),
            dma((TILES // 8,)),
        ],
        microseconds=5.0,
        out_specs=[HBM, VMEM, VMEM, VMEM],
        mark=True,
    )(forcing, send_rows, halo_send.reshape(2, RIM), spectrum)
    arrived = lax.all_to_all(outgoing, "tile", split_axis=0, concat_axis=0, tiled=True)

    up = [(d, d + 1) for d in range(TILES - 1)]
    low_rim = lax.ppermute(to_after, "tile", up)
    high_rim = lax.ppermute(to_before, "tile", [(b, a) for a, b in up])

    blocks = HALF // NB
    scratch = [
        pltpu.VMEM((KCOPIES * 16, PTS), BF),
        pltpu.VMEM((GS, ND, HALF), F32),
        pltpu.VMEM((KCOPIES * 16, 2 * RIM), BF),
        pltpu.VMEM((4, HALF), I32),
        pltpu.VMEM((GS, ND, RIM), F32),
        pltpu.VMEM((GS, ND, RIM), F32),
        pltpu.VMEM((GS, ND, HALF), F32),
        dma((MOVE_SEMS + blocks,)),
    ]
    moved0, rims, mark = call(
        functools.partial(move_kernel, 0),
        "move0",
        [array(GS, ND, HALF), array(KCOPIES * 16, 2 * RIM, dtype=BF)],
        [HBM] * 5,
        scratch,
        microseconds=5.5,
        out_specs=[HBM, HBM],
        behind=True,
        mark=True,
    )(spectrum, operand, low_rim, high_rim, neighbours, mark)
    wind, moments, mark = call(
        wind_kernel,
        "wind",
        [array(80, 128), array(80, 128)],
        [VMEM, HBM, HBM, VMEM],
        [
            pltpu.VMEM((256, 6 * 256), BF),
            pltpu.VMEM((4, PTS), I32),
            pltpu.VMEM((4, PTS), F32),
            dma((2,)),
        ],
        microseconds=6.0,
        behind=True,
        mark=True,
    )(arrived, point_slot, remap_weight, spectrum, mark)
    others = [lax.ppermute(moments, "freq", [(i, (i + n) % 4) for i in range(4)]) for n in (1, 2, 3)]
    moved1, mark = call(
        lambda spec, x, rim, near, *refs: move_kernel(1, spec, x, rim, None, near, *refs),
        "move1",
        [array(GS, ND, HALF)],
        [HBM] * 4,
        scratch,
        microseconds=5.0,
        out_specs=[HBM],
        behind=True,
        mark=True,
    )(spectrum, operand, rims, neighbours, mark)

    diss, slot_sums = call(
        field_kernel,
        "fields",
        [array(16, 128), array(TILES, 2, 128)],
        [VMEM] * 7,
        [pltpu.VMEM((16, 128), F32)],
        microseconds=3.0,
        behind=True,
    )(moments, *others, wind, point_slot, remap_weight, mark)
    arrived_sums = lax.all_to_all(slot_sums, "tile", split_axis=0, concat_axis=0, tiled=True)

    new_spectrum, mark = call(
        source_kernel,
        "source",
        [array(GS, ND, PTS)],
        [HBM, HBM, VMEM, VMEM],
        [
            pltpu.VMEM((GS, ND, PTS), F32),
            pltpu.VMEM((PTS // 128, 40, 128), F32),
            pltpu.VMEM((GS, ND, PTS), F32),
            dma((2 * GS,)),
            dma((GS,)),
        ],
        microseconds=3.0,
        out_specs=[HBM],
        mark=True,
    )(moved0, moved1, wind, diss)

    (returned,) = call(band_kernel, "band", [array(16, 128)], [VMEM] * 2, microseconds=2.5, behind=True)(
        arrived_sums, send_rows, mark
    )
    return (new_spectrum, returned.reshape(1, PTS))


def solution(mesh):
    placed = (
        P("freq", None, "tile"),
        P(None, "tile"),
        P("tile", None),
        P(None, "tile"),
        P(None, "tile"),
        P(None, "tile"),
        P("tile"),
    )
    return jax.shard_map(
        on_device,
        mesh=mesh,
        in_specs=placed,
        out_specs=(P("freq", None, "tile"), P("freq", "tile")),
        check_vma=False,
    )
```

time: 86.3 us -> 88.1 us (1.021)
  local copies, waits for them, and re-layouts: 12.2 us -> 0 us
  Pallas kernels: 34.6 us -> 43.5 us
  waiting for transfers between devices: 4.39 us -> 10.2 us
    unnamed x42 -> x0, local copies, waits for them, and re-layouts: 12.2 us -> none
    pallas_call x9 -> x7, Pallas kernels: 34.6 us -> 43.5 us  [the longest x1 8.18 us: on_device(): call(lambda spec, x, rim, near, *refs: move_kernel(1, spec, x, rim, None,...]
    all_to_all x1, waiting for transfers between devices: 2.72 us -> 5.61 us  [on_device(): lax.all_to_all(slot_sums, 'tile', split_axis=0, concat_axis=0, tiled=True)]
    ppermute x1, waiting for transfers between devices: 1.66 us -> 3.91 us  [on_device(): high_rim = lax.ppermute(to_before, 'tile', [(b, a) for a, b in up])]
  transfers between devices with their start and end apart: 7 -> 7, of which waited for: 2 -> 3; matrix products, arithmetic and copies ran while one was open for 0% -> 0% of each run, Pallas kernels for 23% -> 23%
where the time goes in v3:
time: 88.1 us; the launch traced here: 87.5 us
  Pallas kernels  43.5 us (49%)
  starting transfers between devices  33 us (37%)
  waiting for transfers between devices  10.2 us (12%)
    all_to_all x1, starting transfers between devices, on_device(): lax.all_to_all(outgoing, 'tile', split_axis=0, concat_axis=0, tiled=True)  13.4 us
    all_to_all x1, starting transfers between devices, on_device(): lax.all_to_all(slot_sums, 'tile', split_axis=0, concat_axis=0, tiled=True)  10.6 us
    pallas_call x1, Pallas kernels, on_device(): call(lambda spec, x, rim, near, *refs: move_kernel(1, spec, x, rim, None,...  8.18 us
    pallas_call x1, Pallas kernels, on_device(): call(functools.partial(move_kernel, 0), 'move0', [array(GS, ND, HALF), ar...  8.17 us
    pallas_call x1, Pallas kernels, on_device(): call(wind_kernel, 'wind', [array(80, 128), array(80, 128)], [VMEM, HBM, H...  7.57 us
    pallas_call x1, Pallas kernels, on_device(): call(first_kernel, 'first', [array(TILES, 8, 128), array(GS, ND, RIM), ar...  7.56 us
    all_to_all x1, waiting for transfers between devices, on_device(): lax.all_to_all(slot_sums, 'tile', split_axis=0, concat_axis=0, tiled=True)  5.61 us
    pallas_call x1, Pallas kernels, on_device(): call(source_kernel, 'source', [array(GS, ND, PTS)], [HBM, HBM, VMEM, VMEM...  4.06 us
  transfers between devices with their start and end apart: 7, of which 3 were waited for; matrix products, arithmetic and copies ran while one was open for 0% of the time, Pallas kernels for 23%

profile of v3, /device:TPU:1, one launch (start us, length us, event | category | flops | bytes accessed | tf_op | source)
XLA Modules:
  0.0 87.5 jit_solution(10609221172075831386)
XLA Ops:
  0.6 7.6 %first.1 = (f32[64,8,128]{2,1,0:T(8,128)}, f32[8,24,128]{2,1,0:T(8,128)}, f32[8,24,128]{2,1,0:T(8,128)}, bf16[480,2048]{1,0:T(8,128)(2,1)}, f32[8,128]{1,0:T(8,128)}) custom-call(f32[4,2048]{1,0:T(4,128)} %refs_0_.3, s32[64,256]{1,0:T(8,128)} %refs_1_.5, s32[2,128]{1,0:T(2,128)} %bitcast.3, f32[8,24,2048]{2,1,0:T(8,128)} %refs_0_.5), custom_call_target="tpu_custom_call" | custom-call | bytes 15000000 | tf_op jit(solution)/shard_map/first/pallas_call | solution.py:430
  8.2 13.4 %all-to-all-start = ((f32[64,8,128]{2,1,0:T(8,128)}), f32[64,8,128]{2,1,0:T(8,128)}, u32[]{:S(2)}, u32[]{:S(2)}) async-start(f32[64,8,128]{2,1,0:T(8,128)} %get-tuple-element.25), calls=%async_computation | async-start | bytes 524288 | tf_op jit(solution)/shard_map/all_to_all | solution.py:448
  21.6 3.5 %collective-permute-start = (f32[8,24,128]{2,1,0:T(8,128)}, f32[8,24,128]{2,1,0:T(8,128)}, u32[]{:S(2)}, u32[]{:S(2)}) collective-permute-start(f32[8,24,128]{2,1,0:T(8,128)} %get-tuple-element.20), channel_id=1, source_target_pairs={{0,4},{4,8},{8,12},{12,16},{16,20},{20,24},{24,28},{28,32},{32,36}... | collective-permute-start | bytes 294920 | tf_op jit(solution)/shard_map/ppermute | solution.py:451
  25.1 1.9 %collective-permute-start.1 = (f32[8,24,128]{2,1,0:T(8,128)}, f32[8,24,128]{2,1,0:T(8,128)}, u32[]{:S(2)}, u32[]{:S(2)}) collective-permute-start(f32[8,24,128]{2,1,0:T(8,128)} %get-tuple-element.21), channel_id=1, source_target_pairs={{4,0},{8,4},{12,8},{16,12},{20,16},{24,20},{28,24},{32,28},{36,32}... | collective-permute-start | bytes 294920 | tf_op jit(solution)/shard_map/ppermute | solution.py:452
  27.0 0.7 collective-permute-done.refs_2_
  27.7 3.9 %collective-permute-done.1.refs_3_ = f32[8,24,128]{2,1,0:T(8,128)} collective-permute-done((f32[8,24,128]{2,1,0:T(8,128)}, f32[8,24,128]{2,1,0:T(8,128)}, u32[]{:S(2)}, u32[]{:S(2)}) %collective-permute-start.1) | collective-permute-done | bytes 98336 | tf_op jit(solution)/shard_map/ppermute | solution.py:452
  31.7 8.2 %move0.1 = (f32[8,24,1024]{2,1,0:T(8,128)}, bf16[480,256]{1,0:T(8,128)(2,1)}, f32[8,128]{1,0:T(8,128)}) custom-call(f32[8,24,2048]{2,1,0:T(8,128)} %refs_0_.5, bf16[480,2048]{1,0:T(8,128)(2,1)} %get-tuple-element.19.refs_1_, f32[8,24,128]{2,1,0:T(8,128)} %collective-permute-done.refs_2_, f32[8,24,128]{2,1,0:T(8,128)} %collective-permute-done.1.refs_3_, ...), custom_call_target="tpu_custom_call" | custom-call | bytes 16500000 | tf_op jit(solution)/shard_map/move0/pallas_call | solution.py:465
  39.8 0.0 all-to-all-done.refs_0_
  39.8 7.6 %wind.1 = (f32[80,128]{1,0:T(8,128)}, f32[80,128]{1,0:T(8,128)}, f32[8,128]{1,0:T(8,128)}) custom-call(f32[64,8,128]{2,1,0:T(8,128)} %all-to-all-done.refs_0_, s32[4,2048]{1,0:T(4,128)} %refs_5_.1, f32[4,2048]{1,0:T(4,128)} %refs_6_.1, f32[8,24,2048]{2,1,0:T(8,128)} %refs_0_.5, f32[8,128]{1,0:T(8,128)} %get-tuple-element.26.refs_4_), custom_call_target="tpu_custom_call" | custom-call | bytes 18000000 | tf_op jit(solution)/shard_map/wind/pallas_call | solution.py:476
  47.4 2.6 %collective-permute-start.4 = (f32[80,128]{1,0:T(8,128)}, f32[80,128]{1,0:T(8,128)}, u32[]{:S(2)}, u32[]{:S(2)}) collective-permute-start(f32[80,128]{1,0:T(8,128)} %get-tuple-element.30.refs_0_), channel_id=1, source_target_pairs={{0,3},{1,0},{2,1},{3,2},{4,7},{5,4},{6,5},{7,6},{8,11},{9,8},{10,9... | collective-permute-start | bytes 122888 | tf_op jit(solution)/shard_map/ppermute | solution.py:491
  50.0 0.5 collective-permute-start.3
  50.5 0.6 collective-permute-start.2
  51.1 8.2 %move1.1 = (f32[8,24,1024]{2,1,0:T(8,128)}, f32[8,128]{1,0:T(8,128)}) custom-call(f32[8,24,2048]{2,1,0:T(8,128)} %refs_0_.5, bf16[480,2048]{1,0:T(8,128)(2,1)} %get-tuple-element.19.refs_1_, bf16[480,256]{1,0:T(8,128)(2,1)} %get-tuple-element.24.refs_2_, s32[4,2048]{1,0:T(4,128)} %refs_3_.5, f32[8,128]{1,0:T(8,128)} %get-tuple-element.27.refs_4_), custom_call_target="tpu_custom_call" | custom-call | bytes 15000000 | tf_op jit(solution)/shard_map/move1/pallas_call | solution.py:492
  59.3 0.0 collective-permute-done.4.refs_3_
  59.3 0.0 collective-permute-done.3.refs_2_
  59.3 0.0 collective-permute-done.2.refs_1_
  59.3 4.1 %fields.1 = (f32[16,128]{1,0:T(8,128)}, f32[64,2,128]{2,1,0:T(2,128)}) custom-call(f32[80,128]{1,0:T(8,128)} %get-tuple-element.30.refs_0_, f32[80,128]{1,0:T(8,128)} %collective-permute-done.2.refs_1_, f32[80,128]{1,0:T(8,128)} %collective-permute-done.3.refs_2_, f32[80,128]{1,0:T(8,128)} %collective-permute-done.4.refs_3_, ...), custom_call_target="tpu_custom_call" | custom-call | bytes 9000000 | tf_op jit(solution)/shard_map/fields/pallas_call | solution.py:504
  63.4 10.6 %all-to-all-start.1 = ((f32[64,2,128]{2,1,0:T(2,128)}), f32[64,2,128]{2,1,0:T(2,128)}, u32[]{:S(2)}, u32[]{:S(2)}) async-start(f32[64,2,128]{2,1,0:T(2,128)} %get-tuple-element.34), calls=%async_computation.1 | async-start | bytes 131072 | tf_op jit(solution)/shard_map/all_to_all | solution.py:513
  73.9 4.1 %source.1 = (f32[8,24,2048]{2,1,0:T(8,128)}, f32[8,128]{1,0:T(8,128)}) custom-call(f32[8,24,1024]{2,1,0:T(8,128)} %get-tuple-element.23.refs_0_, f32[8,24,1024]{2,1,0:T(8,128)} %get-tuple-element.28.refs_1_, f32[80,128]{1,0:T(8,128)} %get-tuple-element.29.refs_4_.refs_2_, f32[16,128]{1,0:T(8,128)} %get-tuple-element.32.refs_3_), custom_call_target="tpu_custom_call" | custom-call | bytes 9000000 | tf_op jit(solution)/shard_map/source/pallas_call | solution.py:515
  78.0 5.6 %all-to-all-done.1.refs_0_ = f32[64,2,128]{2,1,0:T(2,128)} async-done(((f32[64,2,128]{2,1,0:T(2,128)}), f32[64,2,128]{2,1,0:T(2,128)}, u32[]{:S(2)}, u32[]{:S(2)}) %all-to-all-start.1) | async-done | bytes 65568 | tf_op jit(solution)/shard_map/all_to_all | solution.py:513
  83.6 3.9 %band.1 = f32[16,128]{1,0:T(8,128)} custom-call(f32[64,2,128]{2,1,0:T(2,128)} %all-to-all-done.1.refs_0_, s32[64,256]{1,0:T(8,128)} %refs_1_.5, f32[8,128]{1,0:T(8,128)} %get-tuple-element.35.refs_2_), custom_call_target="tpu_custom_call" | custom-call | bytes 7500000 | tf_op jit(solution)/shard_map/band/pallas_call | solution.py:532
Async XLA Ops:
  8.2 31.6 %all-to-all-start = ((f32[64,8,128]{2,1,0:T(8,128)}), f32[64,8,128]{2,1,0:T(8,128)}, u32[]{:S(2)}, u32[]{:S(2)}) async-start(f32[64,8,128]{2,1,0:T(8,128)} %get-tuple-element.25), calls=%async_computation | async-start | bytes 524288 | tf_op jit(solution)/shard_map/all_to_all | solution.py:448
  21.6 6.2 %collective-permute-start = (f32[8,24,128]{2,1,0:T(8,128)}, f32[8,24,128]{2,1,0:T(8,128)}, u32[]{:S(2)}, u32[]{:S(2)}) collective-permute-start(f32[8,24,128]{2,1,0:T(8,128)} %get-tuple-element.20), channel_id=1, source_target_pairs={{0,4},{4,8},{8,12},{12,16},{16,20},{20,24},{24,28},{28,32},{32,36}... | collective-permute-start | bytes 294920 | tf_op jit(solution)/shard_map/ppermute | solution.py:451
  25.1 6.5 %collective-permute-start.1 = (f32[8,24,128]{2,1,0:T(8,128)}, f32[8,24,128]{2,1,0:T(8,128)}, u32[]{:S(2)}, u32[]{:S(2)}) collective-permute-start(f32[8,24,128]{2,1,0:T(8,128)} %get-tuple-element.21), channel_id=1, source_target_pairs={{4,0},{8,4},{12,8},{16,12},{20,16},{24,20},{28,24},{32,28},{36,32}... | collective-permute-start | bytes 294920 | tf_op jit(solution)/shard_map/ppermute | solution.py:452
  47.4 11.8 %collective-permute-start.4 = (f32[80,128]{1,0:T(8,128)}, f32[80,128]{1,0:T(8,128)}, u32[]{:S(2)}, u32[]{:S(2)}) collective-permute-start(f32[80,128]{1,0:T(8,128)} %get-tuple-element.30.refs_0_), channel_id=1, source_target_pairs={{0,3},{1,0},{2,1},{3,2},{4,7},{5,4},{6,5},{7,6},{8,11},{9,8},{10,9... | collective-permute-start | bytes 122888 | tf_op jit(solution)/shard_map/ppermute | solution.py:491
  50.0 9.3 %collective-permute-start.3 = (f32[80,128]{1,0:T(8,128)}, f32[80,128]{1,0:T(8,128)}, u32[]{:S(2)}, u32[]{:S(2)}) collective-permute-start(f32[80,128]{1,0:T(8,128)} %get-tuple-element.30.refs_0_), channel_id=1, source_target_pairs={{0,2},{1,3},{2,0},{3,1},{4,6},{5,7},{6,4},{7,5},{8,10},{9,11},{10,... | collective-permute-start | bytes 122888 | tf_op jit(solution)/shard_map/ppermute | solution.py:491
  50.5 8.8 %collective-permute-start.2 = (f32[80,128]{1,0:T(8,128)}, f32[80,128]{1,0:T(8,128)}, u32[]{:S(2)}, u32[]{:S(2)}) collective-permute-start(f32[80,128]{1,0:T(8,128)} %get-tuple-element.30.refs_0_), channel_id=1, source_target_pairs={{0,1},{1,2},{2,3},{3,0},{4,5},{5,6},{6,7},{7,4},{8,9},{9,10},{10,1... | collective-permute-start | bytes 122888 | tf_op jit(solution)/shard_map/ppermute | solution.py:491
  63.4 20.2 %all-to-all-start.1 = ((f32[64,2,128]{2,1,0:T(2,128)}), f32[64,2,128]{2,1,0:T(2,128)}, u32[]{:S(2)}, u32[]{:S(2)}) async-start(f32[64,2,128]{2,1,0:T(2,128)} %get-tuple-element.34), calls=%async_computation.1 | async-start | bytes 131072 | tf_op jit(solution)/shard_map/all_to_all | solution.py:513

commit v4 on v3

--- a/solution.py
+++ b/solution.py
@@ -78,7 +78,6 @@
 KCOPIES = 30
 NB = 512
 HALF = PTS // 2
-MOVE_SEMS = 10
 
 
 def put_parts(ref, source, x_ref, target):
@@ -88,16 +87,36 @@
         x_ref[kp * 16 : kp * 16 + 16, target] = jnp.concatenate([p0, v - p0], axis=0).astype(BF)
 
 
-def first_kernel(
-    forcing_hbm, rows_hbm, list_hbm, spec_hbm, out_hbm, before_ref, after_ref, x_ref,
-    forcing_ref, rows_ref, list_ref, spec_ref, out_ref, sems, out_sems,
-):
-    pairs = ((rows_hbm, rows_ref), (forcing_hbm, forcing_ref), (list_hbm, list_ref), (spec_hbm, spec_ref))
-    copies = [pltpu.make_async_copy(src, dst, sems.at[n]) for n, (src, dst) in enumerate(pairs)]
+def start_copies(pairs, sems, first=0):
+    copies = [pltpu.make_async_copy(src, dst, sems.at[first + n]) for n, (src, dst) in enumerate(pairs)]
     for copy in copies:
         copy.start()
+    return copies
+
+
+def wait_copies(copies):
     for copy in copies:
         copy.wait()
+
+
+def start_copies(pairs, sems, first=0):
+    copies = [pltpu.make_async_copy(src, dst, sems.at[first + n]) for n, (src, dst) in enumerate(pairs)]
+    for copy in copies:
+        copy.start()
+    return copies
+
+
+def wait_copies(copies):
+    for copy in copies:
+        copy.wait()
+
+
+def first_kernel(
+    rows_hbm, forcing_hbm, list_hbm, spec_hbm, out_hbm, before_hbm, after_hbm, x_ref, spec_ref,
+    rows_ref, forcing_ref, list_ref, out_ref, before_ref, after_ref, sems, out_sems,
+):
+    sources = ((rows_hbm, rows_ref), (forcing_hbm, forcing_ref), (list_hbm, list_ref), (spec_hbm, spec_ref))
+    wait_copies(start_copies(sources, sems))
     rims = []
     for side, rim_ref in ((0, before_ref), (1, after_ref)):
         index = jnp.broadcast_to(list_ref[side : side + 1, :], (8, 128))
@@ -130,9 +149,11 @@
         return carry
 
     lax.fori_loop(0, TILES // 8, step, 0)
+    stores = start_copies(((before_ref, before_hbm), (after_ref, after_hbm)), sems)
     for q in range(TILES // 8):
         d = pl.ds(q * 8, 8)
         pltpu.make_async_copy(out_ref.at[d], out_hbm.at[d], out_sems.at[q]).wait()
+    wait_copies(stores)
 
 
 def weight_matrix(slot_ref, weight_ref, cols, width):
@@ -149,14 +170,9 @@
 
 
 def wind_kernel(
-    arrived_ref, slot_hbm, weight_hbm, spec_ref, wind_ref, mom_ref, left_ref, slot_ref, weight_ref, sems
+    arrived_hbm, slot_hbm, weight_hbm, spec_ref, wind_ref, mom_ref, left_ref, arrived_ref, slot_ref, weight_ref, sems
 ):
-    copies = [
-        pltpu.make_async_copy(slot_hbm, slot_ref, sems.at[0]),
-        pltpu.make_async_copy(weight_hbm, weight_ref, sems.at[1]),
-    ]
-    for copy in copies:
-        copy.start()
+    copies = start_copies(((arrived_hbm, arrived_ref), (slot_hbm, slot_ref), (weight_hbm, weight_ref)), sems)
     up, down_scale = group_scale()
     inv_c = [w / G_ACC * up for w in OMEGA]
     inv_omega = [1.0 / w * down_scale for w in OMEGA]
@@ -164,14 +180,12 @@
     omega_c = [w * w / G_ACC * (up * up) for w in OMEGA]
     cos_tiles = [jnp.concatenate([t] * (WB // 128), axis=1) for t in direction_tiles(COS)]
     sin_tiles = [jnp.concatenate([t] * (WB // 128), axis=1) for t in direction_tiles(SIN)]
+    wait_copies(copies)
     for i in range(4):
         for half in range(2):
             p0, p1, p2 = parts3(arrived_ref[:, 2 * i + half, :])
             for n, part in enumerate((p0, p1, p2, p0, p1, p0)):
                 left_ref[i * 64 : i * 64 + 64, n * 256 + half * 128 : n * 256 + half * 128 + 128] = part
-
-    for copy in copies:
-        copy.wait()
 
     def block(c, carry):
         cols = pl.ds(pl.multiple_of(c * WB, WB), WB)
@@ -216,14 +230,18 @@
     lax.fori_loop(0, PTS // WB, block, 0)
 
 
-def field_kernel(m0_ref, m1_ref, m2_ref, m3_ref, wind_ref, slot_ref, weight_ref, diss_ref, sums_ref, own_ref):
+def field_kernel(
+    m0_ref, m1_ref, m2_ref, m3_ref, wind_ref, slot_hbm, weight_hbm, diss_ref, sums_ref, own_ref, slot_ref, weight_ref, sems
+):
+    copies = start_copies(((slot_hbm, slot_ref), (weight_hbm, weight_ref)), sems)
     moments = m0_ref[...] + m1_ref[...] + m2_ref[...] + m3_ref[...]
     total, inv_sigma, inv_root, stress_e, stress_n = (moments[16 * n : 16 * n + 16] for n in range(5))
     east, north, density, speed, friction = (wind_ref[16 * n : 16 * n + 16, :] for n in range(5))
     mean_sigma = total / inv_sigma
     mean_wavenum = jnp.square(total / inv_root)
     steepness = mean_wavenum * mean_wavenum * total * E_UNIT
-    diss_ref[...] = DISSIP_COEF * mean_sigma * jnp.square(steepness / STEEP_PM) / mean_wavenum
+    diss_ref[80:96, :] = DISSIP_COEF * mean_sigma * jnp.square(steepness / STEEP_PM) / mean_wavenum
+    diss_ref[0:80, :] = wind_ref[...]
     scale = WATER_DENSITY / density * G_ACC * E_UNIT
     friction_sq = friction * friction
     east_ratio = scale * stress_e / friction_sq
@@ -233,6 +251,8 @@
     height = 4.0 * jnp.sqrt(E_UNIT * total)
     f = lax.axis_index("freq")
     own_ref[...] = jnp.where(f == 0, east_ratio, jnp.where(f == 1, north_ratio, jnp.where(f == 2, charnock, height)))
+
+    wait_copies(copies)
 
     def block(c, acc):
         cols = pl.ds(pl.multiple_of(c * WB, WB), WB)
@@ -250,7 +270,9 @@
         sums_ref[:, half, :] = acc[:, half * 128 : half * 128 + 128]
 
 
-def band_kernel(arrived_ref, rows_ref, out_ref):
+def band_kernel(arrived_ref, rows_hbm, out_ref, rows_ref, sems):
+    wait_copies(start_copies(((rows_hbm, rows_ref),), sems))
+
     def eight_tiles(q, acc):
         ones, values = [], []
         for t in range(8):
@@ -270,41 +292,21 @@
     out_ref[...] = jnp.transpose(acc[:, :16] + acc[:, 16:])
 
 
-def move_kernel(half, spec_hbm, x_hbm, low_hbm, high_hbm, near_hbm, *refs):
+def move_kernel(half, spec_ref, x_ref, low_ref, high_ref, near_hbm, *refs):
+    start = half * HALF
     if half == 0:
-        out_hbm, rim_hbm, *refs = refs
-    else:
-        out_hbm, *refs = refs
-    x_ref, spec_ref, rim_ref, near_ref, low_ref, high_ref, out_ref, sems = refs
-    start = half * HALF
-    here = pl.ds(start, HALF)
-    copies = []
-
-    def load(source, target):
-        copies.append(pltpu.make_async_copy(source, target, sems.at[len(copies)]))
-        copies[-1].start()
-        return copies[-1]
-
-    near_load = load(near_hbm.at[:, here], near_ref)
-    if half == 0:
-        rim_loads = [load(low_hbm, low_ref), load(high_hbm, high_ref)]
-    else:
-        rim_loads = [load(low_hbm, rim_ref)]
-    piece = KCOPIES * 16 // 5
-    x_loads = [load(x_hbm.at[pl.ds(n * piece, piece)], x_ref.at[pl.ds(n * piece, piece)]) for n in range(5)]
-    spec_load = load(spec_hbm.at[:, :, here], spec_ref)
-    for copy in rim_loads:
-        copy.wait()
-    if half == 0:
+        out_hbm, rim_hbm, near_ref, rim_ref, out_ref, sems = refs
+        copies = start_copies(((near_hbm, near_ref),), sems)
         put_parts(low_ref, slice(0, RIM), rim_ref, slice(0, RIM))
         put_parts(high_ref, slice(0, RIM), rim_ref, slice(RIM, 2 * RIM))
-        load(rim_ref, rim_hbm)
+        stores = start_copies(((rim_ref, rim_hbm),), sems, 1)
+    else:
+        out_hbm, near_ref, rim_ref, out_ref, sems = refs
+        copies = start_copies(((near_hbm, near_ref), (low_ref, rim_ref)), sems)
+        stores = []
+    wait_copies(copies)
     scale = group_scale()[1]
     courant = jnp.concatenate([by_sublane(COURANT) * scale] * (NB // 128), axis=1)
-    near_load.wait()
-    for copy in x_loads:
-        copy.wait()
-    spec_load.wait()
 
     def hot(rows, index):
         match = lax.broadcasted_iota(jnp.int16, (rows, NB), 0) == index
@@ -312,9 +314,10 @@
 
     def block(c, carry):
         outs = pl.ds(pl.multiple_of(c * NB, NB), NB)
+        cols = pl.ds(pl.multiple_of(start + c * NB, NB), NB)
         got = []
         for n, first in enumerate((0, 12, 6, 18)):
-            index = near_ref[n : n + 1, outs]
+            index = near_ref[n : n + 1, cols]
             rim_index = jnp.where(index < RIM, index, jnp.where(index < RIM + PTS, 2 * RIM, index - PTS))
             rows = slice(first * 16, first * 16 + 192)
             own = jnp.dot(x_ref[rows, :], hot(PTS, (index - RIM).astype(jnp.int16)), preferred_element_type=F32)
@@ -328,29 +331,25 @@
             b = k % 12
             from_x = x_of[a * 16 : a * 16 + 8] + x_of[a * 16 + 8 : a * 16 + 16]
             from_y = y_of[b * 16 : b * 16 + 8] + y_of[b * 16 + 8 : b * 16 + 16]
-            spec = spec_ref[:, k, outs]
+            spec = spec_ref[:, k, cols]
             out_ref[:, k, outs] = (
                 spec - (courant * abs(COS[k])) * (spec - from_x) - (courant * abs(SIN[k])) * (spec - from_y)
             )
-        pltpu.make_async_copy(out_ref.at[:, :, outs], out_hbm.at[:, :, outs], sems.at[MOVE_SEMS + c]).start()
+        pltpu.make_async_copy(out_ref.at[:, :, outs], out_hbm.at[:, :, outs], sems.at[2 + c]).start()
         return carry
 
     lax.fori_loop(0, HALF // NB, block, 0)
     for c in range(HALF // NB):
         outs = pl.ds(c * NB, NB)
-        pltpu.make_async_copy(out_ref.at[:, :, outs], out_hbm.at[:, :, outs], sems.at[MOVE_SEMS + c]).wait()
-    if half == 0:
-        copies[-1].wait()
-
-
-def source_kernel(moved0_hbm, moved1_hbm, wind_ref, diss_ref, out_hbm, moved_ref, push_ref, new_ref, loads, stores):
-    copies = []
+        pltpu.make_async_copy(out_ref.at[:, :, outs], out_hbm.at[:, :, outs], sems.at[2 + c]).wait()
+    wait_copies(stores)
+
+
+def source_kernel(moved0_hbm, moved1_hbm, wind_ref, out_hbm, push_ref, new_ref, moved0_ref, moved1_ref, loads, stores):
+    pairs = []
     for i in range(GS):
-        for half, moved_hbm in ((0, moved0_hbm), (1, moved1_hbm)):
-            target = moved_ref.at[i, :, half * HALF : half * HALF + HALF]
-            copies.append(pltpu.make_async_copy(moved_hbm.at[i], target, loads.at[2 * i + half]))
-    for copy in copies:
-        copy.start()
+        pairs += [(moved0_hbm.at[i], moved0_ref.at[i]), (moved1_hbm.at[i], moved1_ref.at[i])]
+    copies = start_copies(pairs, loads)
     up = group_scale()[0]
     cos_tiles, sin_tiles = direction_tiles(COS), direction_tiles(SIN)
 
@@ -364,25 +363,27 @@
         for g in range(3):
             push_ref[c, 8 * g : 8 * g + 8, :] = pull * (east * cos_tiles[g] + north * sin_tiles[g])
         push_ref[c, 24:32, :] = (0.25 * DT_SRC) * (density / WATER_DENSITY)
-        push_ref[c, 32:40, :] = DT_SRC * jnp.broadcast_to(diss_ref[pl.ds(c, 1), :], (8, 128))
+        push_ref[c, 32:40, :] = DT_SRC * jnp.broadcast_to(wind_ref[pl.ds(80 + c, 1), :], (8, 128))
         return carry
 
     lax.fori_loop(0, PTS // 128, prepare, 0)
     for i in range(GS):
         inv_c, omega, wavenum = OMEGA[i] / G_ACC * up, OMEGA[i] * up, OMEGA[i] ** 2 / G_ACC * (up * up)
-        copies[2 * i].wait()
-        copies[2 * i + 1].wait()
-
-        def block(c, carry):
-            cols = pl.ds(pl.multiple_of(c * 128, 128), 128)
-            share, loss = push_ref[c, 24:32, :] * omega, push_ref[c, 32:40, :] * wavenum
-            for g in range(3):
-                rows = slice(8 * g, 8 * g + 8)
-                excess = jnp.maximum(push_ref[c, rows, :] * inv_c - 1.0, 0.0)
-                new_ref[i, rows, cols] = moved_ref[i, rows, cols] * jnp.exp(share * excess - loss)
-            return carry
-
-        lax.fori_loop(0, PTS // 128, block, 0, unroll=4)
+        wait_copies(copies[2 * i : 2 * i + 2])
+        for half, moved_ref in ((0, moved0_ref), (1, moved1_ref)):
+
+            def block(c, carry):
+                at = c + half * (HALF // 128)
+                cols = pl.ds(pl.multiple_of(c * 128, 128), 128)
+                outs = pl.ds(pl.multiple_of(at * 128, 128), 128)
+                share, loss = push_ref[at, 24:32, :] * omega, push_ref[at, 32:40, :] * wavenum
+                for g in range(3):
+                    rows = slice(8 * g, 8 * g + 8)
+                    excess = jnp.maximum(push_ref[at, rows, :] * inv_c - 1.0, 0.0)
+                    new_ref[i, rows, outs] = moved_ref[i, rows, cols] * jnp.exp(share * excess - loss)
+                return carry
+
+            lax.fori_loop(0, HALF // 128, block, 0, unroll=4)
         pltpu.make_async_copy(new_ref.at[i], out_hbm.at[i], stores.at[i]).start()
     for i in range(GS):
         pltpu.make_async_copy(new_ref.at[i], out_hbm.at[i], stores.at[i]).wait()
@@ -396,14 +397,26 @@
     return jax.ShapeDtypeStruct(dims, dtype)
 
 
-def call(body, name, out, specs, scratch=(), mib=64, microseconds=1.0, out_specs=None, behind=False, mark=False):
+def resident(*dims, dtype=F32):
+    return pltpu.VMEM(dims, dtype)
+
+
+def distant(*dims, dtype=F32):
+    return pltpu.HBM(dims, dtype)
+
+
+def in_hbm(x):
+    return pltpu.with_memory_space_constraint(x, pltpu.HBM)
+
+
+def call(body, name, out, specs, scratch=(), mib=24, microseconds=1.0, out_specs=None, behind=False, mark=False):
     out = list(out)
     out_specs = [VMEM] * len(out) if out_specs is None else list(out_specs)
     specs = [*specs, VMEM] if behind else specs
     inputs = len(specs) - behind
     outputs = len(out)
     if mark:
-        out.append(array(8, 128))
+        out.append(resident(8, 128))
         out_specs.append(VMEM)
 
     def kernel(*refs):
@@ -427,24 +440,31 @@
 
 def on_device(spectrum, forcing, send_rows, point_slot, remap_weight, neighbours, halo_send):
     dma = pltpu.SemaphoreType.DMA
-    outgoing, to_before, to_after, operand, mark = call(
+    outgoing, to_before, to_after, operand, spec, mark = call(
         first_kernel,
         "first",
-        [array(TILES, 8, 128), array(GS, ND, RIM), array(GS, ND, RIM), array(KCOPIES * 16, PTS, dtype=BF)],
+        [
+            distant(TILES, 8, 128),
+            distant(GS, ND, RIM),
+            distant(GS, ND, RIM),
+            resident(KCOPIES * 16, PTS, dtype=BF),
+            resident(GS, ND, PTS),
+        ],
         [HBM] * 4,
         [
+            pltpu.VMEM((TILES, CAP), I32),
             pltpu.VMEM((4, PTS), F32),
-            pltpu.VMEM((TILES, CAP), I32),
             pltpu.VMEM((2, RIM), I32),
-            pltpu.VMEM((GS, ND, PTS), F32),
             pltpu.VMEM((TILES, 8, 128), F32),
+            pltpu.VMEM((GS, ND, RIM), F32),
+            pltpu.VMEM((GS, ND, RIM), F32),
             dma((4,)),
             dma((TILES // 8,)),
         ],
         microseconds=5.0,
-        out_specs=[HBM, VMEM, VMEM, VMEM],
+        out_specs=[HBM, HBM, HBM, VMEM, VMEM],
         mark=True,
-    )(forcing, send_rows, halo_send.reshape(2, RIM), spectrum)
+    )(*map(in_hbm, (send_rows, forcing, halo_send.reshape(2, RIM), spectrum)))
     arrived = lax.all_to_all(outgoing, "tile", split_axis=0, concat_axis=0, tiled=True)
 
     up = [(d, d + 1) for d in range(TILES - 1)]
@@ -453,85 +473,89 @@
 
     blocks = HALF // NB
     scratch = [
-        pltpu.VMEM((KCOPIES * 16, PTS), BF),
+        pltpu.VMEM((4, PTS), I32),
+        pltpu.VMEM((KCOPIES * 16, 2 * RIM), BF),
         pltpu.VMEM((GS, ND, HALF), F32),
-        pltpu.VMEM((KCOPIES * 16, 2 * RIM), BF),
-        pltpu.VMEM((4, HALF), I32),
-        pltpu.VMEM((GS, ND, RIM), F32),
-        pltpu.VMEM((GS, ND, RIM), F32),
-        pltpu.VMEM((GS, ND, HALF), F32),
-        dma((MOVE_SEMS + blocks,)),
+        dma((2 + blocks,)),
     ]
     moved0, rims, mark = call(
         functools.partial(move_kernel, 0),
         "move0",
-        [array(GS, ND, HALF), array(KCOPIES * 16, 2 * RIM, dtype=BF)],
-        [HBM] * 5,
+        [distant(GS, ND, HALF), distant(KCOPIES * 16, 2 * RIM, dtype=BF)],
+        [VMEM] * 4 + [HBM],
         scratch,
         microseconds=5.5,
         out_specs=[HBM, HBM],
         behind=True,
         mark=True,
-    )(spectrum, operand, low_rim, high_rim, neighbours, mark)
+    )(spec, operand, low_rim, high_rim, in_hbm(neighbours), mark)
     wind, moments, mark = call(
         wind_kernel,
         "wind",
         [array(80, 128), array(80, 128)],
-        [VMEM, HBM, HBM, VMEM],
+        [HBM, HBM, HBM, VMEM],
         [
             pltpu.VMEM((256, 6 * 256), BF),
+            pltpu.VMEM((TILES, 8, 128), F32),
             pltpu.VMEM((4, PTS), I32),
             pltpu.VMEM((4, PTS), F32),
-            dma((2,)),
+            dma((3,)),
         ],
         microseconds=6.0,
         behind=True,
         mark=True,
-    )(arrived, point_slot, remap_weight, spectrum, mark)
+    )(in_hbm(arrived), in_hbm(point_slot), in_hbm(remap_weight), spec, mark)
     others = [lax.ppermute(moments, "freq", [(i, (i + n) % 4) for i in range(4)]) for n in (1, 2, 3)]
     moved1, mark = call(
-        lambda spec, x, rim, near, *refs: move_kernel(1, spec, x, rim, None, near, *refs),
+        lambda spec_ref, x_ref, rim_ref, near_ref, *refs: move_kernel(1, spec_ref, x_ref, rim_ref, None, near_ref, *refs),
         "move1",
-        [array(GS, ND, HALF)],
-        [HBM] * 4,
+        [distant(GS, ND, HALF)],
+        [VMEM] * 2 + [HBM] * 2,
         scratch,
         microseconds=5.0,
         out_specs=[HBM],
         behind=True,
         mark=True,
-    )(spectrum, operand, rims, neighbours, mark)
-
-    diss, slot_sums = call(
+    )(spec, operand, rims, in_hbm(neighbours), mark)
+
+    state, slot_sums = call(
         field_kernel,
         "fields",
-        [array(16, 128), array(TILES, 2, 128)],
-        [VMEM] * 7,
-        [pltpu.VMEM((16, 128), F32)],
+        [resident(96, 128), array(TILES, 2, 128)],
+        [VMEM] * 5 + [HBM] * 2,
+        [pltpu.VMEM((16, 128), F32), pltpu.VMEM((4, PTS), I32), pltpu.VMEM((4, PTS), F32), dma((2,))],
         microseconds=3.0,
         behind=True,
-    )(moments, *others, wind, point_slot, remap_weight, mark)
+    )(moments, *others, wind, in_hbm(point_slot), in_hbm(remap_weight), mark)
     arrived_sums = lax.all_to_all(slot_sums, "tile", split_axis=0, concat_axis=0, tiled=True)
 
     new_spectrum, mark = call(
         source_kernel,
         "source",
         [array(GS, ND, PTS)],
-        [HBM, HBM, VMEM, VMEM],
+        [HBM, HBM, VMEM],
         [
-            pltpu.VMEM((GS, ND, PTS), F32),
             pltpu.VMEM((PTS // 128, 40, 128), F32),
             pltpu.VMEM((GS, ND, PTS), F32),
+            pltpu.VMEM((GS, ND, HALF), F32),
+            pltpu.VMEM((GS, ND, HALF), F32),
             dma((2 * GS,)),
             dma((GS,)),
         ],
         microseconds=3.0,
         out_specs=[HBM],
         mark=True,
-    )(moved0, moved1, wind, diss)
-
-    (returned,) = call(band_kernel, "band", [array(16, 128)], [VMEM] * 2, microseconds=2.5, behind=True)(
-        arrived_sums, send_rows, mark
-    )
+    )(in_hbm(moved0), in_hbm(moved1), state)
+
+    (returned,) = call(
+        band_kernel,
+        "band",
+        [array(16, 128)],
+        [VMEM, HBM],
+        [pltpu.VMEM((TILES, CAP), I32), dma((1,))],
+        microseconds=2.5,
+        behind=True,
+    )(arrived_sums, in_hbm(send_rows), mark)
     return (new_spectrum, returned.reshape(1, PTS))
 
 

time: 88.1 us -> 80.7 us (0.916)
  Pallas kernels: 43.5 us -> 34.7 us
  waiting for transfers between devices: 10.2 us -> 11.7 us
    pallas_call x7, Pallas kernels: 43.5 us -> 34.7 us  [the longest x1 6.53 us: on_device(): call(wind_kernel, 'wind', [array(80, 128), array(80, 128)], [HBM, HBM, HB...]
    all_to_all x1, waiting for transfers between devices: 5.61 us -> 7.09 us  [on_device(): lax.all_to_all(slot_sums, 'tile', split_axis=0, concat_axis=0, tiled=True)]
  transfers between devices with their start and end apart: 7 -> 7, of which waited for: 3 -> 3; matrix products, arithmetic and copies ran while one was open for 0% -> 0% of each run, Pallas kernels for 23% -> 18%
where the time goes in v4:
time: 80.7 us; the launch traced here: 80.1 us
  Pallas kernels  34.7 us (43%)
  starting transfers between devices  32.9 us (41%)
  waiting for transfers between devices  11.7 us (14%)
    all_to_all x1, starting transfers between devices, on_device(): lax.all_to_all(outgoing, 'tile', split_axis=0, concat_axis=0, tiled=True)  13.4 us
    all_to_all x1, starting transfers between devices, on_device(): lax.all_to_all(slot_sums, 'tile', split_axis=0, concat_axis=0, tiled=True)  10.4 us
    all_to_all x1, waiting for transfers between devices, on_device(): lax.all_to_all(slot_sums, 'tile', split_axis=0, concat_axis=0, tiled=True)  7.09 us
    pallas_call x1, Pallas kernels, on_device(): call(wind_kernel, 'wind', [array(80, 128), array(80, 128)], [HBM, HBM, HB...  6.53 us
    pallas_call x1, Pallas kernels, on_device(): call(first_kernel, 'first', [distant(TILES, 8, 128), distant(GS, ND, RIM)...  6.33 us
    pallas_call x1, Pallas kernels, on_device(): call(functools.partial(move_kernel, 0), 'move0', [distant(GS, ND, HALF),...  5.73 us
    pallas_call x1, Pallas kernels, on_device(): call(lambda spec_ref, x_ref, rim_ref, near_ref, *refs: move_kernel(1, spe...  5.72 us
    pallas_call x1, Pallas kernels, on_device(): call(field_kernel, 'fields', [resident(96, 128), array(TILES, 2, 128)], [...  3.92 us
  transfers between devices with their start and end apart: 7, of which 3 were waited for; matrix products, arithmetic and copies ran while one was open for 0% of the time, Pallas kernels for 18%

profile of v4, /device:TPU:1, one launch (start us, length us, event | category | flops | bytes accessed | tf_op | source)
XLA Modules:
  0.0 80.1 jit_solution(10743503437987723616)
XLA Ops:
  0.6 6.3 %first.1 = (f32[64,8,128]{2,1,0:T(8,128)}, f32[8,24,128]{2,1,0:T(8,128)}, f32[8,24,128]{2,1,0:T(8,128)}, bf16[480,2048]{1,0:T(8,128)(2,1)S(1)}, f32[8,24,2048]{2,1,0:T(8,128)S(1)}, /*index=5*/f32[8,128]{1,0:T(8,128)S(1)}) custom-call(s32[64,256]{1,0:T(8,128)} %refs_1_.5, f32[4,2048]{1,0:T(4,128)} %refs_1_.3, s32[2,128]{1,0:T(2,128)} %bitcast.3, ...), custom_call_target="tpu_custom_call" | custom-call | bytes 15000000 | tf_op jit(solution)/shard_map/first/pallas_call | solution.py:443
  7.0 13.4 %all-to-all-start = ((f32[64,8,128]{2,1,0:T(8,128)}), f32[64,8,128]{2,1,0:T(8,128)}, u32[]{:S(2)}, u32[]{:S(2)}) async-start(f32[64,8,128]{2,1,0:T(8,128)} %get-tuple-element.27), calls=%async_computation | async-start | bytes 524288 | tf_op jit(solution)/shard_map/all_to_all | solution.py:468
  20.3 3.5 %collective-permute-start = (f32[8,24,128]{2,1,0:T(8,128)}, f32[8,24,128]{2,1,0:T(8,128)S(1)}, u32[]{:S(2)}, u32[]{:S(2)}) collective-permute-start(f32[8,24,128]{2,1,0:T(8,128)} %get-tuple-element.22), channel_id=1, source_target_pairs={{0,4},{4,8},{8,12},{12,16},{16,20},{20,24},{24,28},{28,32},{32,36}... | collective-permute-start | bytes 294920 | tf_op jit(solution)/shard_map/ppermute | solution.py:471
  23.9 1.9 %collective-permute-start.1 = (f32[8,24,128]{2,1,0:T(8,128)}, f32[8,24,128]{2,1,0:T(8,128)S(1)}, u32[]{:S(2)}, u32[]{:S(2)}) collective-permute-start(f32[8,24,128]{2,1,0:T(8,128)} %get-tuple-element.23), channel_id=1, source_target_pairs={{4,0},{8,4},{12,8},{16,12},{20,16},{24,20},{28,24},{32,28},{36,32}... | collective-permute-start | bytes 294920 | tf_op jit(solution)/shard_map/ppermute | solution.py:472
  25.8 0.7 collective-permute-done.refs_2_
  26.5 3.9 %collective-permute-done.1.refs_3_ = f32[8,24,128]{2,1,0:T(8,128)S(1)} collective-permute-done((f32[8,24,128]{2,1,0:T(8,128)}, f32[8,24,128]{2,1,0:T(8,128)S(1)}, u32[]{:S(2)}, u32[]{:S(2)}) %collective-permute-start.1) | collective-permute-done | bytes 98336 | tf_op jit(solution)/shard_map/ppermute | solution.py:472
  30.4 5.7 %move0.1 = (f32[8,24,1024]{2,1,0:T(8,128)}, bf16[480,256]{1,0:T(8,128)(2,1)}, f32[8,128]{1,0:T(8,128)S(1)}) custom-call(f32[8,24,2048]{2,1,0:T(8,128)S(1)} %get-tuple-element.20.refs_0_.refs_3_, bf16[480,2048]{1,0:T(8,128)(2,1)S(1)} %get-tuple-element.21.refs_1_, f32[8,24,128]{2,1,0:T(8,128)S(1)} %collective-permute-done.refs_2_, ...), custom_call_target="tpu_custom_call" | custom-call | bytes 16500000 | tf_op jit(solution)/shard_map/move0/pallas_call | solution.py:481
  36.2 0.0 all-to-all-done.refs_0_
  36.2 0.0 copy-start
  36.2 6.5 %wind.1 = (f32[80,128]{1,0:T(8,128)S(1)}, f32[80,128]{1,0:T(8,128)S(1)}, f32[8,128]{1,0:T(8,128)S(1)}) custom-call(f32[64,8,128]{2,1,0:T(8,128)} %all-to-all-done.refs_0_, s32[4,2048]{1,0:T(4,128)} %refs_5_.1, f32[4,2048]{1,0:T(4,128)} %refs_6_.1, f32[8,24,2048]{2,1,0:T(8,128)S(1)} %get-tuple-element.20.refs_0_.refs_3_, f32[8,128]{1,0:T(8,128)S(1)} %get-tuple-element.28.refs_4_), custom_call_target="tpu_custom_call" | custom-call | bytes 18000000 | tf_op jit(solution)/shard_map/wind/pallas_call | solution.py:492
  42.7 2.5 %collective-permute-start.4 = (f32[80,128]{1,0:T(8,128)S(1)}, f32[80,128]{1,0:T(8,128)S(1)}, u32[]{:S(2)}, u32[]{:S(2)}) collective-permute-start(f32[80,128]{1,0:T(8,128)S(1)} %get-tuple-element.31.refs_0_), channel_id=1, source_target_pairs={{0,3},{1,0},{2,1},{3,2},{4,7},{5,4},{6,5},{7,6},{8,11},{9,8},{10,9... | collective-permute-start | bytes 122888 | tf_op jit(solution)/shard_map/ppermute | solution.py:508
  45.2 0.5 collective-permute-start.3
  45.8 0.6 collective-permute-start.2
  46.4 0.0 copy-done
  46.4 5.7 %move1.1 = (f32[8,24,1024]{2,1,0:T(8,128)}, f32[8,128]{1,0:T(8,128)S(1)}) custom-call(f32[8,24,2048]{2,1,0:T(8,128)S(1)} %get-tuple-element.20.refs_0_.refs_3_, bf16[480,2048]{1,0:T(8,128)(2,1)S(1)} %get-tuple-element.21.refs_1_, bf16[480,256]{1,0:T(8,128)(2,1)S(1)} %copy-done, s32[4,2048]{1,0:T(4,128)} %refs_3_.3, f32[8,128]{1,0:T(8,128)S(1)} %get-tuple-element.29.refs_4_), custom_call_target="tpu_custom_call" | custom-call | bytes 15000000 | tf_op jit(solution)/shard_map/move1/pallas_call | solution.py:509
  52.1 0.0 collective-permute-done.4.refs_3_
  52.1 0.0 collective-permute-done.3.refs_2_
  52.1 0.0 collective-permute-done.2.refs_1_
  52.1 3.9 %fields.1 = (f32[96,128]{1,0:T(8,128)S(1)}, f32[64,2,128]{2,1,0:T(2,128)}) custom-call(f32[80,128]{1,0:T(8,128)S(1)} %get-tuple-element.31.refs_0_, f32[80,128]{1,0:T(8,128)S(1)} %collective-permute-done.2.refs_1_, f32[80,128]{1,0:T(8,128)S(1)} %collective-permute-done.3.refs_2_, f32[80,128]{1,0:T(8,128)S(1)} %collective-permute-done.4.refs_3_, ...), custom_call_target="tpu_custom_call" | custom-call | bytes 9000000 | tf_op jit(solution)/shard_map/fields/pallas_call | solution.py:521
  56.1 10.4 %all-to-all-start.1 = ((f32[64,2,128]{2,1,0:T(2,128)}), f32[64,2,128]{2,1,0:T(2,128)S(1)}, u32[]{:S(2)}, u32[]{:S(2)}) async-start(f32[64,2,128]{2,1,0:T(2,128)} %get-tuple-element.36), calls=%async_computation.1 | async-start | bytes 131072 | tf_op jit(solution)/shard_map/all_to_all | solution.py:530
  66.5 2.7 %source.1 = (f32[8,24,2048]{2,1,0:T(8,128)}, f32[8,128]{1,0:T(8,128)S(1)}) custom-call(f32[8,24,1024]{2,1,0:T(8,128)} %get-tuple-element.25.refs_0_, f32[8,24,1024]{2,1,0:T(8,128)} %get-tuple-element.30.refs_1_, f32[96,128]{1,0:T(8,128)S(1)} %get-tuple-element.34.refs_2_), custom_call_target="tpu_custom_call" | custom-call | bytes 9000000 | tf_op jit(solution)/shard_map/source/pallas_call | solution.py:532
  69.2 7.1 %all-to-all-done.1.refs_0_ = f32[64,2,128]{2,1,0:T(2,128)S(1)} async-done(((f32[64,2,128]{2,1,0:T(2,128)}), f32[64,2,128]{2,1,0:T(2,128)S(1)}, u32[]{:S(2)}, u32[]{:S(2)}) %all-to-all-start.1) | async-done | bytes 65568 | tf_op jit(solution)/shard_map/all_to_all | solution.py:530
  76.3 3.8 %band.1 = f32[16,128]{1,0:T(8,128)} custom-call(f32[64,2,128]{2,1,0:T(2,128)S(1)} %all-to-all-done.1.refs_0_, s32[64,256]{1,0:T(8,128)} %refs_1_.5, f32[8,128]{1,0:T(8,128)S(1)} %get-tuple-element.37.refs_2_), custom_call_target="tpu_custom_call" | custom-call | bytes 7500000 | tf_op jit(solution)/shard_map/band/pallas_call | solution.py:550
Async XLA Ops:
  7.0 29.2 %all-to-all-start = ((f32[64,8,128]{2,1,0:T(8,128)}), f32[64,8,128]{2,1,0:T(8,128)}, u32[]{:S(2)}, u32[]{:S(2)}) async-start(f32[64,8,128]{2,1,0:T(8,128)} %get-tuple-element.27), calls=%async_computation | async-start | bytes 524288 | tf_op jit(solution)/shard_map/all_to_all | solution.py:468
  20.3 6.2 %collective-permute-start = (f32[8,24,128]{2,1,0:T(8,128)}, f32[8,24,128]{2,1,0:T(8,128)S(1)}, u32[]{:S(2)}, u32[]{:S(2)}) collective-permute-start(f32[8,24,128]{2,1,0:T(8,128)} %get-tuple-element.22), channel_id=1, source_target_pairs={{0,4},{4,8},{8,12},{12,16},{16,20},{20,24},{24,28},{28,32},{32,36}... | collective-permute-start | bytes 294920 | tf_op jit(solution)/shard_map/ppermute | solution.py:471
  23.9 6.5 %collective-permute-start.1 = (f32[8,24,128]{2,1,0:T(8,128)}, f32[8,24,128]{2,1,0:T(8,128)S(1)}, u32[]{:S(2)}, u32[]{:S(2)}) collective-permute-start(f32[8,24,128]{2,1,0:T(8,128)} %get-tuple-element.23), channel_id=1, source_target_pairs={{4,0},{8,4},{12,8},{16,12},{20,16},{24,20},{28,24},{32,28},{36,32}... | collective-permute-start | bytes 294920 | tf_op jit(solution)/shard_map/ppermute | solution.py:472
  36.2 10.2 %copy-start = (bf16[480,256]{1,0:T(8,128)(2,1)S(1)}, bf16[480,256]{1,0:T(8,128)(2,1)}, u32[]{:S(2)}) copy-start(bf16[480,256]{1,0:T(8,128)(2,1)} %get-tuple-element.26.refs_2_) | copy-start | bytes 737284
  42.7 9.4 %collective-permute-start.4 = (f32[80,128]{1,0:T(8,128)S(1)}, f32[80,128]{1,0:T(8,128)S(1)}, u32[]{:S(2)}, u32[]{:S(2)}) collective-permute-start(f32[80,128]{1,0:T(8,128)S(1)} %get-tuple-element.31.refs_0_), channel_id=1, source_target_pairs={{0,3},{1,0},{2,1},{3,2},{4,7},{5,4},{6,5},{7,6},{8,11},{9,8},{10,9... | collective-permute-start | bytes 122888 | tf_op jit(solution)/shard_map/ppermute | solution.py:508
  45.2 6.9 %collective-permute-start.3 = (f32[80,128]{1,0:T(8,128)S(1)}, f32[80,128]{1,0:T(8,128)S(1)}, u32[]{:S(2)}, u32[]{:S(2)}) collective-permute-start(f32[80,128]{1,0:T(8,128)S(1)} %get-tuple-element.31.refs_0_), channel_id=1, source_target_pairs={{0,2},{1,3},{2,0},{3,1},{4,6},{5,7},{6,4},{7,5},{8,10},{9,11},{10,... | collective-permute-start | bytes 122888 | tf_op jit(solution)/shard_map/ppermute | solution.py:508
  45.8 6.4 %collective-permute-start.2 = (f32[80,128]{1,0:T(8,128)S(1)}, f32[80,128]{1,0:T(8,128)S(1)}, u32[]{:S(2)}, u32[]{:S(2)}) collective-permute-start(f32[80,128]{1,0:T(8,128)S(1)} %get-tuple-element.31.refs_0_), channel_id=1, source_target_pairs={{0,1},{1,2},{2,3},{3,0},{4,5},{5,6},{6,7},{7,4},{8,9},{9,10},{10,1... | collective-permute-start | bytes 122888 | tf_op jit(solution)/shard_map/ppermute | solution.py:508
  56.1 20.2 %all-to-all-start.1 = ((f32[64,2,128]{2,1,0:T(2,128)}), f32[64,2,128]{2,1,0:T(2,128)S(1)}, u32[]{:S(2)}, u32[]{:S(2)}) async-start(f32[64,2,128]{2,1,0:T(2,128)} %get-tuple-element.36), calls=%async_computation.1 | async-start | bytes 131072 | tf_op jit(solution)/shard_map/all_to_all | solution.py:530

commit v5 on v4

--- a/solution.py
+++ b/solution.py
@@ -111,16 +111,42 @@
         copy.wait()
 
 
-def first_kernel(
-    rows_hbm, forcing_hbm, list_hbm, spec_hbm, out_hbm, before_hbm, after_hbm, x_ref, spec_ref,
-    rows_ref, forcing_ref, list_ref, out_ref, before_ref, after_ref, sems, out_sems,
-):
-    sources = ((rows_hbm, rows_ref), (forcing_hbm, forcing_ref), (list_hbm, list_ref), (spec_hbm, spec_ref))
-    wait_copies(start_copies(sources, sems))
+def start_copies(pairs, sems, first=0):
+    copies = [pltpu.make_async_copy(src, dst, sems.at[first + n]) for n, (src, dst) in enumerate(pairs)]
+    for copy in copies:
+        copy.start()
+    return copies
+
+
+def wait_copies(copies):
+    for copy in copies:
+        copy.wait()
+
+
+def rim_kernel(list_hbm, spec_hbm, before_hbm, after_hbm, spec_ref, list_ref, before_ref, after_ref, sems):
+    wait_copies(start_copies(((list_hbm, list_ref), (spec_hbm, spec_ref)), sems))
     rims = []
     for side, rim_ref in ((0, before_ref), (1, after_ref)):
         index = jnp.broadcast_to(list_ref[side : side + 1, :], (8, 128))
         rims.append((index & 127, index >> 7, rim_ref))
+
+    def step(i, carry):
+        for low, high, rim_ref in rims:
+            for g in range(3):
+                rows = slice(8 * g, 8 * g + 8)
+                got = None
+                for h in range(16):
+                    piece = lane_gather(spec_ref[i, rows, h * 128 : h * 128 + 128], low)
+                    got = piece if h == 0 else jnp.where(high == h, piece, got)
+                rim_ref[i, rows, :] = got
+        return carry
+
+    lax.fori_loop(0, GS, step, 0)
+    wait_copies(start_copies(((before_ref, before_hbm), (after_ref, after_hbm)), sems))
+
+
+def outgoing_kernel(rows_hbm, forcing_hbm, out_hbm, rows_ref, forcing_ref, out_ref, sems, out_sems):
+    wait_copies(start_copies(((rows_hbm, rows_ref), (forcing_hbm, forcing_ref)), sems))
 
     def step(q, carry):
         d = pl.ds(pl.multiple_of(q * 8, 8), 8)
@@ -135,25 +161,12 @@
                     got = piece if h == 0 else jnp.where(high == h, piece, got)
                 out_ref[d, 2 * i + half, :] = got
         pltpu.make_async_copy(out_ref.at[d], out_hbm.at[d], out_sems.at[q]).start()
-        for low, high, rim_ref in rims:
-            for g in range(3):
-                rows = slice(8 * g, 8 * g + 8)
-                got = None
-                for h in range(16):
-                    piece = lane_gather(spec_ref[q, rows, h * 128 : h * 128 + 128], low)
-                    got = piece if h == 0 else jnp.where(high == h, piece, got)
-                rim_ref[q, rows, :] = got
-        for half in range(2):
-            cols = pl.ds(pl.multiple_of(q * 256 + half * 128, 128), 128)
-            put_parts(spec_ref, cols, x_ref, cols)
         return carry
 
     lax.fori_loop(0, TILES // 8, step, 0)
-    stores = start_copies(((before_ref, before_hbm), (after_ref, after_hbm)), sems)
     for q in range(TILES // 8):
         d = pl.ds(q * 8, 8)
         pltpu.make_async_copy(out_ref.at[d], out_hbm.at[d], out_sems.at[q]).wait()
-    wait_copies(stores)
 
 
 def weight_matrix(slot_ref, weight_ref, cols, width):
@@ -227,7 +240,7 @@
                 wind_ref[pl.ds(n * 16 + c * (WB // 128) + half, 1), :] = row[:, half * 128 : half * 128 + 128]
         return carry
 
-    lax.fori_loop(0, PTS // WB, block, 0)
+    lax.fori_loop(0, PTS // WB, block, 0, unroll=8)
 
 
 def field_kernel(
@@ -265,7 +278,7 @@
         right = jnp.concatenate([w0, w0, w1], axis=1)
         return acc + lax.dot_general(left, right, (((1,), (1,)), ((), ())), preferred_element_type=F32)
 
-    acc = lax.fori_loop(0, PTS // WB, block, jnp.zeros((TILES, CAP), F32))
+    acc = lax.fori_loop(0, PTS // WB, block, jnp.zeros((TILES, CAP), F32), unroll=8)
     for half in range(2):
         sums_ref[:, half, :] = acc[:, half * 128 : half * 128 + 128]
 
@@ -283,24 +296,35 @@
             high = lax.broadcasted_iota(I32, (16, CAP), 0) == (index >> 7)
             v0, v1 = v0.astype(F32), v1.astype(F32)
             values.append(jnp.concatenate([jnp.where(high, v0, 0.0), jnp.where(high, v1, 0.0)], axis=0).astype(BF))
-            ones.append((lax.broadcasted_iota(I32, (128, CAP), 0) == (index & 127)).astype(F32).astype(BF))
+            match = lax.broadcasted_iota(jnp.int16, (128, CAP), 0) == (index & 127).astype(jnp.int16)
+            ones.append(jnp.where(match, jnp.ones((), BF), jnp.zeros((), BF)))
         left = jnp.concatenate(ones, axis=1)
         right = jnp.concatenate(values, axis=1)
         return acc + lax.dot_general(left, right, (((1,), (1,)), ((), ())), preferred_element_type=F32)
 
-    acc = lax.fori_loop(0, TILES // 8, eight_tiles, jnp.zeros((128, 32), F32))
+    acc = lax.fori_loop(0, TILES // 8, eight_tiles, jnp.zeros((128, 32), F32), unroll=8)
     out_ref[...] = jnp.transpose(acc[:, :16] + acc[:, 16:])
 
 
-def move_kernel(half, spec_ref, x_ref, low_ref, high_ref, near_hbm, *refs):
+def move_kernel(half, spec_ref, low_ref, high_ref, near_hbm, *refs):
     start = half * HALF
     if half == 0:
-        out_hbm, rim_hbm, near_ref, rim_ref, out_ref, sems = refs
+        out_hbm, rim_hbm, x_ref, near_ref, rim_ref, out_ref, sems, low_v, high_v, rim_sems = refs
         copies = start_copies(((near_hbm, near_ref),), sems)
-        put_parts(low_ref, slice(0, RIM), rim_ref, slice(0, RIM))
-        put_parts(high_ref, slice(0, RIM), rim_ref, slice(RIM, 2 * RIM))
+        rim_loads = start_copies(((low_ref, low_v), (high_ref, high_v)), rim_sems)
+
+        def put_block(h, carry):
+            cols = pl.ds(pl.multiple_of(h * 128, 128), 128)
+            put_parts(spec_ref, cols, x_ref, cols)
+            return carry
+
+        lax.fori_loop(0, PTS // 128, put_block, 0)
+        wait_copies(rim_loads)
+        put_parts(low_v, slice(0, RIM), rim_ref, slice(0, RIM))
+        put_parts(high_v, slice(0, RIM), rim_ref, slice(RIM, 2 * RIM))
         stores = start_copies(((rim_ref, rim_hbm),), sems, 1)
     else:
+        x_ref = high_ref
         out_hbm, near_ref, rim_ref, out_ref, sems = refs
         copies = start_copies(((near_hbm, near_ref), (low_ref, rim_ref)), sems)
         stores = []
@@ -440,36 +464,44 @@
 
 def on_device(spectrum, forcing, send_rows, point_slot, remap_weight, neighbours, halo_send):
     dma = pltpu.SemaphoreType.DMA
-    outgoing, to_before, to_after, operand, spec, mark = call(
-        first_kernel,
-        "first",
+    to_before, to_after, spec, mark = call(
+        rim_kernel,
+        "rims",
+        [distant(GS, ND, RIM), distant(GS, ND, RIM), resident(GS, ND, PTS)],
+        [HBM] * 2,
         [
-            distant(TILES, 8, 128),
-            distant(GS, ND, RIM),
-            distant(GS, ND, RIM),
-            resident(KCOPIES * 16, PTS, dtype=BF),
-            resident(GS, ND, PTS),
+            pltpu.VMEM((2, RIM), I32),
+            pltpu.VMEM((GS, ND, RIM), F32),
+            pltpu.VMEM((GS, ND, RIM), F32),
+            dma((2,)),
         ],
-        [HBM] * 4,
+        microseconds=3.0,
+        out_specs=[HBM, HBM, VMEM],
+        mark=True,
+    )(in_hbm(halo_send.reshape(2, RIM)), in_hbm(spectrum))
+    up = [(d, d + 1) for d in range(TILES - 1)]
+    low_rim = lax.ppermute(to_after, "tile", up)
+    high_rim = lax.ppermute(to_before, "tile", [(b, a) for a, b in up])
+
+    outgoing, mark = call(
+        outgoing_kernel,
+        "outgoing",
+        [distant(TILES, 8, 128)],
+        [HBM] * 2,
         [
             pltpu.VMEM((TILES, CAP), I32),
             pltpu.VMEM((4, PTS), F32),
-            pltpu.VMEM((2, RIM), I32),
             pltpu.VMEM((TILES, 8, 128), F32),
-            pltpu.VMEM((GS, ND, RIM), F32),
-            pltpu.VMEM((GS, ND, RIM), F32),
-            dma((4,)),
+            dma((2,)),
             dma((TILES // 8,)),
         ],
-        microseconds=5.0,
-        out_specs=[HBM, HBM, HBM, VMEM, VMEM],
+        microseconds=3.0,
+        out_specs=[HBM],
+        behind=True,
         mark=True,
-    )(*map(in_hbm, (send_rows, forcing, halo_send.reshape(2, RIM), spectrum)))
+    )(in_hbm(send_rows), in_hbm(forcing), mark)
+    outgoing, low_rim, high_rim = lax.optimization_barrier((outgoing, low_rim, high_rim))
     arrived = lax.all_to_all(outgoing, "tile", split_axis=0, concat_axis=0, tiled=True)
-
-    up = [(d, d + 1) for d in range(TILES - 1)]
-    low_rim = lax.ppermute(to_after, "tile", up)
-    high_rim = lax.ppermute(to_before, "tile", [(b, a) for a, b in up])
 
     blocks = HALF // NB
     scratch = [
@@ -478,17 +510,21 @@
         pltpu.VMEM((GS, ND, HALF), F32),
         dma((2 + blocks,)),
     ]
-    moved0, rims, mark = call(
+    moved0, rims, operand, mark = call(
         functools.partial(move_kernel, 0),
         "move0",
-        [distant(GS, ND, HALF), distant(KCOPIES * 16, 2 * RIM, dtype=BF)],
-        [VMEM] * 4 + [HBM],
-        scratch,
-        microseconds=5.5,
-        out_specs=[HBM, HBM],
+        [
+            distant(GS, ND, HALF),
+            distant(KCOPIES * 16, 2 * RIM, dtype=BF),
+            resident(KCOPIES * 16, PTS, dtype=BF),
+        ],
+        [VMEM] + [HBM] * 3,
+        scratch + [pltpu.VMEM((GS, ND, RIM), F32), pltpu.VMEM((GS, ND, RIM), F32), dma((2,))],
+        microseconds=7.5,
+        out_specs=[HBM, HBM, VMEM],
         behind=True,
         mark=True,
-    )(spec, operand, low_rim, high_rim, in_hbm(neighbours), mark)
+    )(spec, in_hbm(low_rim), in_hbm(high_rim), in_hbm(neighbours), mark)
     wind, moments, mark = call(
         wind_kernel,
         "wind",
@@ -507,16 +543,16 @@
     )(in_hbm(arrived), in_hbm(point_slot), in_hbm(remap_weight), spec, mark)
     others = [lax.ppermute(moments, "freq", [(i, (i + n) % 4) for i in range(4)]) for n in (1, 2, 3)]
     moved1, mark = call(
-        lambda spec_ref, x_ref, rim_ref, near_ref, *refs: move_kernel(1, spec_ref, x_ref, rim_ref, None, near_ref, *refs),
+        functools.partial(move_kernel, 1),
         "move1",
         [distant(GS, ND, HALF)],
-        [VMEM] * 2 + [HBM] * 2,
+        [VMEM, HBM, VMEM, HBM],
         scratch,
         microseconds=5.0,
         out_specs=[HBM],
         behind=True,
         mark=True,
-    )(spec, operand, rims, in_hbm(neighbours), mark)
+    )(spec, rims, operand, in_hbm(neighbours), mark)
 
     state, slot_sums = call(
         field_kernel,

time: 80.7 us -> 78.2 us (0.969)
  starting transfers between devices: 32.9 us -> 30.3 us
    all_to_all x1, waiting for transfers between devices: 0.01 us -> 3.86 us  [on_device(): lax.all_to_all(outgoing, 'tile', split_axis=0, concat_axis=0, tiled=True)]
    all_to_all x1, starting transfers between devices: 10.4 us -> 7.36 us  [on_device(): lax.all_to_all(slot_sums, 'tile', split_axis=0, concat_axis=0, tiled=True)]
    ppermute x1, waiting for transfers between devices: 3.91 us -> 0.91 us  [on_device(): high_rim = lax.ppermute(to_before, 'tile', [(b, a) for a, b in up])]
    pallas_call x1, Pallas kernels: 5.73 us -> 8.02 us  [on_device(): call(functools.partial(move_kernel, 0), 'move0', [distant(GS, ND, HALF),...]
    ppermute x1, starting transfers between devices: 3.54 us -> 4.94 us  [on_device(): low_rim = lax.ppermute(to_after, 'tile', up)]
    pallas_call x1, Pallas kernels: 6.53 us -> 5.33 us  [on_device(): call(wind_kernel, 'wind', [array(80, 128), array(80, 128)], [HBM, HBM, HB...]
    pallas_call x1, Pallas kernels: 3.84 us -> 2.78 us  [on_device(): call(band_kernel, 'band', [array(16, 128)], [VMEM, HBM], [pltpu.VMEM((TIL...]
    all_to_all x1, starting transfers between devices: 13.4 us -> 12.4 us  [on_device(): lax.all_to_all(outgoing, 'tile', split_axis=0, concat_axis=0, tiled=True)]
  transfers between devices with their start and end apart: 7 -> 7, of which waited for: 3 -> 3; matrix products, arithmetic and copies ran while one was open for 0% -> 0% of each run, Pallas kernels for 18% -> 25%
where the time goes in v5:
time: 78.2 us; the launch traced here: 77.6 us
  Pallas kernels  34.5 us (44%)
  starting transfers between devices  30.3 us (39%)
  waiting for transfers between devices  11.9 us (15%)
  between operations  0.94 us (1%)
    all_to_all x1, starting transfers between devices, on_device(): lax.all_to_all(outgoing, 'tile', split_axis=0, concat_axis=0, tiled=True)  12.4 us
    pallas_call x1, Pallas kernels, on_device(): call(functools.partial(move_kernel, 0), 'move0', [distant(GS, ND, HALF),...  8.02 us
    all_to_all x1, starting transfers between devices, on_device(): lax.all_to_all(slot_sums, 'tile', split_axis=0, concat_axis=0, tiled=True)  7.36 us
    all_to_all x1, waiting for transfers between devices, on_device(): lax.all_to_all(slot_sums, 'tile', split_axis=0, concat_axis=0, tiled=True)  7.09 us
    pallas_call x1, Pallas kernels, on_device(): call(functools.partial(move_kernel, 1), 'move1', [distant(GS, ND, HALF)],...  5.72 us
    pallas_call x1, Pallas kernels, on_device(): call(wind_kernel, 'wind', [array(80, 128), array(80, 128)], [HBM, HBM, HB...  5.33 us
    ppermute x1, starting transfers between devices, on_device(): low_rim = lax.ppermute(to_after, 'tile', up)  4.94 us
    all_to_all x1, waiting for transfers between devices, on_device(): lax.all_to_all(outgoing, 'tile', split_axis=0, concat_axis=0, tiled=True)  3.86 us
  transfers between devices with their start and end apart: 7, of which 3 were waited for; matrix products, arithmetic and copies ran while one was open for 0% of the time, Pallas kernels for 25%

profile of v5, /device:TPU:1, one launch (start us, length us, event | category | flops | bytes accessed | tf_op | source)
XLA Modules:
  0.0 77.6 jit_solution(6432371666570441972)
XLA Ops:
  0.6 3.5 %rims.1 = (f32[8,24,128]{2,1,0:T(8,128)}, f32[8,24,128]{2,1,0:T(8,128)}, f32[8,24,2048]{2,1,0:T(8,128)S(1)}, f32[8,128]{1,0:T(8,128)S(1)}) custom-call(s32[2,128]{1,0:T(2,128)} %bitcast.3, f32[8,24,2048]{2,1,0:T(8,128)} %refs_1_.4), custom_call_target="tpu_custom_call" | custom-call | bytes 9000000 | tf_op jit(solution)/shard_map/rims/pallas_call | solution.py:467
  4.1 4.9 %collective-permute-start = (f32[8,24,128]{2,1,0:T(8,128)}, f32[8,24,128]{2,1,0:T(8,128)S(1)}, u32[]{:S(2)}, u32[]{:S(2)}) collective-permute-start(f32[8,24,128]{2,1,0:T(8,128)} %get-tuple-element.27), channel_id=1, source_target_pairs={{0,4},{4,8},{8,12},{12,16},{16,20},{20,24},{24,28},{28,32},{32,36}... | collective-permute-start | bytes 294920 | tf_op jit(solution)/shard_map/ppermute | solution.py:483
  9.0 1.9 %collective-permute-start.1 = (f32[8,24,128]{2,1,0:T(8,128)}, f32[8,24,128]{2,1,0:T(8,128)S(1)}, u32[]{:S(2)}, u32[]{:S(2)}) collective-permute-start(f32[8,24,128]{2,1,0:T(8,128)} %get-tuple-element.28), channel_id=1, source_target_pairs={{4,0},{8,4},{12,8},{16,12},{20,16},{24,20},{28,24},{32,28},{36,32}... | collective-permute-start | bytes 294920 | tf_op jit(solution)/shard_map/ppermute | solution.py:484
  11.0 3.3 %outgoing.1 = (f32[64,8,128]{2,1,0:T(8,128)}, f32[8,128]{1,0:T(8,128)S(1)}) custom-call(s32[64,256]{1,0:T(8,128)} %refs_1_.7, f32[4,2048]{1,0:T(4,128)} %refs_1_.5, f32[8,128]{1,0:T(8,128)S(1)} %get-tuple-element.25.refs_2_), custom_call_target="tpu_custom_call" | custom-call | bytes 9000000 | tf_op jit(solution)/shard_map/outgoing/pallas_call | solution.py:486
  14.3 0.0 collective-permute-done.refs_1_
  14.3 0.0 copy-start.1
  14.3 0.9 %collective-permute-done.1.refs_2_ = f32[8,24,128]{2,1,0:T(8,128)S(1)} collective-permute-done((f32[8,24,128]{2,1,0:T(8,128)}, f32[8,24,128]{2,1,0:T(8,128)S(1)}, u32[]{:S(2)}, u32[]{:S(2)}) %collective-permute-start.1) | collective-permute-done | bytes 98336 | tf_op jit(solution)/shard_map/ppermute | solution.py:484
  15.2 0.0 copy-start.2
  15.2 12.4 %all-to-all-start = ((f32[64,8,128]{2,1,0:T(8,128)}), f32[64,8,128]{2,1,0:T(8,128)}, u32[]{:S(2)}, u32[]{:S(2)}) async-start(f32[64,8,128]{2,1,0:T(8,128)} %get-tuple-element.35), calls=%async_computation | async-start | bytes 524288 | tf_op jit(solution)/shard_map/all_to_all | solution.py:504
  27.6 0.0 copy-done.1
  27.6 0.0 copy-done.2
  27.6 8.0 %move0.1 = (f32[8,24,1024]{2,1,0:T(8,128)}, bf16[480,256]{1,0:T(8,128)(2,1)}, bf16[480,2048]{1,0:T(8,128)(2,1)S(1)}, f32[8,128]{1,0:T(8,128)S(1)}) custom-call(f32[8,24,2048]{2,1,0:T(8,128)S(1)} %get-tuple-element.24.refs_0_.refs_3_, f32[8,24,128]{2,1,0:T(8,128)} %copy-done.1, f32[8,24,128]{2,1,0:T(8,128)} %copy-done.2, s32[4,2048]{1,0:T(4,128)} %refs_3_.3, ...), custom_call_target="tpu_custom_call" | custom-call | bytes 22500000 | tf_op jit(solution)/shard_map/move0/pallas_call | solution.py:513
  35.6 3.9 %all-to-all-done.refs_0_ = f32[64,8,128]{2,1,0:T(8,128)} async-done(((f32[64,8,128]{2,1,0:T(8,128)}), f32[64,8,128]{2,1,0:T(8,128)}, u32[]{:S(2)}, u32[]{:S(2)}) %all-to-all-start) | async-done | bytes 262176 | tf_op jit(solution)/shard_map/all_to_all | solution.py:504
  39.5 0.0 copy-start
  39.5 5.3 %wind.1 = (f32[80,128]{1,0:T(8,128)S(1)}, f32[80,128]{1,0:T(8,128)S(1)}, f32[8,128]{1,0:T(8,128)S(1)}) custom-call(f32[64,8,128]{2,1,0:T(8,128)} %all-to-all-done.refs_0_, s32[4,2048]{1,0:T(4,128)} %refs_5_.1, f32[4,2048]{1,0:T(4,128)} %refs_6_.1, f32[8,24,2048]{2,1,0:T(8,128)S(1)} %get-tuple-element.24.refs_0_.refs_3_, f32[8,128]{1,0:T(8,128)S(1)} %get-tuple-element.36.refs_4_), custom_call_target="tpu_custom_call" | custom-call | bytes 18000000 | tf_op jit(solution)/shard_map/wind/pallas_call | solution.py:528
  44.8 2.6 %collective-permute-start.4 = (f32[80,128]{1,0:T(8,128)S(1)}, f32[80,128]{1,0:T(8,128)S(1)}, u32[]{:S(2)}, u32[]{:S(2)}) collective-permute-start(f32[80,128]{1,0:T(8,128)S(1)} %get-tuple-element.39.refs_0_), channel_id=1, source_target_pairs={{0,3},{1,0},{2,1},{3,2},{4,7},{5,4},{6,5},{7,6},{8,11},{9,8},{10,9... | collective-permute-start | bytes 122888 | tf_op jit(solution)/shard_map/ppermute | solution.py:544
  47.4 0.5 collective-permute-start.3
  47.9 0.6 collective-permute-start.2
  48.5 0.0 copy-done
  48.5 5.7 %move1.1 = (f32[8,24,1024]{2,1,0:T(8,128)}, f32[8,128]{1,0:T(8,128)S(1)}) custom-call(f32[8,24,2048]{2,1,0:T(8,128)S(1)} %get-tuple-element.24.refs_0_.refs_3_, bf16[480,256]{1,0:T(8,128)(2,1)S(1)} %copy-done, bf16[480,2048]{1,0:T(8,128)(2,1)S(1)} %get-tuple-element.34.refs_2_, s32[4,2048]{1,0:T(4,128)} %refs_3_.3, f32[8,128]{1,0:T(8,128)S(1)} %get-tuple-element.37.refs_4_), custom_call_target="tpu_custom_call" | custom-call | bytes 15000000 | tf_op jit(solution)/shard_map/move1/pallas_call | solution.py:545
  54.3 0.0 collective-permute-done.4.refs_3_
  54.3 0.0 collective-permute-done.3.refs_2_
  54.3 0.0 collective-permute-done.2.refs_1_
  54.3 3.2 %fields.1 = (f32[96,128]{1,0:T(8,128)S(1)}, f32[64,2,128]{2,1,0:T(2,128)}) custom-call(f32[80,128]{1,0:T(8,128)S(1)} %get-tuple-element.39.refs_0_, f32[80,128]{1,0:T(8,128)S(1)} %collective-permute-done.2.refs_1_, f32[80,128]{1,0:T(8,128)S(1)} %collective-permute-done.3.refs_2_, f32[80,128]{1,0:T(8,128)S(1)} %collective-permute-done.4.refs_3_, ...), custom_call_target="tpu_custom_call" | custom-call | bytes 9000000 | tf_op jit(solution)/shard_map/fields/pallas_call | solution.py:557
  57.5 7.4 %all-to-all-start.1 = ((f32[64,2,128]{2,1,0:T(2,128)}), f32[64,2,128]{2,1,0:T(2,128)S(1)}, u32[]{:S(2)}, u32[]{:S(2)}) async-start(f32[64,2,128]{2,1,0:T(2,128)} %get-tuple-element.44), calls=%async_computation.1 | async-start | bytes 131072 | tf_op jit(solution)/shard_map/all_to_all | solution.py:566
  64.9 2.7 %source.1 = (f32[8,24,2048]{2,1,0:T(8,128)}, f32[8,128]{1,0:T(8,128)S(1)}) custom-call(f32[8,24,1024]{2,1,0:T(8,128)} %get-tuple-element.32.refs_0_, f32[8,24,1024]{2,1,0:T(8,128)} %get-tuple-element.38.refs_1_, f32[96,128]{1,0:T(8,128)S(1)} %get-tuple-element.42.refs_2_), custom_call_target="tpu_custom_call" | custom-call | bytes 9000000 | tf_op jit(solution)/shard_map/source/pallas_call | solution.py:568
  67.5 7.1 %all-to-all-done.1.refs_0_ = f32[64,2,128]{2,1,0:T(2,128)S(1)} async-done(((f32[64,2,128]{2,1,0:T(2,128)}), f32[64,2,128]{2,1,0:T(2,128)S(1)}, u32[]{:S(2)}, u32[]{:S(2)}) %all-to-all-start.1) | async-done | bytes 65568 | tf_op jit(solution)/shard_map/all_to_all | solution.py:566
  74.6 2.8 %band.1 = f32[16,128]{1,0:T(8,128)} custom-call(f32[64,2,128]{2,1,0:T(2,128)S(1)} %all-to-all-done.1.refs_0_, s32[64,256]{1,0:T(8,128)} %refs_1_.7, f32[8,128]{1,0:T(8,128)S(1)} %get-tuple-element.45.refs_2_), custom_call_target="tpu_custom_call" | custom-call | bytes 7500000 | tf_op jit(solution)/shard_map/band/pallas_call | solution.py:586
Async XLA Ops:
  4.1 10.2 %collective-permute-start = (f32[8,24,128]{2,1,0:T(8,128)}, f32[8,24,128]{2,1,0:T(8,128)S(1)}, u32[]{:S(2)}, u32[]{:S(2)}) collective-permute-start(f32[8,24,128]{2,1,0:T(8,128)} %get-tuple-element.27), channel_id=1, source_target_pairs={{0,4},{4,8},{8,12},{12,16},{16,20},{20,24},{24,28},{28,32},{32,36}... | collective-permute-start | bytes 294920 | tf_op jit(solution)/shard_map/ppermute | solution.py:483
  9.0 6.1 %collective-permute-start.1 = (f32[8,24,128]{2,1,0:T(8,128)}, f32[8,24,128]{2,1,0:T(8,128)S(1)}, u32[]{:S(2)}, u32[]{:S(2)}) collective-permute-start(f32[8,24,128]{2,1,0:T(8,128)} %get-tuple-element.28), channel_id=1, source_target_pairs={{4,0},{8,4},{12,8},{16,12},{20,16},{24,20},{28,24},{32,28},{36,32}... | collective-permute-start | bytes 294920 | tf_op jit(solution)/shard_map/ppermute | solution.py:484
  14.3 13.3 %copy-start.1 = (f32[8,24,128]{2,1,0:T(8,128)}, f32[8,24,128]{2,1,0:T(8,128)S(1)}, u32[]{:S(2)}) copy-start(f32[8,24,128]{2,1,0:T(8,128)S(1)} %collective-permute-done.refs_1_) | copy-start | bytes 294916
  15.2 12.4 %copy-start.2 = (f32[8,24,128]{2,1,0:T(8,128)}, f32[8,24,128]{2,1,0:T(8,128)S(1)}, u32[]{:S(2)}) copy-start(f32[8,24,128]{2,1,0:T(8,128)S(1)} %collective-permute-done.1.refs_2_) | copy-start | bytes 294916
  15.2 24.3 %all-to-all-start = ((f32[64,8,128]{2,1,0:T(8,128)}), f32[64,8,128]{2,1,0:T(8,128)}, u32[]{:S(2)}, u32[]{:S(2)}) async-start(f32[64,8,128]{2,1,0:T(8,128)} %get-tuple-element.35), calls=%async_computation | async-start | bytes 524288 | tf_op jit(solution)/shard_map/all_to_all | solution.py:504
  39.5 9.0 %copy-start = (bf16[480,256]{1,0:T(8,128)(2,1)S(1)}, bf16[480,256]{1,0:T(8,128)(2,1)}, u32[]{:S(2)}) copy-start(bf16[480,256]{1,0:T(8,128)(2,1)} %get-tuple-element.33.refs_1_) | copy-start | bytes 737284
  44.8 9.4 %collective-permute-start.4 = (f32[80,128]{1,0:T(8,128)S(1)}, f32[80,128]{1,0:T(8,128)S(1)}, u32[]{:S(2)}, u32[]{:S(2)}) collective-permute-start(f32[80,128]{1,0:T(8,128)S(1)} %get-tuple-element.39.refs_0_), channel_id=1, source_target_pairs={{0,3},{1,0},{2,1},{3,2},{4,7},{5,4},{6,5},{7,6},{8,11},{9,8},{10,9... | collective-permute-start | bytes 122888 | tf_op jit(solution)/shard_map/ppermute | solution.py:544
  47.4 6.9 %collective-permute-start.3 = (f32[80,128]{1,0:T(8,128)S(1)}, f32[80,128]{1,0:T(8,128)S(1)}, u32[]{:S(2)}, u32[]{:S(2)}) collective-permute-start(f32[80,128]{1,0:T(8,128)S(1)} %get-tuple-element.39.refs_0_), channel_id=1, source_target_pairs={{0,2},{1,3},{2,0},{3,1},{4,6},{5,7},{6,4},{7,5},{8,10},{9,11},{10,... | collective-permute-start | bytes 122888 | tf_op jit(solution)/shard_map/ppermute | solution.py:544
  47.9 6.4 %collective-permute-start.2 = (f32[80,128]{1,0:T(8,128)S(1)}, f32[80,128]{1,0:T(8,128)S(1)}, u32[]{:S(2)}, u32[]{:S(2)}) collective-permute-start(f32[80,128]{1,0:T(8,128)S(1)} %get-tuple-element.39.refs_0_), channel_id=1, source_target_pairs={{0,1},{1,2},{2,3},{3,0},{4,5},{5,6},{6,7},{7,4},{8,9},{9,10},{10,1... | collective-permute-start | bytes 122888 | tf_op jit(solution)/shard_map/ppermute | solution.py:544
  57.5 17.2 %all-to-all-start.1 = ((f32[64,2,128]{2,1,0:T(2,128)}), f32[64,2,128]{2,1,0:T(2,128)S(1)}, u32[]{:S(2)}, u32[]{:S(2)}) async-start(f32[64,2,128]{2,1,0:T(2,128)} %get-tuple-element.44), calls=%async_computation.1 | async-start | bytes 131072 | tf_op jit(solution)/shard_map/all_to_all | solution.py:566

commit v6 on v5

--- a/solution.py
+++ b/solution.py
@@ -75,13 +75,12 @@
 
 
 ROLL = 6
-KCOPIES = 30
 NB = 512
 HALF = PTS // 2
 
 
 def put_parts(ref, source, x_ref, target):
-    for kp in range(KCOPIES):
+    for kp in range(ND):
         v = ref[:, (kp + ND - ROLL) % ND, source]
         p0 = v.astype(BF).astype(F32)
         x_ref[kp * 16 : kp * 16 + 16, target] = jnp.concatenate([p0, v - p0], axis=0).astype(BF)
@@ -123,8 +122,13 @@
         copy.wait()
 
 
-def rim_kernel(list_hbm, spec_hbm, before_hbm, after_hbm, spec_ref, list_ref, before_ref, after_ref, sems):
-    wait_copies(start_copies(((list_hbm, list_ref), (spec_hbm, spec_ref)), sems))
+def rim_kernel(
+    list_hbm, spec_hbm, near_hbm, slot_hbm, weight_hbm, before_hbm, after_hbm, spec_ref,
+    near_ref, slot_ref, weight_ref, list_ref, before_ref, after_ref, sems,
+):
+    pairs = ((list_hbm, list_ref), (spec_hbm, spec_ref))
+    first = start_copies(pairs + ((near_hbm, near_ref), (slot_hbm, slot_ref), (weight_hbm, weight_ref)), sems)
+    wait_copies(first[:2])
     rims = []
     for side, rim_ref in ((0, before_ref), (1, after_ref)):
         index = jnp.broadcast_to(list_ref[side : side + 1, :], (8, 128))
@@ -142,7 +146,9 @@
         return carry
 
     lax.fori_loop(0, GS, step, 0)
-    wait_copies(start_copies(((before_ref, before_hbm), (after_ref, after_hbm)), sems))
+    last = start_copies(((before_ref, before_hbm), (after_ref, after_hbm)), sems)
+    wait_copies(first[2:])
+    wait_copies(last)
 
 
 def outgoing_kernel(rows_hbm, forcing_hbm, out_hbm, rows_ref, forcing_ref, out_ref, sems, out_sems):
@@ -163,7 +169,7 @@
         pltpu.make_async_copy(out_ref.at[d], out_hbm.at[d], out_sems.at[q]).start()
         return carry
 
-    lax.fori_loop(0, TILES // 8, step, 0)
+    lax.fori_loop(0, TILES // 8, step, 0, unroll=2)
     for q in range(TILES // 8):
         d = pl.ds(q * 8, 8)
         pltpu.make_async_copy(out_ref.at[d], out_hbm.at[d], out_sems.at[q]).wait()
@@ -173,19 +179,20 @@
     slots = lax.broadcasted_iota(I32, (CAP, width), 0)
     total = None
     for j in range(4):
-        index = slot_ref[j : j + 1, cols] & (CAP - 1)
-        term = jnp.where(slots == index, weight_ref[j : j + 1, cols], 0.0)
+        place = slot_ref[j : j + 1, cols]
+        term = jnp.where(slots == (place & (CAP - 1)), weight_ref[j : j + 1, cols], 0.0)
         total = term if j == 0 else total + term
-    return total, slot_ref[0:1, cols] >> 8
+    return total, place >> 8
 
 
 WB = 256
 
 
 def wind_kernel(
-    arrived_hbm, slot_hbm, weight_hbm, spec_ref, wind_ref, mom_ref, left_ref, arrived_ref, slot_ref, weight_ref, sems
+    x_in_ref, arrived_ref, spec_hbm, low_ref, high_ref, slot_ref, weight_ref, x_ref, wind_ref, mom_ref,
+    left_ref, spec_ref, sems,
 ):
-    copies = start_copies(((arrived_hbm, arrived_ref), (slot_hbm, slot_ref), (weight_hbm, weight_ref)), sems)
+    copies = start_copies(((spec_hbm, spec_ref),), sems)
     up, down_scale = group_scale()
     inv_c = [w / G_ACC * up for w in OMEGA]
     inv_omega = [1.0 / w * down_scale for w in OMEGA]
@@ -193,12 +200,15 @@
     omega_c = [w * w / G_ACC * (up * up) for w in OMEGA]
     cos_tiles = [jnp.concatenate([t] * (WB // 128), axis=1) for t in direction_tiles(COS)]
     sin_tiles = [jnp.concatenate([t] * (WB // 128), axis=1) for t in direction_tiles(SIN)]
-    wait_copies(copies)
+    put_parts(low_ref, slice(0, RIM), x_ref, slice(0, RIM))
+    put_parts(high_ref, slice(0, RIM), x_ref, slice(EXT - RIM, EXT))
     for i in range(4):
         for half in range(2):
             p0, p1, p2 = parts3(arrived_ref[:, 2 * i + half, :])
             for n, part in enumerate((p0, p1, p2, p0, p1, p0)):
                 left_ref[i * 64 : i * 64 + 64, n * 256 + half * 128 : n * 256 + half * 128 + 128] = part
+
+    wait_copies(copies)
 
     def block(c, carry):
         cols = pl.ds(pl.multiple_of(c * WB, WB), WB)
@@ -244,9 +254,9 @@
 
 
 def field_kernel(
-    m0_ref, m1_ref, m2_ref, m3_ref, wind_ref, slot_hbm, weight_hbm, diss_ref, sums_ref, own_ref, slot_ref, weight_ref, sems
+    m0_ref, m1_ref, m2_ref, m3_ref, wind_ref, slot_ref, weight_ref, diss_ref, sums_hbm,
+    own_ref, sums_ref, sems,
 ):
-    copies = start_copies(((slot_hbm, slot_ref), (weight_hbm, weight_ref)), sems)
     moments = m0_ref[...] + m1_ref[...] + m2_ref[...] + m3_ref[...]
     total, inv_sigma, inv_root, stress_e, stress_n = (moments[16 * n : 16 * n + 16] for n in range(5))
     east, north, density, speed, friction = (wind_ref[16 * n : 16 * n + 16, :] for n in range(5))
@@ -265,7 +275,6 @@
     f = lax.axis_index("freq")
     own_ref[...] = jnp.where(f == 0, east_ratio, jnp.where(f == 1, north_ratio, jnp.where(f == 2, charnock, height)))
 
-    wait_copies(copies)
 
     def block(c, acc):
         cols = pl.ds(pl.multiple_of(c * WB, WB), WB)
@@ -281,11 +290,10 @@
     acc = lax.fori_loop(0, PTS // WB, block, jnp.zeros((TILES, CAP), F32), unroll=8)
     for half in range(2):
         sums_ref[:, half, :] = acc[:, half * 128 : half * 128 + 128]
-
-
-def band_kernel(arrived_ref, rows_hbm, out_ref, rows_ref, sems):
-    wait_copies(start_copies(((rows_hbm, rows_ref),), sems))
-
+    wait_copies(start_copies(((sums_ref, sums_hbm),), sems))
+
+
+def band_kernel(arrived_ref, rows_ref, out_ref):
     def eight_tiles(q, acc):
         ones, values = [], []
         for t in range(8):
@@ -306,74 +314,55 @@
     out_ref[...] = jnp.transpose(acc[:, :16] + acc[:, 16:])
 
 
-def move_kernel(half, spec_ref, low_ref, high_ref, near_hbm, *refs):
+def operand_kernel(spec_ref, x_ref):
+    def put_block(h, carry):
+        cols = pl.ds(pl.multiple_of(h * 128, 128), 128)
+        put_parts(spec_ref, cols, x_ref, pl.ds(pl.multiple_of(h * 128 + RIM, 128), 128))
+        return carry
+
+    lax.fori_loop(0, PTS // 128, put_block, 0)
+
+
+def move_kernel(half, near_ref, x_ref, out_ref):
     start = half * HALF
-    if half == 0:
-        out_hbm, rim_hbm, x_ref, near_ref, rim_ref, out_ref, sems, low_v, high_v, rim_sems = refs
-        copies = start_copies(((near_hbm, near_ref),), sems)
-        rim_loads = start_copies(((low_ref, low_v), (high_ref, high_v)), rim_sems)
-
-        def put_block(h, carry):
-            cols = pl.ds(pl.multiple_of(h * 128, 128), 128)
-            put_parts(spec_ref, cols, x_ref, cols)
-            return carry
-
-        lax.fori_loop(0, PTS // 128, put_block, 0)
-        wait_copies(rim_loads)
-        put_parts(low_v, slice(0, RIM), rim_ref, slice(0, RIM))
-        put_parts(high_v, slice(0, RIM), rim_ref, slice(RIM, 2 * RIM))
-        stores = start_copies(((rim_ref, rim_hbm),), sems, 1)
-    else:
-        x_ref = high_ref
-        out_hbm, near_ref, rim_ref, out_ref, sems = refs
-        copies = start_copies(((near_hbm, near_ref), (low_ref, rim_ref)), sems)
-        stores = []
-    wait_copies(copies)
     scale = group_scale()[1]
     courant = jnp.concatenate([by_sublane(COURANT) * scale] * (NB // 128), axis=1)
 
-    def hot(rows, index):
-        match = lax.broadcasted_iota(jnp.int16, (rows, NB), 0) == index
+    def hot(index):
+        match = lax.broadcasted_iota(jnp.int16, (EXT, NB), 0) == index.astype(jnp.int16)
         return jnp.where(match, jnp.ones((), BF), jnp.zeros((), BF))
 
     def block(c, carry):
         outs = pl.ds(pl.multiple_of(c * NB, NB), NB)
         cols = pl.ds(pl.multiple_of(start + c * NB, NB), NB)
+        own = pl.ds(pl.multiple_of(start + c * NB + RIM, RIM), NB)
         got = []
         for n, first in enumerate((0, 12, 6, 18)):
             index = near_ref[n : n + 1, cols]
-            rim_index = jnp.where(index < RIM, index, jnp.where(index < RIM + PTS, 2 * RIM, index - PTS))
-            rows = slice(first * 16, first * 16 + 192)
-            own = jnp.dot(x_ref[rows, :], hot(PTS, (index - RIM).astype(jnp.int16)), preferred_element_type=F32)
-            rim = jnp.dot(rim_ref[rows, :], hot(2 * RIM, rim_index.astype(jnp.int16)), preferred_element_type=F32)
-            got.append(own + rim)
+            if first + 12 <= ND:
+                left = x_ref[first * 16 : first * 16 + 192, :]
+            else:
+                left = jnp.concatenate([x_ref[first * 16 :, :], x_ref[: (first - 12) * 16, :]], axis=0)
+            got.append(jnp.dot(left, hot(index), preferred_element_type=F32))
         for k in range(ND):
-            a = (k + ROLL) % ND
-            x_of = got[0] if a < 12 else got[1]
-            a = a % 12
+            kp = (k + ROLL) % ND
+            x_of = got[0] if kp < 12 else got[1]
+            a = kp % 12
             y_of = got[2] if k < 12 else got[3]
             b = k % 12
             from_x = x_of[a * 16 : a * 16 + 8] + x_of[a * 16 + 8 : a * 16 + 16]
             from_y = y_of[b * 16 : b * 16 + 8] + y_of[b * 16 + 8 : b * 16 + 16]
-            spec = spec_ref[:, k, cols]
+            both = x_ref[kp * 16 : kp * 16 + 16, own].astype(F32)
+            spec = both[:8] + both[8:]
             out_ref[:, k, outs] = (
                 spec - (courant * abs(COS[k])) * (spec - from_x) - (courant * abs(SIN[k])) * (spec - from_y)
             )
-        pltpu.make_async_copy(out_ref.at[:, :, outs], out_hbm.at[:, :, outs], sems.at[2 + c]).start()
         return carry
 
     lax.fori_loop(0, HALF // NB, block, 0)
-    for c in range(HALF // NB):
-        outs = pl.ds(c * NB, NB)
-        pltpu.make_async_copy(out_ref.at[:, :, outs], out_hbm.at[:, :, outs], sems.at[2 + c]).wait()
-    wait_copies(stores)
-
-
-def source_kernel(moved0_hbm, moved1_hbm, wind_ref, out_hbm, push_ref, new_ref, moved0_ref, moved1_ref, loads, stores):
-    pairs = []
-    for i in range(GS):
-        pairs += [(moved0_hbm.at[i], moved0_ref.at[i]), (moved1_hbm.at[i], moved1_ref.at[i])]
-    copies = start_copies(pairs, loads)
+
+
+def source_kernel(moved0_ref, moved1_ref, wind_ref, out_hbm, push_ref, new_ref, stores):
     up = group_scale()[0]
     cos_tiles, sin_tiles = direction_tiles(COS), direction_tiles(SIN)
 
@@ -393,7 +382,7 @@
     lax.fori_loop(0, PTS // 128, prepare, 0)
     for i in range(GS):
         inv_c, omega, wavenum = OMEGA[i] / G_ACC * up, OMEGA[i] * up, OMEGA[i] ** 2 / G_ACC * (up * up)
-        wait_copies(copies[2 * i : 2 * i + 2])
+
         for half, moved_ref in ((0, moved0_ref), (1, moved1_ref)):
 
             def block(c, carry):
@@ -433,7 +422,7 @@
     return pltpu.with_memory_space_constraint(x, pltpu.HBM)
 
 
-def call(body, name, out, specs, scratch=(), mib=24, microseconds=1.0, out_specs=None, behind=False, mark=False):
+def call(body, name, out, specs, scratch=(), mib=24, microseconds=1.0, out_specs=None, behind=False, mark=False, aliases={}):
     out = list(out)
     out_specs = [VMEM] * len(out) if out_specs is None else list(out_specs)
     specs = [*specs, VMEM] if behind else specs
@@ -457,141 +446,124 @@
         out_specs=out_specs,
         scratch_shapes=list(scratch),
         name=name,
+        input_output_aliases=aliases,
         cost_estimate=cost,
-        compiler_params=pltpu.CompilerParams(vmem_limit_bytes=mib * 2**20),
+        compiler_params=pltpu.CompilerParams(vmem_limit_bytes=int(mib * 2**20)),
     )
 
 
 def on_device(spectrum, forcing, send_rows, point_slot, remap_weight, neighbours, halo_send):
     dma = pltpu.SemaphoreType.DMA
-    to_before, to_after, spec, mark = call(
-        rim_kernel,
-        "rims",
-        [distant(GS, ND, RIM), distant(GS, ND, RIM), resident(GS, ND, PTS)],
+    outgoing, rows, mark = call(
+        outgoing_kernel,
+        "outgoing",
+        [distant(TILES, 8, 128), resident(TILES, CAP, dtype=I32)],
         [HBM] * 2,
         [
-            pltpu.VMEM((2, RIM), I32),
-            pltpu.VMEM((GS, ND, RIM), F32),
-            pltpu.VMEM((GS, ND, RIM), F32),
-            dma((2,)),
-        ],
-        microseconds=3.0,
-        out_specs=[HBM, HBM, VMEM],
-        mark=True,
-    )(in_hbm(halo_send.reshape(2, RIM)), in_hbm(spectrum))
-    up = [(d, d + 1) for d in range(TILES - 1)]
-    low_rim = lax.ppermute(to_after, "tile", up)
-    high_rim = lax.ppermute(to_before, "tile", [(b, a) for a, b in up])
-
-    outgoing, mark = call(
-        outgoing_kernel,
-        "outgoing",
-        [distant(TILES, 8, 128)],
-        [HBM] * 2,
-        [
-            pltpu.VMEM((TILES, CAP), I32),
             pltpu.VMEM((4, PTS), F32),
             pltpu.VMEM((TILES, 8, 128), F32),
             dma((2,)),
             dma((TILES // 8,)),
         ],
         microseconds=3.0,
-        out_specs=[HBM],
+        out_specs=[HBM, VMEM],
+        mark=True,
+    )(in_hbm(send_rows), in_hbm(forcing))
+    arrived = lax.all_to_all(outgoing, "tile", split_axis=0, concat_axis=0, tiled=True)
+
+    to_before, to_after, spec, near, slot, weight, mark = call(
+        rim_kernel,
+        "rims",
+        [distant(GS, ND, RIM), distant(GS, ND, RIM), resident(GS, ND, PTS)]
+        + [resident(4, PTS, dtype=I32), resident(4, PTS, dtype=I32), resident(4, PTS)],
+        [HBM] * 5,
+        [
+            pltpu.VMEM((2, RIM), I32),
+            pltpu.VMEM((GS, ND, RIM), F32),
+            pltpu.VMEM((GS, ND, RIM), F32),
+            dma((5,)),
+        ],
+        microseconds=3.0,
+        out_specs=[HBM, HBM] + [VMEM] * 4,
         behind=True,
         mark=True,
-    )(in_hbm(send_rows), in_hbm(forcing), mark)
-    outgoing, low_rim, high_rim = lax.optimization_barrier((outgoing, low_rim, high_rim))
-    arrived = lax.all_to_all(outgoing, "tile", split_axis=0, concat_axis=0, tiled=True)
-
-    blocks = HALF // NB
-    scratch = [
-        pltpu.VMEM((4, PTS), I32),
-        pltpu.VMEM((KCOPIES * 16, 2 * RIM), BF),
-        pltpu.VMEM((GS, ND, HALF), F32),
-        dma((2 + blocks,)),
-    ]
-    moved0, rims, operand, mark = call(
-        functools.partial(move_kernel, 0),
-        "move0",
-        [
-            distant(GS, ND, HALF),
-            distant(KCOPIES * 16, 2 * RIM, dtype=BF),
-            resident(KCOPIES * 16, PTS, dtype=BF),
-        ],
-        [VMEM] + [HBM] * 3,
-        scratch + [pltpu.VMEM((GS, ND, RIM), F32), pltpu.VMEM((GS, ND, RIM), F32), dma((2,))],
-        microseconds=7.5,
-        out_specs=[HBM, HBM, VMEM],
+    )(*map(in_hbm, (halo_send.reshape(2, RIM), spectrum, neighbours, point_slot, remap_weight)), mark)
+    up = [(d, d + 1) for d in range(TILES - 1)]
+    low_rim = lax.ppermute(to_after, "tile", up)
+    high_rim = lax.ppermute(to_before, "tile", [(b, a) for a, b in up])
+    operand, mark = call(
+        operand_kernel,
+        "operand",
+        [resident(ND * 16, EXT, dtype=BF)],
+        [VMEM],
+        microseconds=3.0,
         behind=True,
         mark=True,
-    )(spec, in_hbm(low_rim), in_hbm(high_rim), in_hbm(neighbours), mark)
-    wind, moments, mark = call(
+    )(spec, mark)
+
+    operand, wind, moments, mark = call(
         wind_kernel,
         "wind",
-        [array(80, 128), array(80, 128)],
-        [HBM, HBM, HBM, VMEM],
-        [
-            pltpu.VMEM((256, 6 * 256), BF),
-            pltpu.VMEM((TILES, 8, 128), F32),
-            pltpu.VMEM((4, PTS), I32),
-            pltpu.VMEM((4, PTS), F32),
-            dma((3,)),
-        ],
+        [resident(ND * 16, EXT, dtype=BF), array(80, 128), array(80, 128)],
+        [VMEM, VMEM, HBM] + [VMEM] * 4,
+        [pltpu.VMEM((256, 6 * 256), BF), pltpu.VMEM((GS, ND, PTS), F32), dma((1,))],
         microseconds=6.0,
         behind=True,
         mark=True,
-    )(in_hbm(arrived), in_hbm(point_slot), in_hbm(remap_weight), spec, mark)
+        aliases={0: 0},
+    )(operand, arrived, in_hbm(spectrum), low_rim, high_rim, slot, weight, mark)
     others = [lax.ppermute(moments, "freq", [(i, (i + n) % 4) for i in range(4)]) for n in (1, 2, 3)]
-    moved1, mark = call(
-        functools.partial(move_kernel, 1),
-        "move1",
-        [distant(GS, ND, HALF)],
-        [VMEM, HBM, VMEM, HBM],
-        scratch,
-        microseconds=5.0,
-        out_specs=[HBM],
+
+    def move(half, mark):
+        return call(
+            functools.partial(move_kernel, half),
+            f"move{half}",
+            [resident(GS, ND, HALF)],
+            [VMEM] * 2,
+            microseconds=5.5,
+            behind=True,
+            mark=True,
+        )(near, operand, mark)
+
+    moved0, mark = move(0, mark)
+    state, slot_sums, mark = call(
+        field_kernel,
+        "fields",
+        [resident(96, 128), distant(TILES, 2, 128)],
+        [VMEM] * 7,
+        [
+            pltpu.VMEM((16, 128), F32),
+            pltpu.VMEM((TILES, 2, 128), F32),
+            dma((1,)),
+        ],
+        microseconds=3.0,
+        out_specs=[VMEM, HBM],
         behind=True,
         mark=True,
-    )(spec, rims, operand, in_hbm(neighbours), mark)
-
-    state, slot_sums = call(
-        field_kernel,
-        "fields",
-        [resident(96, 128), array(TILES, 2, 128)],
-        [VMEM] * 5 + [HBM] * 2,
-        [pltpu.VMEM((16, 128), F32), pltpu.VMEM((4, PTS), I32), pltpu.VMEM((4, PTS), F32), dma((2,))],
-        microseconds=3.0,
-        behind=True,
-    )(moments, *others, wind, in_hbm(point_slot), in_hbm(remap_weight), mark)
+    )(moments, *others, wind, slot, weight, mark)
     arrived_sums = lax.all_to_all(slot_sums, "tile", split_axis=0, concat_axis=0, tiled=True)
 
+    moved1, mark = move(1, mark)
     new_spectrum, mark = call(
         source_kernel,
         "source",
         [array(GS, ND, PTS)],
-        [HBM, HBM, VMEM],
-        [
-            pltpu.VMEM((PTS // 128, 40, 128), F32),
-            pltpu.VMEM((GS, ND, PTS), F32),
-            pltpu.VMEM((GS, ND, HALF), F32),
-            pltpu.VMEM((GS, ND, HALF), F32),
-            dma((2 * GS,)),
-            dma((GS,)),
-        ],
+        [VMEM] * 3,
+        [pltpu.VMEM((PTS // 128, 40, 128), F32), pltpu.VMEM((GS, ND, PTS), F32), dma((GS,))],
         microseconds=3.0,
         out_specs=[HBM],
+        behind=True,
         mark=True,
-    )(in_hbm(moved0), in_hbm(moved1), state)
+    )(moved0, moved1, state, mark)
 
     (returned,) = call(
         band_kernel,
         "band",
         [array(16, 128)],
-        [VMEM, HBM],
-        [pltpu.VMEM((TILES, CAP), I32), dma((1,))],
+        [VMEM] * 2,
         microseconds=2.5,
         behind=True,
-    )(arrived_sums, in_hbm(send_rows), mark)
+    )(arrived_sums, rows, mark)
     return (new_spectrum, returned.reshape(1, PTS))
 
 

time: 78.2 us -> 67.9 us (0.87)
  Pallas kernels: 34.5 us -> 27.6 us
  waiting for transfers between devices: 11.9 us -> 6.59 us
  starting transfers between devices: 30.3 us -> 32.6 us
    pallas_call x7 -> x8, Pallas kernels: 31 us -> 24.1 us  [the longest x2 8.28 us: move(): call(functools.partial(move_kernel, half), f'move{half}', [resident(GS, N...]
    all_to_all x1, waiting for transfers between devices: 3.86 us -> 0.01 us  [on_device(): lax.all_to_all(outgoing, 'tile', split_axis=0, concat_axis=0, tiled=True)]
    all_to_all x1, waiting for transfers between devices: 7.09 us -> 3.88 us  [on_device(): lax.all_to_all(slot_sums, 'tile', split_axis=0, concat_axis=0, tiled=True)]
    all_to_all x1, starting transfers between devices: 7.36 us -> 10.3 us  [on_device(): lax.all_to_all(slot_sums, 'tile', split_axis=0, concat_axis=0, tiled=True)]
    ppermute x1, starting transfers between devices: 4.94 us -> 3.54 us  [on_device(): low_rim = lax.ppermute(to_after, 'tile', up)]
    ppermute x1, waiting for transfers between devices: 0.91 us -> 2.07 us  [on_device(): high_rim = lax.ppermute(to_before, 'tile', [(b, a) for a, b in up])]
    all_to_all x1, starting transfers between devices: 12.4 us -> 13.2 us  [on_device(): lax.all_to_all(outgoing, 'tile', split_axis=0, concat_axis=0, tiled=True)]
  transfers between devices with their start and end apart: 7 -> 7, of which waited for: 3 -> 3; matrix products, arithmetic and copies ran while one was open for 0% -> 0% of each run, Pallas kernels for 25% -> 23%
where the time goes in v6:
time: 67.9 us; the launch traced here: 67.6 us
  starting transfers between devices  32.6 us (48%)
  Pallas kernels  27.6 us (41%)
  waiting for transfers between devices  6.59 us (10%)
  between operations  0.75 us (1%)
    all_to_all x1, starting transfers between devices, on_device(): lax.all_to_all(outgoing, 'tile', split_axis=0, concat_axis=0, tiled=True)  13.2 us
    all_to_all x1, starting transfers between devices, on_device(): lax.all_to_all(slot_sums, 'tile', split_axis=0, concat_axis=0, tiled=True)  10.3 us
    pallas_call x2, Pallas kernels, move(): call(functools.partial(move_kernel, half), f'move{half}', [resident(GS, N...  8.28 us
    pallas_call x1, Pallas kernels, on_device(): call(wind_kernel, 'wind', [resident(ND * 16, EXT, dtype=BF), array(80, 12...  4.68 us
    all_to_all x1, waiting for transfers between devices, on_device(): lax.all_to_all(slot_sums, 'tile', split_axis=0, concat_axis=0, tiled=True)  3.88 us
    ppermute x3, starting transfers between devices, on_device(): lax.ppermute(moments, 'freq', [(i, (i + n) % 4) for i in range(4)])  3.69 us
    ppermute x1, starting transfers between devices, on_device(): low_rim = lax.ppermute(to_after, 'tile', up)  3.54 us
    pallas_call x1, Pallas kernels, on_device(): call(rim_kernel, 'rims', [distant(GS, ND, RIM), distant(GS, ND, RIM), res...  3.5 us
  transfers between devices with their start and end apart: 7, of which 3 were waited for; matrix products, arithmetic and copies ran while one was open for 0% of the time, Pallas kernels for 23%

profile of v6, /device:TPU:1, one launch (start us, length us, event | category | flops | bytes accessed | tf_op | source)
XLA Modules:
  0.0 67.6 jit_solution(12742225659455368642)
XLA Ops:
  0.6 3.0 %outgoing.1 = (f32[64,8,128]{2,1,0:T(8,128)}, s32[64,256]{1,0:T(8,128)S(1)}, f32[8,128]{1,0:T(8,128)S(1)}) custom-call(s32[64,256]{1,0:T(8,128)} %refs_0_.1, f32[4,2048]{1,0:T(4,128)} %refs_1_.2), custom_call_target="tpu_custom_call" | custom-call | bytes 9000000 | tf_op jit(solution)/shard_map/outgoing/pallas_call | solution.py:457
  3.6 13.2 %all-to-all-start = ((f32[64,8,128]{2,1,0:T(8,128)}), f32[64,8,128]{2,1,0:T(8,128)S(1)}, u32[]{:S(2)}, u32[]{:S(2)}) async-start(f32[64,8,128]{2,1,0:T(8,128)} %get-tuple-element.32), calls=%async_computation | async-start | bytes 524288 | tf_op jit(solution)/shard_map/all_to_all | solution.py:472
  16.8 3.5 %rims.1 = (f32[8,24,128]{2,1,0:T(8,128)}, f32[8,24,128]{2,1,0:T(8,128)}, f32[8,24,2048]{2,1,0:T(8,128)S(1)}, s32[4,2048]{1,0:T(4,128)S(1)}, s32[4,2048]{1,0:T(4,...) custom-call(s32[2,128]{1,0:T(2,128)} %bitcast.3, f32[8,24,2048]{2,1,0:T(8,128)} %refs_2_.3, s32[4,2048]{1,0:T(4,128)} %refs_2_.2, ...), custom_call_target="tpu_custom_call" | custom-call | bytes 9000000 | tf_op jit(solution)/shard_map/rims/pallas_call | solution.py:474
  20.3 3.5 %collective-permute-start = (f32[8,24,128]{2,1,0:T(8,128)}, f32[8,24,128]{2,1,0:T(8,128)S(1)}, u32[]{:S(2)}, u32[]{:S(2)}) collective-permute-start(f32[8,24,128]{2,1,0:T(8,128)} %get-tuple-element.33), channel_id=1, source_target_pairs={{0,4},{4,8},{8,12},{12,16},{16,20},{20,24},{24,28},{28,32},{32,36}... | collective-permute-start | bytes 294920 | tf_op jit(solution)/shard_map/ppermute | solution.py:492
  23.8 1.9 %collective-permute-start.1 = (f32[8,24,128]{2,1,0:T(8,128)}, f32[8,24,128]{2,1,0:T(8,128)S(1)}, u32[]{:S(2)}, u32[]{:S(2)}) collective-permute-start(f32[8,24,128]{2,1,0:T(8,128)} %get-tuple-element.34), channel_id=1, source_target_pairs={{4,0},{8,4},{12,8},{16,12},{20,16},{24,20},{28,24},{32,28},{36,32}... | collective-permute-start | bytes 294920 | tf_op jit(solution)/shard_map/ppermute | solution.py:493
  25.8 2.1 %operand.1 = (bf16[384,2304]{1,0:T(8,128)(2,1)S(1)}, f32[8,128]{1,0:T(8,128)S(1)}) custom-call(f32[8,24,2048]{2,1,0:T(8,128)S(1)} %get-tuple-element.29.refs_0_, f32[8,128]{1,0:T(8,128)S(1)} %get-tuple-element.30.refs_1_), custom_call_target="tpu_custom_call" | custom-call | bytes 9000000 | tf_op jit(solution)/shard_map/operand/pallas_call | solution.py:494
  27.9 0.0 collective-permute-done.refs_3_
  27.9 2.1 %collective-permute-done.1.refs_4_ = f32[8,24,128]{2,1,0:T(8,128)S(1)} collective-permute-done((f32[8,24,128]{2,1,0:T(8,128)}, f32[8,24,128]{2,1,0:T(8,128)S(1)}, u32[]{:S(2)}, u32[]{:S(2)}) %collective-permute-start.1) | collective-permute-done | bytes 98336 | tf_op jit(solution)/shard_map/ppermute | solution.py:493
  30.0 0.0 all-to-all-done.refs_1_
  30.0 4.7 %wind.1 = (bf16[384,2304]{1,0:T(8,128)(2,1)S(1)}, f32[80,128]{1,0:T(8,128)S(1)}, f32[80,128]{1,0:T(8,128)S(1)}, f32[8,128]{1,0:T(8,128)S(1)}) custom-call(bf16[384,2304]{1,0:T(8,128)(2,1)S(1)} %get-tuple-element.31.refs_0_, f32[64,8,128]{2,1,0:T(8,128)S(1)} %all-to-all-done.refs_1_, f32[8,24,2048]{2,1,0:T(8,128)} %refs_2_.3, ...), custom_call_target="tpu_custom_call", output_to_operand_aliasing={{0}: (0, {})} | custom-call | bytes 18000000 | tf_op jit(solution)/shard_map/wind/pallas_call | solution.py:504
  34.7 2.6 %collective-permute-start.4 = (f32[80,128]{1,0:T(8,128)S(1)}, f32[80,128]{1,0:T(8,128)S(1)}, u32[]{:S(2)}, u32[]{:S(2)}) collective-permute-start(f32[80,128]{1,0:T(8,128)S(1)} %get-tuple-element.41.refs_0_), channel_id=1, source_target_pairs={{0,3},{1,0},{2,1},{3,2},{4,7},{5,4},{6,5},{7,6},{8,11},{9,8},{10,9... | collective-permute-start | bytes 122888 | tf_op jit(solution)/shard_map/ppermute | solution.py:515
  37.2 0.5 collective-permute-start.3
  37.8 0.6 collective-permute-start.2
  38.4 4.1 %move0.1 = (f32[8,24,1024]{2,1,0:T(8,128)S(1)}, f32[8,128]{1,0:T(8,128)S(1)}) custom-call(s32[4,2048]{1,0:T(4,128)S(1)} %get-tuple-element.28.refs_0_, bf16[384,2304]{1,0:T(8,128)(2,1)S(1)} %get-tuple-element.38.refs_1_, f32[8,128]{1,0:T(8,128)S(1)} %get-tuple-element.39.refs_2_), custom_call_target="tpu_custom_call" | custom-call | bytes 16500000 | tf_op jit(solution)/shard_map/move0/pallas_call | solution.py:518
  42.5 0.0 collective-permute-done.4.refs_3_
  42.5 0.0 collective-permute-done.3.refs_2_
  42.5 0.6 collective-permute-done.2.refs_1_
  43.2 2.4 %fields.1 = (f32[96,128]{1,0:T(8,128)S(1)}, f32[64,2,128]{2,1,0:T(2,128)}, f32[8,128]{1,0:T(8,128)S(1)}) custom-call(f32[80,128]{1,0:T(8,128)S(1)} %get-tuple-element.41.refs_0_, f32[80,128]{1,0:T(8,128)S(1)} %collective-permute-done.2.refs_1_, f32[80,128]{1,0:T(8,128)S(1)} %collective-permute-done.3.refs_2_, f32[80,128]{1,0:T(8,128)S(1)} %collective-permute-done.4.refs_3_, ...), custom_call_target="tpu_custom_call" | custom-call | bytes 9000000 | tf_op jit(solution)/shard_map/fields/pallas_call | solution.py:529
  45.5 10.3 %all-to-all-start.1 = ((f32[64,2,128]{2,1,0:T(2,128)}), f32[64,2,128]{2,1,0:T(2,128)S(1)}, u32[]{:S(2)}, u32[]{:S(2)}) async-start(f32[64,2,128]{2,1,0:T(2,128)} %get-tuple-element.49), calls=%async_computation.1 | async-start | bytes 131072 | tf_op jit(solution)/shard_map/all_to_all | solution.py:544
  55.8 4.1 %move1.1 = (f32[8,24,1024]{2,1,0:T(8,128)S(1)}, f32[8,128]{1,0:T(8,128)S(1)}) custom-call(s32[4,2048]{1,0:T(4,128)S(1)} %get-tuple-element.28.refs_0_, bf16[384,2304]{1,0:T(8,128)(2,1)S(1)} %get-tuple-element.38.refs_1_, f32[8,128]{1,0:T(8,128)S(1)} %get-tuple-element.44.refs_2_), custom_call_target="tpu_custom_call" | custom-call | bytes 16500000 | tf_op jit(solution)/shard_map/move1/pallas_call | solution.py:518
  60.0 1.8 %source.1 = (f32[8,24,2048]{2,1,0:T(8,128)}, f32[8,128]{1,0:T(8,128)S(1)}) custom-call(f32[8,24,1024]{2,1,0:T(8,128)S(1)} %get-tuple-element.40.refs_0_, f32[8,24,1024]{2,1,0:T(8,128)S(1)} %get-tuple-element.45.refs_1_, f32[96,128]{1,0:T(8,128)S(1)} %get-tuple-element.46.refs_2_, f32[8,128]{1,0:T(8,128)S(1)} %get-tuple-element.47.refs_3_), custom_call_target="tpu_custom_call" | custom-call | bytes 9000000 | tf_op jit(solution)/shard_map/source/pallas_call | solution.py:547
  61.8 3.9 %all-to-all-done.1.refs_0_ = f32[64,2,128]{2,1,0:T(2,128)S(1)} async-done(((f32[64,2,128]{2,1,0:T(2,128)}), f32[64,2,128]{2,1,0:T(2,128)S(1)}, u32[]{:S(2)}, u32[]{:S(2)}) %all-to-all-start.1) | async-done | bytes 65568 | tf_op jit(solution)/shard_map/all_to_all | solution.py:544
  65.6 1.9 %band.1 = f32[16,128]{1,0:T(8,128)} custom-call(f32[64,2,128]{2,1,0:T(2,128)S(1)} %all-to-all-done.1.refs_0_, s32[64,256]{1,0:T(8,128)S(1)} %get-tuple-element.50.refs_1_, f32[8,128]{1,0:T(8,128)S(1)} %get-tuple-element.51.refs_2_), custom_call_target="tpu_custom_call" | custom-call | bytes 7500000 | tf_op jit(solution)/shard_map/band/pallas_call | solution.py:559
Async XLA Ops:
  3.6 26.4 %all-to-all-start = ((f32[64,8,128]{2,1,0:T(8,128)}), f32[64,8,128]{2,1,0:T(8,128)S(1)}, u32[]{:S(2)}, u32[]{:S(2)}) async-start(f32[64,8,128]{2,1,0:T(8,128)} %get-tuple-element.32), calls=%async_computation | async-start | bytes 524288 | tf_op jit(solution)/shard_map/all_to_all | solution.py:472
  20.3 7.6 %collective-permute-start = (f32[8,24,128]{2,1,0:T(8,128)}, f32[8,24,128]{2,1,0:T(8,128)S(1)}, u32[]{:S(2)}, u32[]{:S(2)}) collective-permute-start(f32[8,24,128]{2,1,0:T(8,128)} %get-tuple-element.33), channel_id=1, source_target_pairs={{0,4},{4,8},{8,12},{12,16},{16,20},{20,24},{24,28},{28,32},{32,36}... | collective-permute-start | bytes 294920 | tf_op jit(solution)/shard_map/ppermute | solution.py:492
  23.8 6.1 %collective-permute-start.1 = (f32[8,24,128]{2,1,0:T(8,128)}, f32[8,24,128]{2,1,0:T(8,128)S(1)}, u32[]{:S(2)}, u32[]{:S(2)}) collective-permute-start(f32[8,24,128]{2,1,0:T(8,128)} %get-tuple-element.34), channel_id=1, source_target_pairs={{4,0},{8,4},{12,8},{16,12},{20,16},{24,20},{28,24},{32,28},{36,32}... | collective-permute-start | bytes 294920 | tf_op jit(solution)/shard_map/ppermute | solution.py:493
  34.7 7.8 %collective-permute-start.4 = (f32[80,128]{1,0:T(8,128)S(1)}, f32[80,128]{1,0:T(8,128)S(1)}, u32[]{:S(2)}, u32[]{:S(2)}) collective-permute-start(f32[80,128]{1,0:T(8,128)S(1)} %get-tuple-element.41.refs_0_), channel_id=1, source_target_pairs={{0,3},{1,0},{2,1},{3,2},{4,7},{5,4},{6,5},{7,6},{8,11},{9,8},{10,9... | collective-permute-start | bytes 122888 | tf_op jit(solution)/shard_map/ppermute | solution.py:515
  37.2 5.3 %collective-permute-start.3 = (f32[80,128]{1,0:T(8,128)S(1)}, f32[80,128]{1,0:T(8,128)S(1)}, u32[]{:S(2)}, u32[]{:S(2)}) collective-permute-start(f32[80,128]{1,0:T(8,128)S(1)} %get-tuple-element.41.refs_0_), channel_id=1, source_target_pairs={{0,2},{1,3},{2,0},{3,1},{4,6},{5,7},{6,4},{7,5},{8,10},{9,11},{10,... | collective-permute-start | bytes 122888 | tf_op jit(solution)/shard_map/ppermute | solution.py:515
  37.8 5.4 %collective-permute-start.2 = (f32[80,128]{1,0:T(8,128)S(1)}, f32[80,128]{1,0:T(8,128)S(1)}, u32[]{:S(2)}, u32[]{:S(2)}) collective-permute-start(f32[80,128]{1,0:T(8,128)S(1)} %get-tuple-element.41.refs_0_), channel_id=1, source_target_pairs={{0,1},{1,2},{2,3},{3,0},{4,5},{5,6},{6,7},{7,4},{8,9},{9,10},{10,1... | collective-permute-start | bytes 122888 | tf_op jit(solution)/shard_map/ppermute | solution.py:515
  45.5 20.1 %all-to-all-start.1 = ((f32[64,2,128]{2,1,0:T(2,128)}), f32[64,2,128]{2,1,0:T(2,128)S(1)}, u32[]{:S(2)}, u32[]{:S(2)}) async-start(f32[64,2,128]{2,1,0:T(2,128)} %get-tuple-element.49), calls=%async_computation.1 | async-start | bytes 131072 | tf_op jit(solution)/shard_map/all_to_all | solution.py:544

commit v7 on v6

--- a/solution.py
+++ b/solution.py
@@ -76,7 +76,7 @@
 
 ROLL = 6
 NB = 512
-HALF = PTS // 2
+PARTS = ((0, 1024), (1024, PTS - 1024))
 
 
 def put_parts(ref, source, x_ref, target):
@@ -145,7 +145,7 @@
                 rim_ref[i, rows, :] = got
         return carry
 
-    lax.fori_loop(0, GS, step, 0)
+    lax.fori_loop(0, GS, step, 0, unroll=2)
     last = start_copies(((before_ref, before_hbm), (after_ref, after_hbm)), sems)
     wait_copies(first[2:])
     wait_copies(last)
@@ -169,37 +169,42 @@
         pltpu.make_async_copy(out_ref.at[d], out_hbm.at[d], out_sems.at[q]).start()
         return carry
 
-    lax.fori_loop(0, TILES // 8, step, 0, unroll=2)
+    lax.fori_loop(0, TILES // 8, step, 0, unroll=4)
     for q in range(TILES // 8):
         d = pl.ds(q * 8, 8)
         pltpu.make_async_copy(out_ref.at[d], out_hbm.at[d], out_sems.at[q]).wait()
 
 
-def weight_matrix(slot_ref, weight_ref, cols, width):
-    slots = lax.broadcasted_iota(I32, (CAP, width), 0)
-    total = None
-    for j in range(4):
-        place = slot_ref[j : j + 1, cols]
-        term = jnp.where(slots == (place & (CAP - 1)), weight_ref[j : j + 1, cols], 0.0)
-        total = term if j == 0 else total + term
-    return total, place >> 8
+def weight_parts(slot_ref, weight_ref, cols, width, count):
+    place = [slot_ref[j : j + 1, cols] for j in range(4)]
+    slot = [p & (CAP - 1) for p in place]
+    weight = [weight_ref[j : j + 1, cols] for j in range(4)]
+    for j in range(1, 4):
+        for i in range(j):
+            same = slot[j] == slot[i]
+            weight[i] = weight[i] + jnp.where(same, weight[j], 0.0)
+            weight[j] = jnp.where(same, 0.0, weight[j])
+    slots = lax.broadcasted_iota(jnp.int16, (CAP, width), 0)
+    total = [jnp.zeros((CAP, width), BF)] * count
+    for j in (3, 2, 1, 0):
+        match = slots == slot[j].astype(jnp.int16)
+        split = parts3(weight[j]) if count == 3 else parts2(weight[j])
+        total = [jnp.where(match, part, rest) for part, rest in zip(split, total)]
+    return total, place[0] >> 8
 
 
 WB = 256
 
 
 def wind_kernel(
-    x_in_ref, arrived_ref, spec_hbm, low_ref, high_ref, slot_ref, weight_ref, x_ref, wind_ref, mom_ref,
-    left_ref, spec_ref, sems,
+    x_in_ref, arrived_ref, low_ref, high_ref, slot_ref, weight_ref, x_ref, wind_ref, mom_ref, left_ref
 ):
-    copies = start_copies(((spec_hbm, spec_ref),), sems)
     up, down_scale = group_scale()
-    inv_c = [w / G_ACC * up for w in OMEGA]
-    inv_omega = [1.0 / w * down_scale for w in OMEGA]
-    inv_root = [math.sqrt(G_ACC) / w * down_scale for w in OMEGA]
-    omega_c = [w * w / G_ACC * (up * up) for w in OMEGA]
-    cos_tiles = [jnp.concatenate([t] * (WB // 128), axis=1) for t in direction_tiles(COS)]
-    sin_tiles = [jnp.concatenate([t] * (WB // 128), axis=1) for t in direction_tiles(SIN)]
+    wide = lambda values: jnp.concatenate([by_sublane(values)] * (WB // 128), axis=1)
+    inv_c = wide([w / G_ACC for w in OMEGA]) * up
+    inv_omega = wide([1.0 / w for w in OMEGA]) * down_scale
+    inv_root = wide([math.sqrt(G_ACC) / w for w in OMEGA]) * down_scale
+    omega_c = wide([w * w / G_ACC for w in OMEGA]) * (up * up)
     put_parts(low_ref, slice(0, RIM), x_ref, slice(0, RIM))
     put_parts(high_ref, slice(0, RIM), x_ref, slice(EXT - RIM, EXT))
     for i in range(4):
@@ -208,12 +213,10 @@
             for n, part in enumerate((p0, p1, p2, p0, p1, p0)):
                 left_ref[i * 64 : i * 64 + 64, n * 256 + half * 128 : n * 256 + half * 128 + 128] = part
 
-    wait_copies(copies)
-
     def block(c, carry):
         cols = pl.ds(pl.multiple_of(c * WB, WB), WB)
-        weights, band = weight_matrix(slot_ref, weight_ref, cols, WB)
-        w0, w1, w2 = parts3(weights)
+        own = pl.ds(pl.multiple_of(c * WB + RIM, RIM), WB)
+        (w0, w1, w2), band = weight_parts(slot_ref, weight_ref, cols, WB, 3)
         right = jnp.concatenate([w0, w0, w0, w1, w1, w2], axis=0)
         mixed = jnp.dot(left_ref[...], right, preferred_element_type=F32)
         mine = lax.broadcasted_iota(I32, (TILES, WB), 0) == band
@@ -225,23 +228,24 @@
         pull = 28.0 * friction
         share = 0.25 * (density / WATER_DENSITY)
         spread = lambda v: jnp.broadcast_to(v, (8, WB))
-        east8, north8, speed8, pull8 = spread(east), spread(north), spread(speed), spread(pull)
+        push_east, push_north = spread(pull * east / speed), spread(pull * north / speed)
         m0 = jnp.zeros((8, WB), F32)
-        ms, mk, sx, sy = m0, m0, m0, m0
-        for g in range(3):
-            cos8, sin8 = cos_tiles[g], sin_tiles[g]
-            push = pull8 * ((east8 * cos8 + north8 * sin8) / speed8)
-            stress = jnp.zeros((8, WB), F32)
-            for i in range(GS):
-                spec = spec_ref[i, 8 * g : 8 * g + 8, cols]
-                m0 = m0 + spec
-                ms = ms + spec * inv_omega[i]
-                mk = mk + spec * inv_root[i]
-                excess = jnp.maximum(push * inv_c[i] - 1.0, 0.0)
-                stress = stress + (excess * omega_c[i]) * spec
-            sx = sx + stress * cos8
-            sy = sy + stress * sin8
+        sx, sy = m0, m0
+
+        def energy(k):
+            kp = (k + ROLL) % ND
+            both = x_ref[kp * 16 : kp * 16 + 16, own].astype(F32)
+            return both[:8] + both[8:]
+
+        for k in range(ND // 2):
+            one, other = energy(k), energy(k + ND // 2)
+            m0 = m0 + (one + other)
+            push = (push_east * COS[k] + push_north * SIN[k]) * inv_c
+            stress = jnp.maximum(push - 1.0, 0.0) * one - jnp.maximum(-push - 1.0, 0.0) * other
+            sx = sx + stress * COS[k]
+            sy = sy + stress * SIN[k]
         down = lambda v: jnp.sum(v, axis=0, keepdims=True)
+        ms, mk, sx, sy = m0 * inv_omega, m0 * inv_root, sx * omega_c, sy * omega_c
         for n, row in enumerate((down(m0), down(ms), down(mk), down(sx) * share, down(sy) * share)):
             for half in range(WB // 128):
                 mom_ref[pl.ds(n * 16 + c * (WB // 128) + half, 1), :] = row[:, half * 128 : half * 128 + 128]
@@ -278,8 +282,7 @@
 
     def block(c, acc):
         cols = pl.ds(pl.multiple_of(c * WB, WB), WB)
-        weights, band = weight_matrix(slot_ref, weight_ref, cols, WB)
-        w0, w1 = parts2(weights)
+        (w0, w1), band = weight_parts(slot_ref, weight_ref, cols, WB, 2)
         field = jnp.concatenate([own_ref[pl.ds(c * (WB // 128) + half, 1), :] for half in range(WB // 128)], axis=1)
         spread = jnp.where(lax.broadcasted_iota(I32, (TILES, WB), 0) == band, field, 0.0)
         f0, f1 = parts2(spread)
@@ -320,11 +323,11 @@
         put_parts(spec_ref, cols, x_ref, pl.ds(pl.multiple_of(h * 128 + RIM, 128), 128))
         return carry
 
-    lax.fori_loop(0, PTS // 128, put_block, 0)
+    lax.fori_loop(0, PTS // 128, put_block, 0, unroll=2)
 
 
 def move_kernel(half, near_ref, x_ref, out_ref):
-    start = half * HALF
+    start, count = PARTS[half]
     scale = group_scale()[1]
     courant = jnp.concatenate([by_sublane(COURANT) * scale] * (NB // 128), axis=1)
 
@@ -359,7 +362,7 @@
             )
         return carry
 
-    lax.fori_loop(0, HALF // NB, block, 0)
+    lax.fori_loop(0, count // NB, block, 0)
 
 
 def source_kernel(moved0_ref, moved1_ref, wind_ref, out_hbm, push_ref, new_ref, stores):
@@ -383,10 +386,10 @@
     for i in range(GS):
         inv_c, omega, wavenum = OMEGA[i] / G_ACC * up, OMEGA[i] * up, OMEGA[i] ** 2 / G_ACC * (up * up)
 
-        for half, moved_ref in ((0, moved0_ref), (1, moved1_ref)):
+        for (start, count), moved_ref in zip(PARTS, (moved0_ref, moved1_ref)):
 
             def block(c, carry):
-                at = c + half * (HALF // 128)
+                at = c + start // 128
                 cols = pl.ds(pl.multiple_of(c * 128, 128), 128)
                 outs = pl.ds(pl.multiple_of(at * 128, 128), 128)
                 share, loss = push_ref[at, 24:32, :] * omega, push_ref[at, 32:40, :] * wavenum
@@ -396,7 +399,7 @@
                     new_ref[i, rows, outs] = moved_ref[i, rows, cols] * jnp.exp(share * excess - loss)
                 return carry
 
-            lax.fori_loop(0, HALF // 128, block, 0, unroll=4)
+            lax.fori_loop(0, count // 128, block, 0, unroll=4)
         pltpu.make_async_copy(new_ref.at[i], out_hbm.at[i], stores.at[i]).start()
     for i in range(GS):
         pltpu.make_async_copy(new_ref.at[i], out_hbm.at[i], stores.at[i]).wait()
@@ -505,20 +508,20 @@
         wind_kernel,
         "wind",
         [resident(ND * 16, EXT, dtype=BF), array(80, 128), array(80, 128)],
-        [VMEM, VMEM, HBM] + [VMEM] * 4,
-        [pltpu.VMEM((256, 6 * 256), BF), pltpu.VMEM((GS, ND, PTS), F32), dma((1,))],
+        [VMEM] * 6,
+        [pltpu.VMEM((256, 6 * 256), BF)],
         microseconds=6.0,
         behind=True,
         mark=True,
         aliases={0: 0},
-    )(operand, arrived, in_hbm(spectrum), low_rim, high_rim, slot, weight, mark)
+    )(operand, arrived, low_rim, high_rim, slot, weight, mark)
     others = [lax.ppermute(moments, "freq", [(i, (i + n) % 4) for i in range(4)]) for n in (1, 2, 3)]
 
     def move(half, mark):
         return call(
             functools.partial(move_kernel, half),
             f"move{half}",
-            [resident(GS, ND, HALF)],
+            [resident(GS, ND, PARTS[half][1])],
             [VMEM] * 2,
             microseconds=5.5,
             behind=True,

time: 67.9 us -> 66.6 us (0.981)
  Pallas kernels: 27.6 us -> 26.3 us
where the time goes in v7:
time: 66.6 us; the launch traced here: 66.3 us
  starting transfers between devices  32.6 us (49%)
  Pallas kernels  26.3 us (39%)
  waiting for transfers between devices  6.64 us (10%)
  between operations  0.75 us (1%)
    all_to_all x1, starting transfers between devices, on_device(): lax.all_to_all(outgoing, 'tile', split_axis=0, concat_axis=0, tiled=True)  13.2 us
    all_to_all x1, starting transfers between devices, on_device(): lax.all_to_all(slot_sums, 'tile', split_axis=0, concat_axis=0, tiled=True)  10.3 us
    pallas_call x2, Pallas kernels, move(): call(functools.partial(move_kernel, half), f'move{half}', [resident(GS, N...  8.28 us
    pallas_call x1, Pallas kernels, on_device(): call(wind_kernel, 'wind', [resident(ND * 16, EXT, dtype=BF), array(80, 12...  4.23 us
    all_to_all x1, waiting for transfers between devices, on_device(): lax.all_to_all(slot_sums, 'tile', split_axis=0, concat_axis=0, tiled=True)  3.88 us
    ppermute x3, starting transfers between devices, on_device(): lax.ppermute(moments, 'freq', [(i, (i + n) % 4) for i in range(4)])  3.68 us
    ppermute x1, starting transfers between devices, on_device(): low_rim = lax.ppermute(to_after, 'tile', up)  3.54 us
    pallas_call x1, Pallas kernels, on_device(): call(rim_kernel, 'rims', [distant(GS, ND, RIM), distant(GS, ND, RIM), res...  3.25 us
  transfers between devices with their start and end apart: 7, of which 3 were waited for; matrix products, arithmetic and copies ran while one was open for 0% of the time, Pallas kernels for 23%

profile of v7, /device:TPU:1, one launch (start us, length us, event | category | flops | bytes accessed | tf_op | source)
XLA Modules:
  0.0 66.3 jit_solution(17056736396222440651)
XLA Ops:
  0.6 2.8 %outgoing.1 = (f32[64,8,128]{2,1,0:T(8,128)}, s32[64,256]{1,0:T(8,128)S(1)}, f32[8,128]{1,0:T(8,128)S(1)}) custom-call(s32[64,256]{1,0:T(8,128)} %refs_0_.1, f32[4,2048]{1,0:T(4,128)} %refs_1_.2), custom_call_target="tpu_custom_call" | custom-call | bytes 9000000 | tf_op jit(solution)/shard_map/outgoing/pallas_call | solution.py:460
  3.5 13.2 %all-to-all-start = ((f32[64,8,128]{2,1,0:T(8,128)}), f32[64,8,128]{2,1,0:T(8,128)S(1)}, u32[]{:S(2)}, u32[]{:S(2)}) async-start(f32[64,8,128]{2,1,0:T(8,128)} %get-tuple-element.32), calls=%async_computation | async-start | bytes 524288 | tf_op jit(solution)/shard_map/all_to_all | solution.py:475
  16.6 3.3 %rims.1 = (f32[8,24,128]{2,1,0:T(8,128)}, f32[8,24,128]{2,1,0:T(8,128)}, f32[8,24,2048]{2,1,0:T(8,128)S(1)}, s32[4,2048]{1,0:T(4,128)S(1)}, s32[4,2048]{1,0:T(4,...) custom-call(s32[2,128]{1,0:T(2,128)} %bitcast.3, f32[8,24,2048]{2,1,0:T(8,128)} %refs_1_.3, s32[4,2048]{1,0:T(4,128)} %refs_2_.1, ...), custom_call_target="tpu_custom_call" | custom-call | bytes 9000000 | tf_op jit(solution)/shard_map/rims/pallas_call | solution.py:477
  19.9 3.5 %collective-permute-start = (f32[8,24,128]{2,1,0:T(8,128)}, f32[8,24,128]{2,1,0:T(8,128)S(1)}, u32[]{:S(2)}, u32[]{:S(2)}) collective-permute-start(f32[8,24,128]{2,1,0:T(8,128)} %get-tuple-element.33), channel_id=1, source_target_pairs={{0,4},{4,8},{8,12},{12,16},{16,20},{20,24},{24,28},{28,32},{32,36}... | collective-permute-start | bytes 294920 | tf_op jit(solution)/shard_map/ppermute | solution.py:495
  23.4 1.9 %collective-permute-start.1 = (f32[8,24,128]{2,1,0:T(8,128)}, f32[8,24,128]{2,1,0:T(8,128)S(1)}, u32[]{:S(2)}, u32[]{:S(2)}) collective-permute-start(f32[8,24,128]{2,1,0:T(8,128)} %get-tuple-element.34), channel_id=1, source_target_pairs={{4,0},{8,4},{12,8},{16,12},{20,16},{24,20},{28,24},{32,28},{36,32}... | collective-permute-start | bytes 294920 | tf_op jit(solution)/shard_map/ppermute | solution.py:496
  25.4 2.1 %operand.1 = (bf16[384,2304]{1,0:T(8,128)(2,1)S(1)}, f32[8,128]{1,0:T(8,128)S(1)}) custom-call(f32[8,24,2048]{2,1,0:T(8,128)S(1)} %get-tuple-element.29.refs_0_, f32[8,128]{1,0:T(8,128)S(1)} %get-tuple-element.30.refs_1_), custom_call_target="tpu_custom_call" | custom-call | bytes 9000000 | tf_op jit(solution)/shard_map/operand/pallas_call | solution.py:497
  27.5 0.0 collective-permute-done.refs_2_
  27.5 2.1 %collective-permute-done.1.refs_3_ = f32[8,24,128]{2,1,0:T(8,128)S(1)} collective-permute-done((f32[8,24,128]{2,1,0:T(8,128)}, f32[8,24,128]{2,1,0:T(8,128)S(1)}, u32[]{:S(2)}, u32[]{:S(2)}) %collective-permute-start.1) | collective-permute-done | bytes 98336 | tf_op jit(solution)/shard_map/ppermute | solution.py:496
  29.6 0.0 all-to-all-done.refs_1_
  29.6 4.2 %wind.1 = (bf16[384,2304]{1,0:T(8,128)(2,1)S(1)}, f32[80,128]{1,0:T(8,128)S(1)}, f32[80,128]{1,0:T(8,128)S(1)}, f32[8,128]{1,0:T(8,128)S(1)}) custom-call(bf16[384,2304]{1,0:T(8,128)(2,1)S(1)} %get-tuple-element.31.refs_0_, f32[64,8,128]{2,1,0:T(8,128)S(1)} %all-to-all-done.refs_1_, ...), custom_call_target="tpu_custom_call", output_to_operand_aliasing={{0}: (0, {})} | custom-call | bytes 18000000 | tf_op jit(solution)/shard_map/wind/pallas_call | solution.py:507
  33.8 2.6 %collective-permute-start.4 = (f32[80,128]{1,0:T(8,128)S(1)}, f32[80,128]{1,0:T(8,128)S(1)}, u32[]{:S(2)}, u32[]{:S(2)}) collective-permute-start(f32[80,128]{1,0:T(8,128)S(1)} %get-tuple-element.41.refs_0_), channel_id=1, source_target_pairs={{0,3},{1,0},{2,1},{3,2},{4,7},{5,4},{6,5},{7,6},{8,11},{9,8},{10,9... | collective-permute-start | bytes 122888 | tf_op jit(solution)/shard_map/ppermute | solution.py:518
  36.4 0.5 collective-permute-start.3
  36.9 0.6 collective-permute-start.2
  37.5 4.1 %move0.1 = (f32[8,24,1024]{2,1,0:T(8,128)S(1)}, f32[8,128]{1,0:T(8,128)S(1)}) custom-call(s32[4,2048]{1,0:T(4,128)S(1)} %get-tuple-element.28.refs_0_, bf16[384,2304]{1,0:T(8,128)(2,1)S(1)} %get-tuple-element.38.refs_1_, f32[8,128]{1,0:T(8,128)S(1)} %get-tuple-element.39.refs_2_), custom_call_target="tpu_custom_call" | custom-call | bytes 16500000 | tf_op jit(solution)/shard_map/move0/pallas_call | solution.py:521
  41.7 0.0 collective-permute-done.4.refs_3_
  41.7 0.0 collective-permute-done.3.refs_2_
  41.7 0.6 collective-permute-done.2.refs_1_
  42.3 1.9 %fields.1 = (f32[96,128]{1,0:T(8,128)S(1)}, f32[64,2,128]{2,1,0:T(2,128)}, f32[8,128]{1,0:T(8,128)S(1)}) custom-call(f32[80,128]{1,0:T(8,128)S(1)} %get-tuple-element.41.refs_0_, f32[80,128]{1,0:T(8,128)S(1)} %collective-permute-done.2.refs_1_, f32[80,128]{1,0:T(8,128)S(1)} %collective-permute-done.3.refs_2_, f32[80,128]{1,0:T(8,128)S(1)} %collective-permute-done.4.refs_3_, ...), custom_call_target="tpu_custom_call" | custom-call | bytes 9000000 | tf_op jit(solution)/shard_map/fields/pallas_call | solution.py:532
  44.2 10.3 %all-to-all-start.1 = ((f32[64,2,128]{2,1,0:T(2,128)}), f32[64,2,128]{2,1,0:T(2,128)S(1)}, u32[]{:S(2)}, u32[]{:S(2)}) async-start(f32[64,2,128]{2,1,0:T(2,128)} %get-tuple-element.49), calls=%async_computation.1 | async-start | bytes 131072 | tf_op jit(solution)/shard_map/all_to_all | solution.py:547
  54.5 4.1 %move1.1 = (f32[8,24,1024]{2,1,0:T(8,128)S(1)}, f32[8,128]{1,0:T(8,128)S(1)}) custom-call(s32[4,2048]{1,0:T(4,128)S(1)} %get-tuple-element.28.refs_0_, bf16[384,2304]{1,0:T(8,128)(2,1)S(1)} %get-tuple-element.38.refs_1_, f32[8,128]{1,0:T(8,128)S(1)} %get-tuple-element.44.refs_2_), custom_call_target="tpu_custom_call" | custom-call | bytes 16500000 | tf_op jit(solution)/shard_map/move1/pallas_call | solution.py:521
  58.7 1.8 %source.1 = (f32[8,24,2048]{2,1,0:T(8,128)}, f32[8,128]{1,0:T(8,128)S(1)}) custom-call(f32[8,24,1024]{2,1,0:T(8,128)S(1)} %get-tuple-element.40.refs_0_, f32[8,24,1024]{2,1,0:T(8,128)S(1)} %get-tuple-element.45.refs_1_, f32[96,128]{1,0:T(8,128)S(1)} %get-tuple-element.46.refs_2_, f32[8,128]{1,0:T(8,128)S(1)} %get-tuple-element.47.refs_3_), custom_call_target="tpu_custom_call" | custom-call | bytes 9000000 | tf_op jit(solution)/shard_map/source/pallas_call | solution.py:550
  60.4 3.9 %all-to-all-done.1.refs_0_ = f32[64,2,128]{2,1,0:T(2,128)S(1)} async-done(((f32[64,2,128]{2,1,0:T(2,128)}), f32[64,2,128]{2,1,0:T(2,128)S(1)}, u32[]{:S(2)}, u32[]{:S(2)}) %all-to-all-start.1) | async-done | bytes 65568 | tf_op jit(solution)/shard_map/all_to_all | solution.py:547
  64.3 1.9 %band.1 = f32[16,128]{1,0:T(8,128)} custom-call(f32[64,2,128]{2,1,0:T(2,128)S(1)} %all-to-all-done.1.refs_0_, s32[64,256]{1,0:T(8,128)S(1)} %get-tuple-element.50.refs_1_, f32[8,128]{1,0:T(8,128)S(1)} %get-tuple-element.51.refs_2_), custom_call_target="tpu_custom_call" | custom-call | bytes 7500000 | tf_op jit(solution)/shard_map/band/pallas_call | solution.py:562
Async XLA Ops:
  3.5 26.1 %all-to-all-start = ((f32[64,8,128]{2,1,0:T(8,128)}), f32[64,8,128]{2,1,0:T(8,128)S(1)}, u32[]{:S(2)}, u32[]{:S(2)}) async-start(f32[64,8,128]{2,1,0:T(8,128)} %get-tuple-element.32), calls=%async_computation | async-start | bytes 524288 | tf_op jit(solution)/shard_map/all_to_all | solution.py:475
  19.9 7.6 %collective-permute-start = (f32[8,24,128]{2,1,0:T(8,128)}, f32[8,24,128]{2,1,0:T(8,128)S(1)}, u32[]{:S(2)}, u32[]{:S(2)}) collective-permute-start(f32[8,24,128]{2,1,0:T(8,128)} %get-tuple-element.33), channel_id=1, source_target_pairs={{0,4},{4,8},{8,12},{12,16},{16,20},{20,24},{24,28},{28,32},{32,36}... | collective-permute-start | bytes 294920 | tf_op jit(solution)/shard_map/ppermute | solution.py:495
  23.4 6.1 %collective-permute-start.1 = (f32[8,24,128]{2,1,0:T(8,128)}, f32[8,24,128]{2,1,0:T(8,128)S(1)}, u32[]{:S(2)}, u32[]{:S(2)}) collective-permute-start(f32[8,24,128]{2,1,0:T(8,128)} %get-tuple-element.34), channel_id=1, source_target_pairs={{4,0},{8,4},{12,8},{16,12},{20,16},{24,20},{28,24},{32,28},{36,32}... | collective-permute-start | bytes 294920 | tf_op jit(solution)/shard_map/ppermute | solution.py:496
  33.8 7.8 %collective-permute-start.4 = (f32[80,128]{1,0:T(8,128)S(1)}, f32[80,128]{1,0:T(8,128)S(1)}, u32[]{:S(2)}, u32[]{:S(2)}) collective-permute-start(f32[80,128]{1,0:T(8,128)S(1)} %get-tuple-element.41.refs_0_), channel_id=1, source_target_pairs={{0,3},{1,0},{2,1},{3,2},{4,7},{5,4},{6,5},{7,6},{8,11},{9,8},{10,9... | collective-permute-start | bytes 122888 | tf_op jit(solution)/shard_map/ppermute | solution.py:518
  36.4 5.3 %collective-permute-start.3 = (f32[80,128]{1,0:T(8,128)S(1)}, f32[80,128]{1,0:T(8,128)S(1)}, u32[]{:S(2)}, u32[]{:S(2)}) collective-permute-start(f32[80,128]{1,0:T(8,128)S(1)} %get-tuple-element.41.refs_0_), channel_id=1, source_target_pairs={{0,2},{1,3},{2,0},{3,1},{4,6},{5,7},{6,4},{7,5},{8,10},{9,11},{10,... | collective-permute-start | bytes 122888 | tf_op jit(solution)/shard_map/ppermute | solution.py:518
  36.9 5.4 %collective-permute-start.2 = (f32[80,128]{1,0:T(8,128)S(1)}, f32[80,128]{1,0:T(8,128)S(1)}, u32[]{:S(2)}, u32[]{:S(2)}) collective-permute-start(f32[80,128]{1,0:T(8,128)S(1)} %get-tuple-element.41.refs_0_), channel_id=1, source_target_pairs={{0,1},{1,2},{2,3},{3,0},{4,5},{5,6},{6,7},{7,4},{8,9},{9,10},{10,1... | collective-permute-start | bytes 122888 | tf_op jit(solution)/shard_map/ppermute | solution.py:518
  44.2 20.1 %all-to-all-start.1 = ((f32[64,2,128]{2,1,0:T(2,128)}), f32[64,2,128]{2,1,0:T(2,128)S(1)}, u32[]{:S(2)}, u32[]{:S(2)}) async-start(f32[64,2,128]{2,1,0:T(2,128)} %get-tuple-element.49), calls=%async_computation.1 | async-start | bytes 131072 | tf_op jit(solution)/shard_map/all_to_all | solution.py:547

commit v8 on v7

--- a/solution.py
+++ b/solution.py
@@ -123,15 +123,18 @@
 
 
 def rim_kernel(
-    list_hbm, spec_hbm, near_hbm, slot_hbm, weight_hbm, before_hbm, after_hbm, spec_ref,
-    near_ref, slot_ref, weight_ref, list_ref, before_ref, after_ref, sems,
+    list_hbm, spec_hbm, near_hbm, slot_hbm, weight_hbm, inner_hbm, outer_hbm, spec_ref,
+    near_ref, slot_ref, weight_ref, list_ref, inner_ref, outer_ref, sems,
 ):
     pairs = ((list_hbm, list_ref), (spec_hbm, spec_ref))
     first = start_copies(pairs + ((near_hbm, near_ref), (slot_hbm, slot_ref), (weight_hbm, weight_ref)), sems)
     wait_copies(first[:2])
     rims = []
-    for side, rim_ref in ((0, before_ref), (1, after_ref)):
-        index = jnp.broadcast_to(list_ref[side : side + 1, :], (8, 128))
+    even = lax.rem(lax.axis_index("tile"), 2) == 0
+    to_last, to_next = list_ref[0:1, :], list_ref[1:2, :]
+    lists = (jnp.where(even, to_next, to_last), jnp.where(even, to_last, to_next))
+    for chosen, rim_ref in zip(lists, (inner_ref, outer_ref)):
+        index = jnp.broadcast_to(chosen, (8, 128))
         rims.append((index & 127, index >> 7, rim_ref))
 
     def step(i, carry):
@@ -146,7 +149,7 @@
         return carry
 
     lax.fori_loop(0, GS, step, 0, unroll=2)
-    last = start_copies(((before_ref, before_hbm), (after_ref, after_hbm)), sems)
+    last = start_copies(((inner_ref, inner_hbm), (outer_ref, outer_hbm)), sems)
     wait_copies(first[2:])
     wait_copies(last)
 
@@ -205,8 +208,10 @@
     inv_omega = wide([1.0 / w for w in OMEGA]) * down_scale
     inv_root = wide([math.sqrt(G_ACC) / w for w in OMEGA]) * down_scale
     omega_c = wide([w * w / G_ACC for w in OMEGA]) * (up * up)
-    put_parts(low_ref, slice(0, RIM), x_ref, slice(0, RIM))
-    put_parts(high_ref, slice(0, RIM), x_ref, slice(EXT - RIM, EXT))
+    even = lax.rem(lax.axis_index("tile"), 2) == 0
+    upper, lower = jnp.where(even, EXT - RIM, 0), jnp.where(even, 0, EXT - RIM)
+    put_parts(low_ref, slice(0, RIM), x_ref, pl.ds(pl.multiple_of(upper, RIM), RIM))
+    put_parts(high_ref, slice(0, RIM), x_ref, pl.ds(pl.multiple_of(lower, RIM), RIM))
     for i in range(4):
         for half in range(2):
             p0, p1, p2 = parts3(arrived_ref[:, 2 * i + half, :])
@@ -474,7 +479,7 @@
     )(in_hbm(send_rows), in_hbm(forcing))
     arrived = lax.all_to_all(outgoing, "tile", split_axis=0, concat_axis=0, tiled=True)
 
-    to_before, to_after, spec, near, slot, weight, mark = call(
+    inner, outer, spec, near, slot, weight, mark = call(
         rim_kernel,
         "rims",
         [distant(GS, ND, RIM), distant(GS, ND, RIM), resident(GS, ND, PTS)]
@@ -491,9 +496,12 @@
         behind=True,
         mark=True,
     )(*map(in_hbm, (halo_send.reshape(2, RIM), spectrum, neighbours, point_slot, remap_weight)), mark)
-    up = [(d, d + 1) for d in range(TILES - 1)]
-    low_rim = lax.ppermute(to_after, "tile", up)
-    high_rim = lax.ppermute(to_before, "tile", [(b, a) for a, b in up])
+    trades = []
+    for first in (0, 1):
+        pairs = [(d, d + 1) for d in range(first, TILES - 1, 2)]
+        trades.append(pairs + [(b, a) for a, b in pairs])
+    inner_rim = lax.ppermute(inner, "tile", trades[0])
+    outer_rim = lax.ppermute(outer, "tile", trades[1])
     operand, mark = call(
         operand_kernel,
         "operand",
@@ -514,7 +522,7 @@
         behind=True,
         mark=True,
         aliases={0: 0},
-    )(operand, arrived, low_rim, high_rim, slot, weight, mark)
+    )(operand, arrived, inner_rim, outer_rim, slot, weight, mark)
     others = [lax.ppermute(moments, "freq", [(i, (i + n) % 4) for i in range(4)]) for n in (1, 2, 3)]
 
     def move(half, mark):

time: 66.6 us -> 64.9 us (0.974)
  starting transfers between devices: 32.6 us -> 30.8 us
    all_to_all x1, waiting for transfers between devices: 0.01 us -> 1.76 us  [on_device(): lax.all_to_all(outgoing, 'tile', split_axis=0, concat_axis=0, tiled=True)]
    ppermute x2, starting transfers between devices: 5.46 us -> 3.76 us  [the longest x1 3.22 us: on_device(): outer_rim = lax.ppermute(outer, 'tile', trades[1])]
    ppermute x2, waiting for transfers between devices: 2.13 us -> 1.11 us  [the longest x1 1.11 us: on_device(): outer_rim = lax.ppermute(outer, 'tile', trades[1])]
  transfers between devices with their start and end apart: 7 -> 7, of which waited for: 3 -> 3; matrix products, arithmetic and copies ran while one was open for 0% -> 0% of each run, Pallas kernels for 23% -> 24%
where the time goes in v8:
time: 64.9 us; the launch traced here: 64.6 us
  starting transfers between devices  30.8 us (47%)
  Pallas kernels  26.3 us (41%)
  waiting for transfers between devices  6.76 us (10%)
  between operations  0.75 us (1%)
    all_to_all x1, starting transfers between devices, on_device(): lax.all_to_all(outgoing, 'tile', split_axis=0, concat_axis=0, tiled=True)  13.2 us
    all_to_all x1, starting transfers between devices, on_device(): lax.all_to_all(slot_sums, 'tile', split_axis=0, concat_axis=0, tiled=True)  10.2 us
    pallas_call x2, Pallas kernels, move(): call(functools.partial(move_kernel, half), f'move{half}', [resident(GS, N...  8.27 us
    pallas_call x1, Pallas kernels, on_device(): call(wind_kernel, 'wind', [resident(ND * 16, EXT, dtype=BF), array(80, 12...  4.26 us
    all_to_all x1, waiting for transfers between devices, on_device(): lax.all_to_all(slot_sums, 'tile', split_axis=0, concat_axis=0, tiled=True)  3.88 us
    ppermute x3, starting transfers between devices, on_device(): lax.ppermute(moments, 'freq', [(i, (i + n) % 4) for i in range(4)])  3.68 us
    pallas_call x1, Pallas kernels, on_device(): call(rim_kernel, 'rims', [distant(GS, ND, RIM), distant(GS, ND, RIM), res...  3.26 us
    ppermute x1, starting transfers between devices, on_device(): outer_rim = lax.ppermute(outer, 'tile', trades[1])  3.22 us
  transfers between devices with their start and end apart: 7, of which 3 were waited for; matrix products, arithmetic and copies ran while one was open for 0% of the time, Pallas kernels for 24%

profile of v8, /device:TPU:1, one launch (start us, length us, event | category | flops | bytes accessed | tf_op | source)
XLA Modules:
  0.0 64.6 jit_solution(13283151817835811645)
XLA Ops:
  0.6 2.8 %outgoing.1 = (f32[64,8,128]{2,1,0:T(8,128)}, s32[64,256]{1,0:T(8,128)S(1)}, f32[8,128]{1,0:T(8,128)S(1)}) custom-call(s32[64,256]{1,0:T(8,128)} %refs_0_.1, f32[4,2048]{1,0:T(4,128)} %refs_1_.2), custom_call_target="tpu_custom_call" | custom-call | bytes 9000000 | tf_op jit(solution)/shard_map/outgoing/pallas_call | solution.py:465
  3.5 13.2 %all-to-all-start = ((f32[64,8,128]{2,1,0:T(8,128)}), f32[64,8,128]{2,1,0:T(8,128)S(1)}, u32[]{:S(2)}, u32[]{:S(2)}) async-start(f32[64,8,128]{2,1,0:T(8,128)} %get-tuple-element.32), calls=%async_computation | async-start | bytes 524288 | tf_op jit(solution)/shard_map/all_to_all | solution.py:480
  16.6 3.3 %rims.1 = (f32[8,24,128]{2,1,0:T(8,128)}, f32[8,24,128]{2,1,0:T(8,128)}, f32[8,24,2048]{2,1,0:T(8,128)S(1)}, s32[4,2048]{1,0:T(4,128)S(1)}, s32[4,2048]{1,0:T(4,...) custom-call(s32[2,128]{1,0:T(2,128)} %bitcast.3, f32[8,24,2048]{2,1,0:T(8,128)} %refs_1_.3, s32[4,2048]{1,0:T(4,128)} %refs_2_.1, ...), custom_call_target="tpu_custom_call" | custom-call | bytes 9000000 | tf_op jit(solution)/shard_map/rims/pallas_call | solution.py:482
  19.9 0.5 collective-permute-start
  20.4 3.2 %collective-permute-start.1 = (f32[8,24,128]{2,1,0:T(8,128)}, f32[8,24,128]{2,1,0:T(8,128)S(1)}, u32[]{:S(2)}, u32[]{:S(2)}) collective-permute-start(f32[8,24,128]{2,1,0:T(8,128)} %get-tuple-element.34), channel_id=1, source_target_pairs={{4,8},{12,16},{20,24},{28,32},{36,40},{44,48},{52,56},{60,64},{68,... | collective-permute-start | bytes 294920 | tf_op jit(solution)/shard_map/ppermute | solution.py:504
  23.7 2.1 %operand.1 = (bf16[384,2304]{1,0:T(8,128)(2,1)S(1)}, f32[8,128]{1,0:T(8,128)S(1)}) custom-call(f32[8,24,2048]{2,1,0:T(8,128)S(1)} %get-tuple-element.29.refs_0_, f32[8,128]{1,0:T(8,128)S(1)} %get-tuple-element.30.refs_1_), custom_call_target="tpu_custom_call" | custom-call | bytes 9000000 | tf_op jit(solution)/shard_map/operand/pallas_call | solution.py:505
  25.8 0.0 collective-permute-done.refs_2_
  25.8 1.1 %collective-permute-done.1.refs_3_ = f32[8,24,128]{2,1,0:T(8,128)S(1)} collective-permute-done((f32[8,24,128]{2,1,0:T(8,128)}, f32[8,24,128]{2,1,0:T(8,128)S(1)}, u32[]{:S(2)}, u32[]{:S(2)}) %collective-permute-start.1) | collective-permute-done | bytes 98336 | tf_op jit(solution)/shard_map/ppermute | solution.py:504
  26.9 1.8 %all-to-all-done.refs_1_ = f32[64,8,128]{2,1,0:T(8,128)S(1)} async-done(((f32[64,8,128]{2,1,0:T(8,128)}), f32[64,8,128]{2,1,0:T(8,128)S(1)}, u32[]{:S(2)}, u32[]{:S(2)}) %all-to-all-start) | async-done | bytes 262176 | tf_op jit(solution)/shard_map/all_to_all | solution.py:480
  28.6 4.3 %wind.1 = (bf16[384,2304]{1,0:T(8,128)(2,1)S(1)}, f32[80,128]{1,0:T(8,128)S(1)}, f32[80,128]{1,0:T(8,128)S(1)}, f32[8,128]{1,0:T(8,128)S(1)}) custom-call(bf16[384,2304]{1,0:T(8,128)(2,1)S(1)} %get-tuple-element.31.refs_0_, f32[64,8,128]{2,1,0:T(8,128)S(1)} %all-to-all-done.refs_1_, ...), custom_call_target="tpu_custom_call", output_to_operand_aliasing={{0}: (0, {})} | custom-call | bytes 18000000 | tf_op jit(solution)/shard_map/wind/pallas_call | solution.py:515
  32.9 2.5 %collective-permute-start.4 = (f32[80,128]{1,0:T(8,128)S(1)}, f32[80,128]{1,0:T(8,128)S(1)}, u32[]{:S(2)}, u32[]{:S(2)}) collective-permute-start(f32[80,128]{1,0:T(8,128)S(1)} %get-tuple-element.41.refs_0_), channel_id=1, source_target_pairs={{0,3},{1,0},{2,1},{3,2},{4,7},{5,4},{6,5},{7,6},{8,11},{9,8},{10,9... | collective-permute-start | bytes 122888 | tf_op jit(solution)/shard_map/ppermute | solution.py:526
  35.4 0.5 collective-permute-start.3
  36.0 0.6 collective-permute-start.2
  36.6 4.1 %move0.1 = (f32[8,24,1024]{2,1,0:T(8,128)S(1)}, f32[8,128]{1,0:T(8,128)S(1)}) custom-call(s32[4,2048]{1,0:T(4,128)S(1)} %get-tuple-element.28.refs_0_, bf16[384,2304]{1,0:T(8,128)(2,1)S(1)} %get-tuple-element.38.refs_1_, f32[8,128]{1,0:T(8,128)S(1)} %get-tuple-element.39.refs_2_), custom_call_target="tpu_custom_call" | custom-call | bytes 16500000 | tf_op jit(solution)/shard_map/move0/pallas_call | solution.py:529
  40.7 0.0 collective-permute-done.4.refs_3_
  40.7 0.0 collective-permute-done.3.refs_2_
  40.7 0.0 collective-permute-done.2.refs_1_
  40.8 1.9 %fields.1 = (f32[96,128]{1,0:T(8,128)S(1)}, f32[64,2,128]{2,1,0:T(2,128)}, f32[8,128]{1,0:T(8,128)S(1)}) custom-call(f32[80,128]{1,0:T(8,128)S(1)} %get-tuple-element.41.refs_0_, f32[80,128]{1,0:T(8,128)S(1)} %collective-permute-done.2.refs_1_, f32[80,128]{1,0:T(8,128)S(1)} %collective-permute-done.3.refs_2_, f32[80,128]{1,0:T(8,128)S(1)} %collective-permute-done.4.refs_3_, ...), custom_call_target="tpu_custom_call" | custom-call | bytes 9000000 | tf_op jit(solution)/shard_map/fields/pallas_call | solution.py:540
  42.7 10.2 %all-to-all-start.1 = ((f32[64,2,128]{2,1,0:T(2,128)}), f32[64,2,128]{2,1,0:T(2,128)S(1)}, u32[]{:S(2)}, u32[]{:S(2)}) async-start(f32[64,2,128]{2,1,0:T(2,128)} %get-tuple-element.49), calls=%async_computation.1 | async-start | bytes 131072 | tf_op jit(solution)/shard_map/all_to_all | solution.py:555
  52.9 4.1 %move1.1 = (f32[8,24,1024]{2,1,0:T(8,128)S(1)}, f32[8,128]{1,0:T(8,128)S(1)}) custom-call(s32[4,2048]{1,0:T(4,128)S(1)} %get-tuple-element.28.refs_0_, bf16[384,2304]{1,0:T(8,128)(2,1)S(1)} %get-tuple-element.38.refs_1_, f32[8,128]{1,0:T(8,128)S(1)} %get-tuple-element.44.refs_2_), custom_call_target="tpu_custom_call" | custom-call | bytes 16500000 | tf_op jit(solution)/shard_map/move1/pallas_call | solution.py:529
  57.0 1.8 %source.1 = (f32[8,24,2048]{2,1,0:T(8,128)}, f32[8,128]{1,0:T(8,128)S(1)}) custom-call(f32[8,24,1024]{2,1,0:T(8,128)S(1)} %get-tuple-element.40.refs_0_, f32[8,24,1024]{2,1,0:T(8,128)S(1)} %get-tuple-element.45.refs_1_, f32[96,128]{1,0:T(8,128)S(1)} %get-tuple-element.46.refs_2_, f32[8,128]{1,0:T(8,128)S(1)} %get-tuple-element.47.refs_3_), custom_call_target="tpu_custom_call" | custom-call | bytes 9000000 | tf_op jit(solution)/shard_map/source/pallas_call | solution.py:558
  58.8 3.9 %all-to-all-done.1.refs_0_ = f32[64,2,128]{2,1,0:T(2,128)S(1)} async-done(((f32[64,2,128]{2,1,0:T(2,128)}), f32[64,2,128]{2,1,0:T(2,128)S(1)}, u32[]{:S(2)}, u32[]{:S(2)}) %all-to-all-start.1) | async-done | bytes 65568 | tf_op jit(solution)/shard_map/all_to_all | solution.py:555
  62.6 1.9 %band.1 = f32[16,128]{1,0:T(8,128)} custom-call(f32[64,2,128]{2,1,0:T(2,128)S(1)} %all-to-all-done.1.refs_0_, s32[64,256]{1,0:T(8,128)S(1)} %get-tuple-element.50.refs_1_, f32[8,128]{1,0:T(8,128)S(1)} %get-tuple-element.51.refs_2_), custom_call_target="tpu_custom_call" | custom-call | bytes 7500000 | tf_op jit(solution)/shard_map/band/pallas_call | solution.py:570
Async XLA Ops:
  3.5 25.2 %all-to-all-start = ((f32[64,8,128]{2,1,0:T(8,128)}), f32[64,8,128]{2,1,0:T(8,128)S(1)}, u32[]{:S(2)}, u32[]{:S(2)}) async-start(f32[64,8,128]{2,1,0:T(8,128)} %get-tuple-element.32), calls=%async_computation | async-start | bytes 524288 | tf_op jit(solution)/shard_map/all_to_all | solution.py:480
  19.9 5.9 %collective-permute-start = (f32[8,24,128]{2,1,0:T(8,128)}, f32[8,24,128]{2,1,0:T(8,128)S(1)}, u32[]{:S(2)}, u32[]{:S(2)}) collective-permute-start(f32[8,24,128]{2,1,0:T(8,128)} %get-tuple-element.33), channel_id=1, source_target_pairs={{0,4},{8,12},{16,20},{24,28},{32,36},{40,44},{48,52},{56,60},{64,6... | collective-permute-start | bytes 294920 | tf_op jit(solution)/shard_map/ppermute | solution.py:503
  20.4 6.4 %collective-permute-start.1 = (f32[8,24,128]{2,1,0:T(8,128)}, f32[8,24,128]{2,1,0:T(8,128)S(1)}, u32[]{:S(2)}, u32[]{:S(2)}) collective-permute-start(f32[8,24,128]{2,1,0:T(8,128)} %get-tuple-element.34), channel_id=1, source_target_pairs={{4,8},{12,16},{20,24},{28,32},{36,40},{44,48},{52,56},{60,64},{68,... | collective-permute-start | bytes 294920 | tf_op jit(solution)/shard_map/ppermute | solution.py:504
  32.9 7.8 %collective-permute-start.4 = (f32[80,128]{1,0:T(8,128)S(1)}, f32[80,128]{1,0:T(8,128)S(1)}, u32[]{:S(2)}, u32[]{:S(2)}) collective-permute-start(f32[80,128]{1,0:T(8,128)S(1)} %get-tuple-element.41.refs_0_), channel_id=1, source_target_pairs={{0,3},{1,0},{2,1},{3,2},{4,7},{5,4},{6,5},{7,6},{8,11},{9,8},{10,9... | collective-permute-start | bytes 122888 | tf_op jit(solution)/shard_map/ppermute | solution.py:526
  35.4 5.3 %collective-permute-start.3 = (f32[80,128]{1,0:T(8,128)S(1)}, f32[80,128]{1,0:T(8,128)S(1)}, u32[]{:S(2)}, u32[]{:S(2)}) collective-permute-start(f32[80,128]{1,0:T(8,128)S(1)} %get-tuple-element.41.refs_0_), channel_id=1, source_target_pairs={{0,2},{1,3},{2,0},{3,1},{4,6},{5,7},{6,4},{7,5},{8,10},{9,11},{10,... | collective-permute-start | bytes 122888 | tf_op jit(solution)/shard_map/ppermute | solution.py:526
  36.0 4.8 %collective-permute-start.2 = (f32[80,128]{1,0:T(8,128)S(1)}, f32[80,128]{1,0:T(8,128)S(1)}, u32[]{:S(2)}, u32[]{:S(2)}) collective-permute-start(f32[80,128]{1,0:T(8,128)S(1)} %get-tuple-element.41.refs_0_), channel_id=1, source_target_pairs={{0,1},{1,2},{2,3},{3,0},{4,5},{5,6},{6,7},{7,4},{8,9},{9,10},{10,1... | collective-permute-start | bytes 122888 | tf_op jit(solution)/shard_map/ppermute | solution.py:526
  42.7 20.0 %all-to-all-start.1 = ((f32[64,2,128]{2,1,0:T(2,128)}), f32[64,2,128]{2,1,0:T(2,128)S(1)}, u32[]{:S(2)}, u32[]{:S(2)}) async-start(f32[64,2,128]{2,1,0:T(2,128)} %get-tuple-element.49), calls=%async_computation.1 | async-start | bytes 131072 | tf_op jit(solution)/shard_map/all_to_all | solution.py:555
